TPU v7x, 512 devices: a whole 4x8x8 slice. The times are simulated.
512 devices in a mesh: row: 32 (over x, y), col: 16 (over z, core).
Axes of the slice: x: 4, y: 8, z: 8, core: 2. Of those that a mesh axis runs over, the one named last changes fastest.
Arguments:
- activations: bfloat16 [6144, 49, 512], P(('row', 'col'))
- pre_activation: bfloat16 [6144, 49, 1024], P(('row', 'col')), may hold values from -6 to 6
- pooled_grad: float32 [6144, 1024], P(('row', 'col')), may hold values from -300 to 300
- weights: bfloat16 [512, 1024], replicated, as said below
- master: float32 [512, 1024], P('row', 'col')
- velocity: float32 [512, 1024], P('row', 'col'), may hold values from -0.6 to 0.6
- bn_params: float32 [2, 1024], replicated, may hold values from 0.5 to 1.5
- bn_velocity: float32 [2, 1024], replicated, may hold values from -0.6 to 0.6
Outputs:
- input_grad: bfloat16 [6144, 49, 512], P(('row', 'col'))
- new_master: float32 [512, 1024], P('row', 'col')
- new_velocity: float32 [512, 1024], P('row', 'col')
- new_weights: bfloat16 [512, 1024], replicated
- new_bn: float32 [2, 1024], replicated
- new_bn_velocity: float32 [2, 1024], replicated
Inputs may be any that keep to these rules, and one draw needn't show every extreme that they name: weights lies within one bfloat16 rounding of master, entry by entry.
All inputs are finite; a program needn't handle non-finite values.
Results may differ from a plain program's by a relative error of at most 0.0045.
The roundings to bfloat16 on the way count: a program that leaves them out, or rounds other values in their place, can miss the bound.
Values may be sent and summed in bfloat16 or wider, within the bound.
No kernel may reach another device: no remote copies, remote signals or barrier semaphores. Data moves between devices by JAX's collectives and lax.ppermute only.
A program may use at most 64 MiB of HBM per device.

v0:
```python
import jax
import jax.numpy as jnp
from jax import lax
from jax.sharding import PartitionSpec as P

epsilon = 1e-05
trust_coef = 0.001
weight_decay = 0.0001
momentum = 0.9
learn_rate = 12.0


def body(
    activations, pre_activation, pooled_grad, weights, master, velocity, bn_params, bn_velocity
):
    images, positions, in_chan = activations.shape
    out_chan = weights.shape[1]
    row_count = images * positions
    n_row = lax.axis_size("row")
    n_col = lax.axis_size("col")
    group_element_count = row_count * n_col
    total_images = images * n_row * n_col
    norm_scale_weight = bn_params[0]
    flat_in = activations.reshape(row_count, in_chan)
    conv_low = jnp.dot(flat_in, weights, preferred_element_type=jnp.float32).astype(jnp.bfloat16)
    expand_conv_output = lax.optimization_barrier(conv_low).astype(jnp.float32)
    stats = lax.psum(
        (
            jnp.sum(expand_conv_output, axis=0),
            jnp.sum(expand_conv_output * expand_conv_output, axis=0),
        ),
        "col",
    )
    group_mean_value = stats[0] / group_element_count
    variance = stats[1] / group_element_count - group_mean_value * group_mean_value
    inverse_deviation = lax.rsqrt(variance + epsilon)
    upstream_all = jnp.broadcast_to(
        (pooled_grad / positions)[:, None, :], pre_activation.shape
    ).reshape(row_count, out_chan)
    incoming_gradient = jnp.where(
        pre_activation.reshape(row_count, out_chan) > 0, upstream_all, jnp.zeros_like(upstream_all)
    )
    normalized_input = (expand_conv_output - group_mean_value) * inverse_deviation
    local_up = jnp.sum(incoming_gradient, axis=0)
    local_upstream_normalized = jnp.sum(incoming_gradient * normalized_input, axis=0)
    group_totals_reduced = lax.psum((local_up, local_upstream_normalized), "col")
    expand_conv_gradient = (
        norm_scale_weight
        * inverse_deviation
        * (
            incoming_gradient
            - group_totals_reduced[0] / group_element_count
            - normalized_input * group_totals_reduced[1] / group_element_count
        )
    ).astype(jnp.bfloat16)
    back = lax.dot_general(
        expand_conv_gradient, weights, (((1,), (1,)), ((), ())), preferred_element_type=jnp.float32
    )
    input_grad = back.astype(jnp.bfloat16).reshape(images, positions, in_chan)
    row_part = lax.psum_scatter(
        lax.dot_general(
            flat_in,
            expand_conv_gradient,
            (((0,), (0,)), ((), ())),
            preferred_element_type=jnp.float32,
        ),
        "row",
        scatter_dimension=0,
        tiled=True,
    )
    grad_sum = lax.psum_scatter(row_part, "col", scatter_dimension=1, tiled=True)
    weight_grad = grad_sum * (1.0 / total_images)
    master_sq = jnp.sum(master * master)
    grad_sq = jnp.sum(weight_grad * weight_grad)
    bn_tot = lax.psum((group_totals_reduced[1], group_totals_reduced[0]), "row")
    norms = lax.psum((master_sq, grad_sq), ("row", "col"))
    upx_total, up_total = (bn_tot[0], bn_tot[1])
    master_total, grad_total = (norms[0], norms[1])
    wnorm = jnp.sqrt(master_total)
    gnorm = jnp.sqrt(grad_total)
    trust = trust_coef * wnorm / (gnorm + weight_decay * wnorm)
    new_velocity = momentum * velocity + learn_rate * trust * (weight_grad + weight_decay * master)
    new_master = master - new_velocity
    shard_low = new_master.astype(jnp.bfloat16)
    wide_rows = lax.all_gather(shard_low, "col", axis=1, tiled=True)
    new_weights = lax.all_gather(wide_rows, "row", axis=0, tiled=True)
    bn_grad = jnp.stack([upx_total, up_total]) * (1.0 / total_images)
    new_bn_velocity = momentum * bn_velocity + learn_rate * bn_grad
    new_bn = bn_params - new_bn_velocity
    return (input_grad, new_master, new_velocity, new_weights, new_bn, new_bn_velocity)


def solution(mesh):
    placed = (
        P(("row", "col"), None, None),
        P(("row", "col"), None, None),
        P(("row", "col"), None),
        P(),
        P("row", "col"),
        P("row", "col"),
        P(),
        P(),
    )
    return jax.shard_map(
        body,
        mesh=mesh,
        in_specs=placed,
        out_specs=(P(("row", "col"), None, None), P("row", "col"), P("row", "col"), P(), P(), P()),
        check_vma=False,
    )
```

profile of v0, /device:TPU:1, one launch (start us, length us, event | category | flops | bytes accessed | tf_op | source)
XLA Modules:
  0.0 561.5 jit_solution(478443962725745759)
XLA Ops:
  7.2 0.0 copy-start
  7.2 0.0 copy-start.6
  7.2 0.0 copy-start.1
  7.2 0.0 reduce-scatter.7.cloned.1.call-start
  7.2 1.4 reshape.30
  8.7 0.0 copy-done
  8.7 0.0 copy-start.4
  8.7 1.8 convolution_convert_fusion
  10.5 0.0 copy-done.6
  10.6 0.0 copy-done.1
  10.6 2.0 fusion.9
  12.6 0.0 copy-done.4
  12.6 0.0 slice-start
  12.6 1.9 select_n.9
  14.5 1.6 convert_reduce_fusion
  16.1 31.1 %all-reduce.3 = (f32[1024]{0:T(1024)S(1)}, f32[1024]{0:T(1024)S(1)}) all-reduce(f32[1024]{0:T(1024)S(1)} %get-tuple-element.25, f32[1024]{0:T(1024)S(1)} %get-tuple-element.24), channel_id=1, replica_groups=mesh['row'=32,'col'=16] {'col'}, use_global_device_ids=true, to_apply=%region_1.0 | all-reduce | flops 2048 | bytes 16384 | tf_op jit(solution)/shard_map/psum | solution.py:27
  47.2 0.0 slice-done
  47.2 1.7 fusion.4
  49.0 26.3 %all-reduce.2 = (f32[1024]{0:T(1024)S(1)}, f32[1024]{0:T(1024)S(1)}) all-reduce(f32[1024]{0:T(1024)S(1)} %fusion.4, f32[1024]{0:T(1024)S(1)} %get-tuple-element.39), channel_id=1, replica_groups=mesh['row'=32,'col'=16] {'col'}, use_global_device_ids=true, to_apply=%region_7.8 | all-reduce | flops 2048 | bytes 16384 | tf_op jit(solution)/shard_map/psum | solution.py:46
  75.3 0.0 copy-start.5
  75.3 2.0 fusion.8
  77.3 0.0 copy-start.2
  77.3 1.0 copy-done.2
  78.4 0.0 copy-done.5
  78.4 1.0 convolution_bitcast_fusion
  79.4 1.9 copy.37
  81.3 0.0 copy-start.7
  81.3 0.0 copy-start.10
  81.3 0.0 copy-start.3
  81.3 0.0 reduce-scatter.7.cloned.1.call-update
  81.3 0.0 reduce-scatter.9.cloned.1.call-start
  81.4 212.4 %reduce-scatter.7.cloned.1.call-done = f32[16,1024]{1,0:T(8,128)} async-done(((f32[512,1024]{1,0:T(8,128)}), f32[16,1024]{1,0:T(8,128)}) %reduce-scatter.7.cloned.1.call-update) | async-done | bytes 65552 | tf_op jit(solution)/shard_map/reduce_scatter | solution.py:60
  293.7 1.8 copy.39
  295.6 0.0 reduce-scatter.9.cloned.1.call-update
  295.6 0.0 all-gather.3.cloned.1.call-start
  295.6 62.7 %reduce-scatter.9.cloned.1.call-done = f32[64,16]{1,0:T(8,128)} async-done(((f32[1024,16]{1,0:T(8,128)}), f32[64,16]{1,0:T(8,128)}) %reduce-scatter.9.cloned.1.call-update) | async-done | bytes 4112
  358.3 0.8 copy.40
  359.1 0.0 copy-done.7
  359.1 0.6 multiply_reduce_fusion
  359.8 99.8 %all-reduce = (f32[]{:T(128)}, f32[]{:T(128)}) all-reduce(f32[]{:T(128)} %get-tuple-element.45, f32[]{:T(128)} %get-tuple-element.44), channel_id=1, replica_groups=mesh['row'=32,'col'=16] {'row','col'}, use_global_device_ids=true, to_apply=%region_9.10 | all-reduce | flops 2 | bytes 16 | tf_op jit(solution)/shard_map/psum | solution.py:76
  460.9 0.0 copy-done.10
  460.9 0.6 convert_bitcast_fusion
  461.6 16.7 %all-gather = bf16[16,64,16]{1,2,0:T(8,128)(2,1)S(1)} all-gather(bf16[1,64,16]{1,2,0:T(8,128)(2,1)S(1)} %get-tuple-element.36), channel_id=1, replica_groups=mesh['row'=32,'col'=16] {'col'}, dimensions={0}, use_global_device_ids=true | all-gather | bytes 34816 | tf_op jit(solution)/shard_map/all_gather | solution.py:85
  478.2 0.7 reshape.33
  479.0 0.0 all-gather.3.cloned.1.call-update
  479.0 0.0 copy-done.3
  479.0 0.0 copy-start.8
  479.0 0.0 copy-start.9
  479.0 0.8 convolution_convert_fusion.1
  479.8 1.0 reshape.31
  480.9 58.0 %all-reduce.1 = (f32[1,1024]{1,0:T(1,128)S(1)}, f32[1,1024]{1,0:T(1,128)S(1)}) all-reduce(f32[1,1024]{1,0:T(1,128)S(1)} %bitcast.25, f32[1,1024]{1,0:T(1,128)S(1)} %bitcast.26), channel_id=1, replica_groups=mesh['row'=32,'col'=16] {'row'}, use_global_device_ids=true, to_apply=%region_15.16 | all-reduce | flops 2048 | bytes 16384 | tf_op jit(solution)/shard_map/psum | solution.py:75
  538.9 0.0 copy-done.8
  538.9 0.0 copy-done.9
  538.9 0.6 fusion.12
  539.5 13.2 %all-gather.3.cloned.1.call-done = bf16[512,1024]{1,0:T(8,128)(2,1)} async-done(((bf16[16,1024]{1,0:T(8,128)(2,1)}), bf16[512,1024]{1,0:T(8,128)(2,1)}) %all-gather.3.cloned.1.call-update) | async-done | bytes 1048592 | tf_op jit(solution)/shard_map/all_gather | solution.py:86
  552.7 2.3 copy.42
  (4 shorter events, 0.0 us)
Async XLA Ops:
  7.2 1.5 copy-start
  7.2 3.4 copy-start.6
  7.2 3.4 copy-start.1
  7.2 286.5 %reduce-scatter.7.cloned.1.call-start = ((), (), s32[]{:S(2)}) async-start(), calls=%async_computation.3 | async-start | bytes 2162688 | tf_op jit(solution)/shard_map/reduce_scatter | solution.py:60
  8.7 3.9 copy-start.4
  12.6 34.6 %slice-start = ((f32[2,1024]{1,0:T(2,128)}), f32[1,1024]{1,0:T(1,128)S(1)}, s32[]{:S(2)}) async-start(f32[2,1024]{1,0:T(2,128)} %param.14), calls=%async_computation.5 | async-start | bytes 8192 | tf_op jit(solution)/shard_map/slice | solution.py:23
  75.3 3.1 copy-start.5
  77.3 1.0 copy-start.2
  81.3 277.9 %copy-start.7 = (f32[16,64]{1,0:T(8,128)S(1)}, f32[16,64]{1,0:T(8,128)}, u32[]{:S(2)}) copy-start(f32[16,64]{1,0:T(8,128)} %param.12) | copy-start | bytes 12292
  81.3 379.7 %copy-start.10 = (f32[16,64]{1,0:T(8,128)S(1)}, f32[16,64]{1,0:T(8,128)}, u32[]{:S(2)}) copy-start(f32[16,64]{1,0:T(8,128)} %param.13) | copy-start | bytes 12292
  81.3 397.7 %copy-start.3 = (bf16[588,1024]{1,0:T(8,128)(2,1)S(1)}, bf16[588,1024]{1,0:T(8,128)(2,1)}, u32[]{:S(2)}) copy-start(bf16[588,1024]{1,0:T(8,128)(2,1)} %copy-done.2) | copy-start | bytes 3612676
  81.3 277.0 %reduce-scatter.9.cloned.1.call-start = ((), (), s32[]{:S(2)}) async-start(), calls=%async_computation.4 | async-start | bytes 557056
  295.6 257.1 %all-gather.3.cloned.1.call-start = ((), (), s32[]{:S(2)}) async-start(), calls=%async_computation.2 | async-start | bytes 1081344 | tf_op jit(solution)/shard_map/all_gather | solution.py:86
  479.0 59.9 %copy-start.8 = (f32[2,1024]{1,0:T(2,128)S(1)}, f32[2,1024]{1,0:T(2,128)}, u32[]{:S(2)}) copy-start(f32[2,1024]{1,0:T(2,128)} %param.14) | copy-start | bytes 24580
  479.0 59.9 %copy-start.9 = (f32[2,1024]{1,0:T(2,128)S(1)}, f32[2,1024]{1,0:T(2,128)}, u32[]{:S(2)}) copy-start(f32[2,1024]{1,0:T(2,128)} %param.15) | copy-start | bytes 24580
Sparse Core Ops, SparseCore 0:
  81.4 212.2 reduce-scatter.6
  297.3 60.9 reduce-scatter.8
  479.1 73.5 all-gather.2
where the time goes:
time: 565 us; the launch traced here: 561 us
  waiting for transfers between devices  288 us (51%)
  blocking collectives  232 us (41%)
  between operations  15.4 us (3%)
  local copies, waits for them, and re-layouts  13 us (2%)
  other arithmetic  9.31 us (2%)
    reduce_scatter x1, waiting for transfers between devices, body(): lax.psum_scatter(lax.dot_general(flat_in, expand_conv_gradient, (((0,), (...  212 us
    psum x1, blocking collectives, body(): norms = lax.psum((master_sq, grad_sq), ('row', 'col'))  99.8 us
    unnamed x4, waiting for transfers between devices  62.7 us
    psum x1, blocking collectives, body(): bn_tot = lax.psum((group_totals_reduced[1], group_totals_reduced[0]), 'row')  58 us
    psum x1, blocking collectives, body(): lax.psum((jnp.sum(expand_conv_output, axis=0), jnp.sum(expand_conv_output...  31.1 us
    psum x1, blocking collectives, body(): lax.psum((local_up, local_upstream_normalized), 'col')  26.3 us
    all_gather x1, blocking collectives, body(): wide_rows = lax.all_gather(shard_low, 'col', axis=1, tiled=True)  16.7 us
    all_gather x1, waiting for transfers between devices, body(): new_weights = lax.all_gather(wide_rows, 'row', axis=0, tiled=True)  13.2 us
  transfers between devices with their start and end apart: 3, of which 3 were waited for; matrix products, arithmetic and copies ran while one was open for 0% of the time, Pallas kernels for 0%

commit v1 on v0

v1 whole, which is shorter than its diff:
```python
import functools

import jax
import jax.numpy as jnp
import numpy as np
from jax import lax
from jax.experimental import pallas as pl
from jax.experimental.pallas import tpu as pltpu
from jax.sharding import Mesh, PartitionSpec as P

epsilon = 1e-05
trust_coef = 0.001
weight_decay = 0.0001
momentum = 0.9
learn_rate = 12.0

IMG, PIX, STRIDE = 12, 49, 64
CIN, COUT = 512, 1024
ROWS = IMG * STRIDE
HALF = CIN // 2
N_ROW, N_COL = 32, 16
M = PIX * IMG * N_COL
BATCH = IMG * N_ROW * N_COL
CHUNKS = COUT // 128
GROUP, PEERS, ALL = ("z", "core"), ("x", "y", "z"), ("x", "y", "z", "core")
STAT_ROWS = 48
SIDE_ROWS = 24
bf16, f32 = jnp.bfloat16, jnp.float32


def params(megabytes=48):
    return pltpu.CompilerParams(vmem_limit_bytes=megabytes << 20)


def fold(line):
    return jnp.concatenate([line[:, 128 * k : 128 * k + 128] for k in range(line.shape[1] // 128)], axis=0)


def unfold(block):
    return jnp.concatenate([block[k : k + 1] for k in range(block.shape[0])], axis=1)


def stats_kernel(act_ref, pre_ref, pool_ref, w_ref, master_ref, vel_ref, conv_ref, actp_ref, msg_ref):
    actp_ref[...] = jnp.zeros_like(actp_ref)
    for i in range(IMG):
        actp_ref[STRIDE * i : STRIDE * i + PIX, :] = act_ref[i]
    conv_ref[...] = jnp.dot(actp_ref[...], w_ref[...], preferred_element_type=f32).astype(bf16)
    total = jnp.zeros((1, COUT), f32)
    square = jnp.zeros((1, COUT), f32)
    up = jnp.zeros((1, COUT), f32)
    up_conv = jnp.zeros((1, COUT), f32)
    for i in range(IMG):
        conv = conv_ref[STRIDE * i : STRIDE * i + STRIDE, :].astype(f32)
        total += jnp.sum(conv, axis=0, keepdims=True)
        square += jnp.sum(conv * conv, axis=0, keepdims=True)
        passed = pre_ref[i].astype(f32) > 0
        share = pool_ref[i : i + 1, :] / PIX
        up += share * jnp.sum(jnp.where(passed, 1.0, 0.0), axis=0, keepdims=True)
        up_conv += share * jnp.sum(jnp.where(passed, conv[:PIX], 0.0), axis=0, keepdims=True)
    act_total = jnp.sum(actp_ref[...].astype(f32), axis=0, keepdims=True)
    master = master_ref[...]
    norm = jnp.sum(jnp.sum(master * master, axis=1, keepdims=True), axis=0, keepdims=True)
    decayed = master - momentum * vel_ref[...]
    msg = jnp.concatenate(
        [
            fold(total),
            fold(square),
            fold(up),
            fold(up_conv),
            fold(act_total),
            jnp.broadcast_to(norm, (4, 128)),
            jnp.concatenate([decayed[:8], decayed[8:]], axis=1),
        ],
        axis=0,
    )
    for p in range(N_COL):
        msg_ref[p] = msg


def split(line):
    high = line.astype(bf16)
    return [high, (line - high.astype(f32)).astype(bf16)]


def grad_kernel(core_ref, stat_ref, conv_ref, actp_ref, pre_ref, pool_ref, bn_ref, cg_ref, keep_ref, send_ref, side_ref, grad):
    core = core_ref[0]
    sums = jnp.sum(stat_ref[:, :40, :], axis=0)
    total = unfold(sums[0:8])
    square = unfold(sums[8:16])
    sum_up = unfold(sums[16:24])
    up_conv = unfold(sums[24:32])
    act_mean = sums[32:36] / M
    norm = jnp.concatenate([sums[36:37]] * CHUNKS, axis=1)
    mean = total / M
    variance = square / M - mean * mean
    rstd = lax.rsqrt(variance + epsilon)
    sum_upx = rstd * (up_conv - mean * sum_up)
    scale = bn_ref[0:1, :] * rstd
    shift = scale * (sum_up / M)
    slope = scale * (sum_upx / M) * rstd
    cg_ref[...] = jnp.zeros_like(cg_ref)
    cg_total = jnp.zeros((1, COUT), f32)
    for i in range(IMG):
        conv = conv_ref[STRIDE * i : STRIDE * i + STRIDE, :].astype(f32)[:PIX]
        on = scale * (pool_ref[i : i + 1, :] / PIX) - shift
        cg = jnp.where(pre_ref[i].astype(f32) > 0, on, -shift) - slope * (conv - mean)
        low = cg.astype(bf16)
        cg_ref[STRIDE * i : STRIDE * i + PIX, :] = low
        cg_total += jnp.sum(low.astype(f32), axis=0, keepdims=True)
    grad[...] = lax.dot_general(
        actp_ref[...], cg_ref[...], (((0,), (0,)), ((), ())), preferred_element_type=f32
    )
    column = jnp.transpose(jnp.concatenate([unfold(act_mean)] * 8, axis=0))[:, 0:1]
    grad[...] = grad[...] - column * cg_total
    keep_ref[...] = grad[pl.ds(pl.multiple_of(core * HALF, HALF), HALF), :]
    send_ref[...] = grad[pl.ds(pl.multiple_of((1 - core) * HALF, HALF), HALF), :].astype(bf16)
    tops, bottoms = [], []
    for k in range(N_COL):
        block = stat_ref[k, 40:48, :]
        tops.append(block[:, :64])
        bottoms.append(block[:, 64:])
    decayed = jnp.concatenate([jnp.concatenate(tops, axis=1), jnp.concatenate(bottoms, axis=1)], axis=0)
    norm_high = norm.astype(bf16)
    norm_rest = norm - norm_high.astype(f32)
    extra = [h.astype(f32) for h in split(sum_up) + split(sum_upx) + [norm_high] + split(norm_rest)]
    extra.append(jnp.zeros((1, COUT), f32))
    side_ref[...] = jnp.concatenate([decayed, jnp.concatenate(extra, axis=0)], axis=0).astype(bf16)


def back_kernel(cg_ref, w_ref, out_ref):
    back = lax.dot_general(cg_ref[...], w_ref[...], (((1,), (1,)), ((), ())), preferred_element_type=f32)
    for i in range(IMG):
        out_ref[i] = back[STRIDE * i : STRIDE * i + PIX].astype(bf16)


def pair_kernel(keep_ref, got_ref, out_ref):
    both = (keep_ref[...] + got_ref[...].astype(f32)).reshape(HALF // 8, 8, COUT)
    for j in range(CHUNKS):
        out_ref[:, j] = both[:, :, 128 * j : 128 * j + 128].astype(bf16)


def sum_kernel(got_ref, out_ref):
    total = jnp.sum(got_ref[...].astype(f32), axis=0) * (1.0 / BATCH)
    out_ref[...] = jnp.broadcast_to(total.astype(bf16)[None], out_ref.shape)


def update_kernel(
    place_ref, mine_ref, other_ref, side_ref, w_ref, master_ref, vel_ref, bn_ref, bnv_ref,
    new_master_ref, new_vel_ref, new_w_ref, new_bn_ref, new_bnv_ref, grad,
):
    core, row, col = place_ref[0], place_ref[1], place_ref[2]
    square = jnp.zeros((8, 128), f32)
    for part, start in ((mine_ref, core * HALF), (other_ref, (1 - core) * HALF)):
        for j in range(CHUNKS):
            block = part[:, j].astype(f32)
            square += jnp.sum(block * block, axis=0)
            grad[pl.ds(pl.multiple_of(start, HALF), HALF), 128 * j : 128 * j + 128] = block.reshape(HALF, 128)
    grad_total = jnp.sum(jnp.sum(square, axis=1, keepdims=True), axis=0, keepdims=True)
    side = side_ref[...].astype(f32).reshape(N_ROW, SIDE_ROWS, COUT)
    extra = jnp.sum(side[:, 16:24, :], axis=0)
    up_total = extra[0:1] + extra[1:2]
    upx_total = extra[2:3] + extra[3:4]
    master_total = (extra[4:5] + extra[5:6] + extra[6:7])[:, 0:1]
    wnorm = jnp.sqrt(master_total)
    gnorm = jnp.sqrt(grad_total)
    rate = learn_rate * (trust_coef * wnorm / (gnorm + weight_decay * wnorm))
    decayed = side[:, :16, :].reshape(CIN, COUT)
    new_w_ref[...] = (decayed - rate * (grad[...] + weight_decay * w_ref[...].astype(f32))).astype(bf16)
    pair = grad[pl.ds(pl.multiple_of(row * 16, 16), 16), pl.ds(pl.multiple_of((col // 2) * 128, 128), 128)]
    own = jnp.where(col % 2 == 0, pair[:, :64], pair[:, 64:])
    new_vel = momentum * vel_ref[...] + rate * (own + weight_decay * master_ref[...])
    new_vel_ref[...] = new_vel
    new_master_ref[...] = master_ref[...] - new_vel
    bn_grad = jnp.concatenate([upx_total, up_total], axis=0) * (1.0 / BATCH)
    new_bnv = momentum * bnv_ref[...] + learn_rate * bn_grad
    new_bnv_ref[...] = new_bnv
    new_bn_ref[...] = bn_ref[...] - new_bnv


def shape(dims, kind):
    return jax.ShapeDtypeStruct(dims, kind)


SMEM = pl.BlockSpec(memory_space=pltpu.SMEM)
VMEM = pl.BlockSpec(memory_space=pltpu.VMEM)


def body(activations, pre_activation, pooled_grad, weights, master, velocity, bn_params, bn_velocity):
    core = lax.axis_index("core").astype(jnp.int32)
    row = (lax.axis_index("x") * 8 + lax.axis_index("y")).astype(jnp.int32)
    col = (lax.axis_index("z") * 2 + lax.axis_index("core")).astype(jnp.int32)
    place = jnp.stack([core, row, col])
    conv, act, msg = pl.pallas_call(
        stats_kernel,
        out_shape=(shape((ROWS, COUT), bf16), shape((ROWS, CIN), bf16), shape((N_COL, STAT_ROWS, 128), f32)),
        in_specs=[VMEM] * 6,
        out_specs=(VMEM,) * 3,
        compiler_params=params(),
        name="conv_stats",
    )(activations, pre_activation, pooled_grad, weights, master, velocity)
    stats = lax.all_to_all(msg, GROUP, 0, 0)
    conv_grad, keep, send, side = pl.pallas_call(
        grad_kernel,
        out_shape=(
            shape((ROWS, COUT), bf16),
            shape((HALF, COUT), f32),
            shape((HALF, COUT), bf16),
            shape((SIDE_ROWS, COUT), bf16),
        ),
        in_specs=[SMEM] + [VMEM] * 6,
        out_specs=(VMEM,) * 4,
        scratch_shapes=[pltpu.VMEM((CIN, COUT), f32)],
        compiler_params=params(),
        name="conv_grad",
    )(place, stats, conv, act, pre_activation, pooled_grad, bn_params)
    side_all = lax.all_gather(side, ("x", "y"), axis=0, tiled=True)
    swap = [(0, 1), (1, 0)]
    got = lax.ppermute(send, "core", swap)
    input_grad = pl.pallas_call(
        back_kernel,
        out_shape=shape((IMG, PIX, CIN), bf16),
        in_specs=[VMEM] * 2,
        out_specs=VMEM,
        compiler_params=params(),
        cost_estimate=pl.CostEstimate(flops=2 * ROWS * CIN * COUT, bytes_accessed=4 << 20, transcendentals=0),
        name="input_grad",
    )(conv_grad, weights)
    blocks = pl.pallas_call(
        pair_kernel,
        out_shape=shape((HALF // 8, CHUNKS, 8, 128), bf16),
        in_specs=[VMEM] * 2,
        out_specs=VMEM,
        compiler_params=params(),
        name="pair_sum",
    )(keep, got)
    arrived = lax.all_to_all(blocks.reshape(256, 8, 128), PEERS, 0, 0)
    block = pl.pallas_call(
        sum_kernel,
        out_shape=shape((256, 8, 128), bf16),
        in_specs=[VMEM],
        out_specs=VMEM,
        compiler_params=params(),
        name="block_sum",
    )(arrived)
    mine = lax.all_to_all(block, PEERS, 0, 0)
    other = lax.ppermute(mine, "core", swap)
    tiles = (HALF // 8, CHUNKS, 8, 128)
    new_master, new_velocity, new_weights, new_bn, new_bn_velocity = pl.pallas_call(
        update_kernel,
        out_shape=(
            shape((16, 64), f32),
            shape((16, 64), f32),
            shape((CIN, COUT), bf16),
            shape((2, COUT), f32),
            shape((2, COUT), f32),
        ),
        in_specs=[SMEM] + [VMEM] * 8,
        out_specs=(VMEM,) * 5,
        scratch_shapes=[pltpu.VMEM((CIN, COUT), f32)],
        compiler_params=params(),
        name="update",
    )(place, mine.reshape(tiles), other.reshape(tiles), side_all, weights, master, velocity, bn_params, bn_velocity)
    return input_grad, new_master, new_velocity, new_weights, new_bn, new_bn_velocity


def solution(mesh):
    fine = Mesh(mesh.devices.reshape(4, 8, 8, 2), ALL)
    block = P(("x", "y"), ("z", "core"))
    return jax.shard_map(
        body,
        mesh=fine,
        in_specs=(P(ALL, None, None), P(ALL, None, None), P(ALL, None), P(), block, block, P(), P()),
        out_specs=(P(ALL, None, None), block, block, P(), P(), P()),
        check_vma=False,
    )
```

time: 565 us -> 145 us (0.26)
  the two profiles are of different devices: /device:TPU:1 before, /device:TPU:6 now
where the time goes in v1:
time: 145 us; the launch traced here: 144 us
  blocking collectives  66.3 us (46%)
  waiting for transfers between devices  23 us (16%)
  starting transfers between devices  15.5 us (11%)
  between operations  14.2 us (10%)
  local copies, waits for them, and re-layouts  12.7 us (9%)
  Pallas kernels  12.6 us (9%)
    all_to_all x1, blocking collectives, body(): arrived = lax.all_to_all(blocks.reshape(256, 8, 128), PEERS, 0, 0)  35.2 us
    all_to_all x1, blocking collectives, body(): mine = lax.all_to_all(block, PEERS, 0, 0)  31.1 us
    all_to_all x1, waiting for transfers between devices, body(): stats = lax.all_to_all(msg, GROUP, 0, 0)  13.6 us
    unnamed x38, local copies, waits for them, and re-layouts  12.7 us
    all_to_all x1, starting transfers between devices, body(): stats = lax.all_to_all(msg, GROUP, 0, 0)  10.4 us
    all_gather x1, waiting for transfers between devices, body(): side_all = lax.all_gather(side, ('x', 'y'), axis=0, tiled=True)  7.74 us
    pallas_call x1, Pallas kernels, body(): pl.pallas_call(grad_kernel, out_shape=(shape((ROWS, COUT), bf16), shape((...  4.02 us
    pallas_call x1, Pallas kernels, body(): pl.pallas_call(update_kernel, out_shape=(shape((16, 64), f32), shape((16,...  3.55 us
  transfers between devices with their start and end apart: 4, of which 3 were waited for; matrix products, arithmetic and copies ran while one was open for 0% of the time, Pallas kernels for 2%

profile of v1, /device:TPU:6, one launch (start us, length us, event | category | flops | bytes accessed | tf_op | source)
XLA Modules:
  0.0 144.4 jit_solution(13160422462749965689)
XLA Ops:
  7.2 0.0 copy-start
  7.2 1.2 copy-done
  8.4 0.0 copy-start.2
  8.4 1.3 copy-done.2
  9.7 0.0 copy-start.10
  9.7 1.1 copy-done.10
  10.8 0.0 copy-start.11
  10.8 0.8 copy-done.11
  11.7 0.0 copy-start.13
  11.7 0.7 copy-done.13
  12.4 0.0 copy-start.15
  12.4 0.7 copy-done.15
  13.1 0.0 copy-start.3
  13.1 0.0 copy-start.12
  13.1 0.0 copy-start.17
  13.1 2.7 %conv_stats.1 = (bf16[768,1024]{1,0:T(8,128)(2,1)S(1)}, bf16[768,512]{1,0:T(8,128)(2,1)S(1)}, f32[16,48,128]{2,1,0:T(8,128)}) custom-call(bf16[12,49,512]{2,1,0:T(8,128)(2,1)S(1)} %copy-done.10, bf16[12,49,1024]{2,1,0:T(8,128)(2,1)S(1)} %copy-done.2, f32[12,1024]{1,0:T(8,128)S(1)} %copy-done.11, bf16[512,1024]{1,0:T(8,128)(2,1)S(1)} %copy-done, ...), custom_call_target="tpu_custom_call" | custom-call | tf_op jit(solution)/shard_map/conv_stats/pallas_call | solution.py:193
  15.8 0.0 copy-start.4
  15.8 1.2 copy-done.4
  17.0 0.0 copy-start.8
  17.0 0.9 copy-done.8
  17.8 10.4 %all-to-all-start = ((f32[16,48,128]{2,1,0:T(8,128)}), f32[16,48,128]{2,1,0:T(8,128)S(1)}, u32[]{:S(2)}, u32[]{:S(2)}) async-start(f32[16,48,128]{2,1,0:T(8,128)} %get-tuple-element.18), calls=%async_computation | async-start | bytes 786432 | tf_op jit(solution)/shard_map/all_to_all | solution.py:201
  28.3 0.0 all-gather.2.cloned.1.call-start
  28.3 0.1 pad_add_fusion.core_ref.place_ref
  28.4 13.6 %all-to-all-done.stat_ref = f32[16,48,128]{2,1,0:T(8,128)S(1)} async-done(((f32[16,48,128]{2,1,0:T(8,128)}), f32[16,48,128]{2,1,0:T(8,128)S(1)}, u32[]{:S(2)}, u32[]{:S(2)}) %all-to-all-start) | async-done | bytes 393248 | tf_op jit(solution)/shard_map/all_to_all | solution.py:201
  42.0 0.0 copy-done.3
  42.0 0.0 copy-done.12
  42.0 0.0 copy-done.17
  42.0 0.0 copy-start.9
  42.0 1.1 copy-done.9
  43.1 4.0 %conv_grad.1 = (bf16[768,1024]{1,0:T(8,128)(2,1)S(1)}, f32[256,1024]{1,0:T(8,128)S(1)}, bf16[256,1024]{1,0:T(8,128)(2,1)}, bf16[24,1024]{1,0:T(8,128)(2,1)}) custom-call(s32[3]{0:T(128)S(1)} %pad_add_fusion.core_ref.place_ref, f32[16,48,128]{2,1,0:T(8,128)S(1)} %all-to-all-done.stat_ref, bf16[768,1024]{1,0:T(8,128)(2,1)} %copy-done.4, ...), custom_call_target="tpu_custom_call" | custom-call | tf_op jit(solution)/shard_map/conv_grad/pallas_call | solution.py:202
  47.1 0.0 copy-start.6
  47.1 1.0 copy-done.6
  48.1 3.2 %collective-permute-start = (bf16[256,1024]{1,0:T(8,128)(2,1)}, bf16[256,1024]{1,0:T(8,128)(2,1)S(1)}, u32[]{:S(2)}, u32[]{:S(2)}) collective-permute-start(bf16[256,1024]{1,0:T(8,128)(2,1)} %get-tuple-element.23), channel_id=1, source_target_pairs={{0,1},{1,0},{2,3},{3,2},{4,5},{5,4},{6,7},{7,6},{8,9},{9,8},{10,11... | collective-permute-start | bytes 1572872 | tf_op jit(solution)/shard_map/ppermute | solution.py:218
  51.3 0.0 all-gather.2.cloned.1.call-update
  51.3 1.7 %collective-permute-done.got_ref = bf16[256,1024]{1,0:T(8,128)(2,1)S(1)} collective-permute-done((bf16[256,1024]{1,0:T(8,128)(2,1)}, bf16[256,1024]{1,0:T(8,128)(2,1)S(1)}, u32[]{:S(2)}, u32[]{:S(2)}) %collective-permute-start) | collective-permute-done | bytes 524320 | tf_op jit(solution)/shard_map/ppermute | solution.py:218
  53.0 0.0 copy-start.7
  53.0 1.2 copy-done.7
  54.2 0.2 pair_sum.1
  54.4 0.0 copy-start.1
  54.4 35.2 %all_to_all.15.got_ref = bf16[256,8,128]{2,1,0:T(8,128)(2,1)S(1)} all-to-all(bf16[256,8,128]{2,1,0:T(8,128)(2,1)S(1)} %bitcast.7), channel_id=1, replica_groups=mesh['x'=4,'y'=8,'z'=8,'core'=2] {'x','y','z'}, dimensions={0} | all-to-all | bytes 1048576 | tf_op jit(solution)/shard_map/all_to_all | solution.py:236
  89.6 0.3 block_sum.1
  89.9 31.1 %all_to_all.16 = bf16[256,8,128]{2,1,0:T(8,128)(2,1)S(1)} all-to-all(bf16[256,8,128]{2,1,0:T(8,128)(2,1)S(1)} %block_sum.1), channel_id=1, replica_groups=mesh['x'=4,'y'=8,'z'=8,'core'=2] {'x','y','z'}, dimensions={0} | all-to-all | bytes 1048576 | tf_op jit(solution)/shard_map/all_to_all | solution.py:245
  121.0 1.9 %collective-permute-start.1 = (bf16[256,8,128]{2,1,0:T(8,128)(2,1)S(1)}, bf16[256,8,128]{2,1,0:T(8,128)(2,1)}, u32[]{:S(2)}, u32[]{:S(2)}) collective-permute-start(bf16[256,8,128]{2,1,0:T(8,128)(2,1)S(1)} %all_to_all.16), channel_id=1, source_target_pairs={{0,1},{1,0},{2,3},{3,2},{4,5},{5,4},{6,7},{7,6},{8,9},{9,8},{10,11... | collective-permute-start | bytes 1572872 | tf_op jit(solution)/shard_map/ppermute | solution.py:246
  122.9 0.0 copy-done.1
  123.0 0.0 copy-start.14
  123.0 0.0 copy-start.16
  123.0 0.0 copy-start.18
  123.0 1.9 %input_grad.1 = bf16[12,49,512]{2,1,0:T(8,128)(2,1)} custom-call(bf16[768,1024]{1,0:T(8,128)(2,1)S(1)} %get-tuple-element.21.cg_ref, bf16[512,1024]{1,0:T(8,128)(2,1)S(1)} %copy-done.1), custom_call_target="tpu_custom_call" | custom-call | flops 805306368 | bytes 4194304 | tf_op jit(solution)/shard_map/input_grad/pallas_call | solution.py:219
  124.9 7.7 %all-gather.2.cloned.1.call-done.side_ref = bf16[768,1024]{1,0:T(8,128)(2,1)} async-done(((bf16[24,1024]{1,0:T(8,128)(2,1)}), bf16[768,1024]{1,0:T(8,128)(2,1)}) %all-gather.2.cloned.1.call-update) | async-done | bytes 1572880 | tf_op jit(solution)/shard_map/all_gather | solution.py:216
  132.6 0.0 collective-permute-done.1
  132.6 0.0 copy-done.14
  132.6 0.0 copy-done.16
  132.6 0.0 copy-done.18
  132.6 0.0 copy-start.5
  132.6 1.4 copy-done.5
  134.0 3.5 %update.1 = (f32[16,64]{1,0:T(8,128)}, f32[16,64]{1,0:T(8,128)}, bf16[512,1024]{1,0:T(8,128)(2,1)}, f32[2,1024]{1,0:T(2,128)}, f32[2,1024]{1,0:T(2,128)}) custom-call(s32[3]{0:T(128)S(1)} %pad_add_fusion.core_ref.place_ref, bf16[32,8,8,128]{3,2,1,0:T(8,128)(2,1)S(1)} %bitcast.6, bf16[32,8,8,128]{3,2,1,0:T(8,128)(2,1)} %bitcast.5.other_ref, ...), custom_call_target="tpu_custom_call" | custom-call | tf_op jit(solution)/shard_map/update/pallas_call | solution.py:248
Async XLA Ops:
  7.2 1.2 copy-start
  8.4 1.3 copy-start.2
  9.7 1.1 copy-start.10
  10.8 0.8 copy-start.11
  11.7 0.7 copy-start.13
  12.4 0.7 copy-start.15
  13.1 28.9 %copy-start.3 = (bf16[12,49,1024]{2,1,0:T(8,128)(2,1)S(1)}, bf16[12,49,1024]{2,1,0:T(8,128)(2,1)}, u32[]{:S(2)}) copy-start(bf16[12,49,1024]{2,1,0:T(8,128)(2,1)} %pre_ref.3) | copy-start | bytes 3612676
  13.1 28.9 %copy-start.12 = (f32[12,1024]{1,0:T(8,128)S(1)}, f32[12,1024]{1,0:T(8,128)}, u32[]{:S(2)}) copy-start(f32[12,1024]{1,0:T(8,128)} %pool_ref.3) | copy-start | bytes 147460
  13.1 28.9 %copy-start.17 = (f32[2,1024]{1,0:T(2,128)S(1)}, f32[2,1024]{1,0:T(2,128)}, u32[]{:S(2)}) copy-start(f32[2,1024]{1,0:T(2,128)} %bn_ref.3) | copy-start | bytes 24580
  15.8 1.2 copy-start.4
  17.0 0.9 copy-start.8
  17.8 24.1 %all-to-all-start = ((f32[16,48,128]{2,1,0:T(8,128)}), f32[16,48,128]{2,1,0:T(8,128)S(1)}, u32[]{:S(2)}, u32[]{:S(2)}) async-start(f32[16,48,128]{2,1,0:T(8,128)} %get-tuple-element.18), calls=%async_computation | async-start | bytes 786432 | tf_op jit(solution)/shard_map/all_to_all | solution.py:201
  28.3 104.3 %all-gather.2.cloned.1.call-start = ((), (), s32[]{:S(2)}) async-start(), calls=%async_computation.3 | async-start | bytes 1622016 | tf_op jit(solution)/shard_map/all_gather | solution.py:216
  42.0 1.1 copy-start.9
  47.1 1.0 copy-start.6
  48.1 4.9 %collective-permute-start = (bf16[256,1024]{1,0:T(8,128)(2,1)}, bf16[256,1024]{1,0:T(8,128)(2,1)S(1)}, u32[]{:S(2)}, u32[]{:S(2)}) collective-permute-start(bf16[256,1024]{1,0:T(8,128)(2,1)} %get-tuple-element.23), channel_id=1, source_target_pairs={{0,1},{1,0},{2,3},{3,2},{4,5},{5,4},{6,7},{7,6},{8,9},{9,8},{10,11... | collective-permute-start | bytes 1572872 | tf_op jit(solution)/shard_map/ppermute | solution.py:218
  53.0 1.2 copy-start.7
  54.4 68.6 %copy-start.1 = (bf16[512,1024]{1,0:T(8,128)(2,1)S(1)}, bf16[512,1024]{1,0:T(8,128)(2,1)}, u32[]{:S(2)}) copy-start(bf16[512,1024]{1,0:T(8,128)(2,1)} %w_ref.5) | copy-start | bytes 3145732
  121.0 11.6 %collective-permute-start.1 = (bf16[256,8,128]{2,1,0:T(8,128)(2,1)S(1)}, bf16[256,8,128]{2,1,0:T(8,128)(2,1)}, u32[]{:S(2)}, u32[]{:S(2)}) collective-permute-start(bf16[256,8,128]{2,1,0:T(8,128)(2,1)S(1)} %all_to_all.16), channel_id=1, source_target_pairs={{0,1},{1,0},{2,3},{3,2},{4,5},{5,4},{6,7},{7,6},{8,9},{9,8},{10,11... | collective-permute-start | bytes 1572872 | tf_op jit(solution)/shard_map/ppermute | solution.py:246
  123.0 9.7 %copy-start.14 = (f32[16,64]{1,0:T(8,128)S(1)}, f32[16,64]{1,0:T(8,128)}, u32[]{:S(2)}) copy-start(f32[16,64]{1,0:T(8,128)} %master_ref.3) | copy-start | bytes 12292
  123.0 9.6 %copy-start.16 = (f32[16,64]{1,0:T(8,128)S(1)}, f32[16,64]{1,0:T(8,128)}, u32[]{:S(2)}) copy-start(f32[16,64]{1,0:T(8,128)} %vel_ref.3) | copy-start | bytes 12292
  123.0 9.6 %copy-start.18 = (f32[2,1024]{1,0:T(2,128)S(1)}, f32[2,1024]{1,0:T(2,128)}, u32[]{:S(2)}) copy-start(f32[2,1024]{1,0:T(2,128)} %bnv_ref.1) | copy-start | bytes 24580
  132.6 1.4 copy-start.5
Sparse Core Ops, SparseCore 0:
  51.4 81.1 all-gather.1

commit v2 on v1

v2 whole, which is shorter than its diff:
```python
import jax
import jax.numpy as jnp
from jax import lax
from jax.experimental import pallas as pl
from jax.experimental.pallas import tpu as pltpu
from jax.sharding import Mesh, PartitionSpec as P

epsilon = 1e-05
trust_coef = 0.001
weight_decay = 0.0001
momentum = 0.9
learn_rate = 12.0

IMG, PIX, STRIDE = 12, 49, 64
CIN, COUT = 512, 1024
ROWS = IMG * STRIDE
HALF = CIN // 2
N_ROW, N_COL, N_Z = 32, 16, 8
M = PIX * IMG * N_COL
BATCH = IMG * N_ROW * N_COL
CHUNKS = COUT // 128
GROUP, LAYER, PEERS, ALL = ("z", "core"), ("x", "y"), ("x", "y", "z"), ("x", "y", "z", "core")
STAT_ROWS = 40
SIDE_ROWS = 24
WIDE_ROWS = 528
PARTS = 4
bf16, f32 = jnp.bfloat16, jnp.float32


def params(megabytes=20):
    return pltpu.CompilerParams(vmem_limit_bytes=megabytes << 20)


def fold(line):
    return jnp.concatenate([line[:, 128 * k : 128 * k + 128] for k in range(line.shape[1] // 128)], axis=0)


def unfold(block):
    return jnp.concatenate([block[k : k + 1] for k in range(block.shape[0])], axis=1)


def split(line):
    high = line.astype(bf16).astype(f32)
    middle = (line - high).astype(bf16).astype(f32)
    return high, middle, line - high - middle


def rows_of(count, lines, dims):
    row = lax.broadcasted_iota(jnp.int32, dims, 0)
    block = jnp.zeros(dims, f32)
    for k in range(count):
        block = jnp.where(row == k, jnp.broadcast_to(lines[k], dims), block)
    return block


def stats_kernel(act_hbm, pre_hbm, pool_hbm, w_hbm, conv_hbm, msg_ref, act, pre, pool, w, actp, conv, sem_in, sem_out):
    step = IMG // PARTS
    loads = []
    for k in range(PARTS):
        part = pl.ds(step * k, step)
        strip = pl.ds(CIN // PARTS * k, CIN // PARTS)
        loads.append(pltpu.make_async_copy(w_hbm.at[strip], w.at[strip], sem_in.at[0, k]))
        loads.append(pltpu.make_async_copy(act_hbm.at[part], act.at[part], sem_in.at[1, k]))
    for copy in loads:
        copy.start()
    later = [pltpu.make_async_copy(pool_hbm, pool, sem_in.at[3, 0])]
    for k in range(PARTS):
        part = pl.ds(step * k, step)
        later.append(pltpu.make_async_copy(pre_hbm.at[part], pre.at[part], sem_in.at[2, k]))
    for copy in later:
        copy.start()
    actp[...] = jnp.zeros_like(actp)
    for copy in loads:
        copy.wait()
    for i in range(IMG):
        actp[STRIDE * i : STRIDE * i + PIX, :] = act[i]
    stores = []
    for k in range(2):
        strip = pl.ds(ROWS // 2 * k, ROWS // 2)
        conv[strip, :] = jnp.dot(actp[strip, :], w[...], preferred_element_type=f32).astype(bf16)
        stores.append(pltpu.make_async_copy(conv.at[strip], conv_hbm.at[strip], sem_out.at[k]))
        stores[-1].start()
    for copy in later:
        copy.wait()
    total = jnp.zeros((1, COUT), f32)
    square = jnp.zeros((1, COUT), f32)
    up = jnp.zeros((1, COUT), f32)
    up_conv = jnp.zeros((1, COUT), f32)
    for i in range(IMG):
        value = conv[STRIDE * i : STRIDE * i + STRIDE, :].astype(f32)
        total += jnp.sum(value, axis=0, keepdims=True)
        square += jnp.sum(value * value, axis=0, keepdims=True)
        passed = pre[i].astype(f32) > 0
        share = pool[i : i + 1, :] / PIX
        up += share * jnp.sum(jnp.where(passed, 1.0, 0.0), axis=0, keepdims=True)
        up_conv += share * jnp.sum(jnp.where(passed, value[:PIX], 0.0), axis=0, keepdims=True)
    act_total = jnp.sum(actp[...].astype(f32), axis=0, keepdims=True)
    msg = jnp.concatenate(
        [fold(total), fold(square), fold(up), fold(up_conv), fold(act_total), jnp.zeros((4, 128), f32)], axis=0
    )
    for p in range(N_COL):
        msg_ref[p] = msg
    for copy in stores:
        copy.wait()


def grad_kernel(
    place_ref, stat_ref, conv_ref, act_ref, pre_ref, pool_ref, bn_ref, cg_ref, keep_ref, send_ref, line_ref, actp, lines
):
    core, layer = place_ref[0], place_ref[3]
    sums = jnp.sum(stat_ref[...], axis=0)
    sum_up = sums[16:24]
    act_mean = (unfold(sums[32:36]) / M).astype(bf16).astype(f32)
    mean = sums[0:8] / M
    variance = sums[8:16] / M - mean * mean
    rstd = lax.rsqrt(variance + epsilon)
    sum_upx = rstd * (sums[24:32] - mean * sum_up)
    lines[0:8, :] = sum_up
    lines[8:16, :] = sum_upx
    line_ref[...] = jnp.broadcast_to(lines[pl.ds(core * 8 + layer, 1), :], (8, 128))
    scale = fold(bn_ref[0:1, :]) * rstd
    shift = unfold(scale * (sum_up / M))
    slope = unfold(scale * (sum_upx / M) * rstd)
    mean = unfold(mean)
    scale = unfold(scale)
    actp[...] = jnp.zeros_like(actp)
    for i in range(IMG):
        actp[STRIDE * i : STRIDE * i + PIX, :] = act_ref[i]
    cg_ref[...] = jnp.zeros_like(cg_ref)
    cg_total = jnp.zeros((1, COUT), f32)
    for i in range(IMG):
        conv = conv_ref[STRIDE * i : STRIDE * i + STRIDE, :].astype(f32)[:PIX]
        on = scale * (pool_ref[i : i + 1, :] / PIX) - shift
        low = (jnp.where(pre_ref[i].astype(f32) > 0, on, -shift) - slope * (conv - mean)).astype(bf16)
        cg_ref[STRIDE * i : STRIDE * i + PIX, :] = low
        cg_total += jnp.sum(low.astype(f32), axis=0, keepdims=True)
    edge = actp[48:64, :].astype(f32)
    row = lax.broadcasted_iota(jnp.int32, edge.shape, 0)
    actp[48:64, :] = jnp.where((row >= 1) & (row < 4), -act_mean, edge).astype(bf16)
    high, middle, rest = split(cg_total)
    edge = cg_ref[48:64, :].astype(f32)
    cg_ref[48:64, :] = (edge + rows_of(4, [jnp.zeros_like(high), high, middle, rest], edge.shape)).astype(bf16)
    for half, out_ref in ((1 - core, send_ref), (core, keep_ref)):
        columns = actp[:, pl.ds(pl.multiple_of(half * HALF, HALF), HALF)]
        part = lax.dot_general(columns, cg_ref[...], (((0,), (0,)), ((), ())), preferred_element_type=f32)
        out_ref[...] = part.astype(out_ref.dtype)


def back_kernel(cg_ref, w_ref, out_ref):
    back = lax.dot_general(cg_ref[...], w_ref[...], (((1,), (1,)), ((), ())), preferred_element_type=f32)
    for i in range(IMG):
        out_ref[i] = back[STRIDE * i : STRIDE * i + PIX].astype(bf16)


def pair_kernel(keep_ref, got_ref, out_ref):
    both = (keep_ref[...] + got_ref[...].astype(f32)).reshape(HALF // 8, 8, COUT)
    for j in range(CHUNKS):
        out_ref[:, j] = both[:, :, 128 * j : 128 * j + 128].astype(bf16)


def block_kernel(got_ref, line_ref, master_ref, vel_ref, out_ref):
    total = jnp.sum(got_ref[...].astype(f32), axis=0) * (1.0 / BATCH)
    master = master_ref[...]
    decayed = master - momentum * vel_ref[...]
    decayed = jnp.concatenate([decayed[:8], decayed[8:]], axis=1)
    norm = jnp.sum(jnp.sum(master * master, axis=1, keepdims=True), axis=0, keepdims=True)
    extra = rows_of(6, split(line_ref[...]) + split(jnp.broadcast_to(norm, (8, 128))), (8, 128))
    block = jnp.concatenate([total, decayed, extra], axis=0).astype(bf16)
    out_ref[...] = jnp.broadcast_to(block[None], out_ref.shape)


def layer_kernel(got_ref, out_ref):
    extra = jnp.sum(got_ref[:, 16:24, :].astype(f32), axis=0)
    line = extra[0:1] + extra[1:2] + extra[2:3]
    norm = extra[3:4] + extra[4:5] + extra[5:6]
    extra = rows_of(6, split(line) + split(norm), (16, 128)).astype(bf16)
    grad = got_ref[:, 0:8, :].astype(f32).reshape(HALF, 128).astype(bf16)
    decayed = got_ref[:, 8:16, :].astype(f32).reshape(HALF, 128).astype(bf16)
    for p in range(N_Z):
        out_ref[p, 0:256, :] = grad
        out_ref[p, 256:512, :] = decayed
        out_ref[p, 512:528, :] = extra


def update_kernel(
    place_ref, mine_ref, other_ref, w_ref, master_ref, vel_ref, bn_ref, bnv_ref,
    new_master_ref, new_vel_ref, new_w_hbm, new_bn_ref, new_bnv_ref, new_w, sems,
):
    core, row, col = place_ref[0], place_ref[1], place_ref[2]

    def run(parts):
        square = jnp.zeros((8, 128), f32)
        norm = jnp.zeros((1, 128), f32)
        totals = []
        for part in parts:
            line = []
            for z in range(N_Z):
                block = part[z, 0:256, :].astype(f32)
                square += jnp.sum((block * block).reshape(32, 8, 128), axis=0)
                extra = part[z, 512:528, :].astype(f32)
                line.append(extra[0:1] + extra[1:2] + extra[2:3])
                norm += extra[3:4] + extra[4:5] + extra[5:6]
            totals.append(jnp.concatenate(line, axis=1))
        grad_total = jnp.sum(jnp.sum(square, axis=1, keepdims=True), axis=0, keepdims=True)
        wnorm = jnp.sqrt(norm[:, 0:1])
        gnorm = jnp.sqrt(grad_total)
        rate = learn_rate * (trust_coef * wnorm / (gnorm + weight_decay * wnorm))
        stores = []
        for z in range(N_Z):
            even, odd = [part[z, 256:512, :].astype(f32).reshape(32, 8, 128) for part in parts]
            top = jnp.concatenate([even[:, :, :64], odd[:, :, :64]], axis=2)
            bottom = jnp.concatenate([even[:, :, 64:], odd[:, :, 64:]], axis=2)
            decayed = jnp.stack([top, bottom], axis=1).reshape(CIN, 128)
            columns = slice(128 * z, 128 * z + 128)
            for h in range(2):
                rows = slice(HALF * h, HALF * h + HALF)
                step = parts[h][z, 0:256, :].astype(f32) + weight_decay * w_ref[rows, columns].astype(f32)
                new_w[rows, columns] = (decayed[rows] - rate * step).astype(bf16)
            stores.append(pltpu.make_async_copy(new_w.at[:, columns], new_w_hbm.at[:, columns], sems.at[z]))
            stores[-1].start()
        bn_grad = jnp.concatenate([totals[1], totals[0]], axis=0) * (1.0 / BATCH)
        new_bnv = momentum * bnv_ref[...] + learn_rate * bn_grad
        new_bnv_ref[...] = new_bnv
        new_bn_ref[...] = bn_ref[...] - new_bnv
        for h in range(2):

            @pl.when(row // 16 == h)
            def _():
                pair = parts[h][col // 2, pl.ds(pl.multiple_of(row % 16 * 16, 16), 16), :].astype(f32)
                own = jnp.where(core == 0, pair[:, :64], pair[:, 64:])
                new_vel = momentum * vel_ref[...] + rate * (own + weight_decay * master_ref[...])
                new_vel_ref[...] = new_vel
                new_master_ref[...] = master_ref[...] - new_vel

        for copy in stores:
            copy.wait()

    @pl.when(core == 0)
    def _():
        run((mine_ref, other_ref))

    @pl.when(core == 1)
    def _():
        run((other_ref, mine_ref))


def shape(dims, kind):
    return jax.ShapeDtypeStruct(dims, kind)


SMEM = pl.BlockSpec(memory_space=pltpu.SMEM)
VMEM = pl.BlockSpec(memory_space=pltpu.VMEM)
HBM = pl.BlockSpec(memory_space=pltpu.HBM)


def body(activations, pre_activation, pooled_grad, weights, master, velocity, bn_params, bn_velocity):
    core = lax.axis_index("core").astype(jnp.int32)
    layer = lax.axis_index("z").astype(jnp.int32)
    row = (lax.axis_index("x") * 8 + lax.axis_index("y")).astype(jnp.int32)
    place = jnp.stack([core, row, layer * 2 + core, layer])
    conv, msg = pl.pallas_call(
        stats_kernel,
        out_shape=(shape((ROWS, COUT), bf16), shape((N_COL, STAT_ROWS, 128), f32)),
        in_specs=[HBM] * 4,
        out_specs=(HBM, VMEM),
        scratch_shapes=[
            pltpu.VMEM((IMG, PIX, CIN), bf16),
            pltpu.VMEM((IMG, PIX, COUT), bf16),
            pltpu.VMEM((IMG, COUT), f32),
            pltpu.VMEM((CIN, COUT), bf16),
            pltpu.VMEM((ROWS, CIN), bf16),
            pltpu.VMEM((ROWS, COUT), bf16),
            pltpu.SemaphoreType.DMA((4, PARTS)),
            pltpu.SemaphoreType.DMA((2,)),
        ],
        compiler_params=params(),
        name="conv_stats",
    )(activations, pre_activation, pooled_grad, weights)
    stats = lax.all_to_all(msg, GROUP, 0, 0)
    conv_grad, keep, send, line = pl.pallas_call(
        grad_kernel,
        out_shape=(
            shape((ROWS, COUT), bf16),
            shape((HALF, COUT), f32),
            shape((HALF, COUT), bf16),
            shape((8, 128), f32),
        ),
        in_specs=[SMEM] + [VMEM] * 6,
        out_specs=(VMEM,) * 4,
        scratch_shapes=[pltpu.VMEM((ROWS, CIN), bf16), pltpu.VMEM((16, 128), f32)],
        compiler_params=params(),
        name="conv_grad",
    )(place, stats, conv, activations, pre_activation, pooled_grad, bn_params)
    swap = [(0, 1), (1, 0)]
    got = lax.ppermute(send, "core", swap)
    input_grad = pl.pallas_call(
        back_kernel,
        out_shape=shape((IMG, PIX, CIN), bf16),
        in_specs=[VMEM] * 2,
        out_specs=VMEM,
        compiler_params=params(),
        cost_estimate=pl.CostEstimate(flops=2 * ROWS * CIN * COUT, bytes_accessed=4 << 20, transcendentals=0),
        name="input_grad",
    )(conv_grad, weights)
    blocks = pl.pallas_call(
        pair_kernel,
        out_shape=shape((HALF // 8, CHUNKS, 8, 128), bf16),
        in_specs=[VMEM] * 2,
        out_specs=VMEM,
        compiler_params=params(),
        name="pair_sum",
    )(keep, got)
    arrived = lax.all_to_all(blocks.reshape(256, 8, 128), PEERS, 0, 0)
    block = pl.pallas_call(
        block_kernel,
        out_shape=shape((N_ROW, SIDE_ROWS, 128), bf16),
        in_specs=[VMEM] * 4,
        out_specs=VMEM,
        compiler_params=params(),
        name="block_sum",
    )(arrived, line, master, velocity)
    wide = pl.pallas_call(
        layer_kernel,
        out_shape=shape((N_Z, WIDE_ROWS, 128), bf16),
        in_specs=[VMEM],
        out_specs=VMEM,
        compiler_params=params(),
        name="layer_join",
    )(lax.all_to_all(block, LAYER, 0, 0))
    mine = lax.all_to_all(wide, "z", 0, 0)
    other = lax.ppermute(mine, "core", swap)
    new_master, new_velocity, new_weights, new_bn, new_bn_velocity = pl.pallas_call(
        update_kernel,
        out_shape=(
            shape((16, 64), f32),
            shape((16, 64), f32),
            shape((CIN, COUT), bf16),
            shape((2, COUT), f32),
            shape((2, COUT), f32),
        ),
        in_specs=[SMEM] + [VMEM] * 7,
        out_specs=(VMEM, VMEM, HBM, VMEM, VMEM),
        scratch_shapes=[pltpu.VMEM((CIN, COUT), bf16), pltpu.SemaphoreType.DMA((N_Z,))],
        compiler_params=params(),
        name="update",
    )(place, mine, other, weights, master, velocity, bn_params, bn_velocity)
    return input_grad, new_master, new_velocity, new_weights, new_bn, new_bn_velocity


def solution(mesh):
    fine = Mesh(mesh.devices.reshape(4, 8, 8, 2), ALL)
    block = P(("x", "y"), ("z", "core"))
    return jax.shard_map(
        body,
        mesh=fine,
        in_specs=(P(ALL, None, None), P(ALL, None, None), P(ALL, None), P(), block, block, P(), P()),
        out_specs=(P(ALL, None, None), block, block, P(), P(), P()),
        check_vma=False,
    )
```

time: 145 us -> 133 us (0.917)
  the two profiles are of different devices: /device:TPU:6 before, /device:TPU:1 now
where the time goes in v2:
time: 133 us
  blocking collectives  75.2 us (57%)
  starting transfers between devices  20.9 us (16%)
  waiting for transfers between devices  15.3 us (12%)
  Pallas kernels  13.4 us (10%)
  local copies, waits for them, and re-layouts  7.1 us (5%)
    all_to_all x1, blocking collectives, body(): arrived = lax.all_to_all(blocks.reshape(256, 8, 128), PEERS, 0, 0)  32.8 us
    all_to_all x1, blocking collectives, body(): mine = lax.all_to_all(wide, 'z', 0, 0)  27.8 us
    all_to_all x1, blocking collectives, body(): lax.all_to_all(block, LAYER, 0, 0)  14.6 us
    all_to_all x1, waiting for transfers between devices, body(): stats = lax.all_to_all(msg, GROUP, 0, 0)  13 us
    all_to_all x1, starting transfers between devices, body(): stats = lax.all_to_all(msg, GROUP, 0, 0)  11.8 us
    ppermute x1, starting transfers between devices, body(): other = lax.ppermute(mine, 'core', swap)  7.15 us
    unnamed x28, local copies, waits for them, and re-layouts  7.1 us
    pallas_call x1, Pallas kernels, body(): pl.pallas_call(stats_kernel, out_shape=(shape((ROWS, COUT), bf16), shape(...  5.17 us
  transfers between devices with their start and end apart: 3, of which 3 were waited for; matrix products, arithmetic and copies ran while one was open for 0% of the time, Pallas kernels for 1%

profile of v2, /device:TPU:1, one launch (start us, length us, event | category | flops | bytes accessed | tf_op | source)
XLA Modules:
  0.0 132.7 jit_solution(12999388203299113317)
XLA Ops:
  0.6 0.0 copy-start
  0.6 1.2 copy-done
  1.9 0.0 copy-start.2
  1.9 1.3 %copy-done.2 = bf16[12,49,1024]{2,1,0:T(8,128)(2,1)S(1)} copy-done((bf16[12,49,1024]{2,1,0:T(8,128)(2,1)S(1)}, bf16[12,49,1024]{2,1,0:T(8,128)(2,1)}, u32[]{:S(2)}) %copy-start.2) | copy-done | bytes 1204248
  3.2 0.0 copy-start.4
  3.2 1.1 copy-done.4
  4.3 0.0 copy-start.8
  4.3 0.8 copy-done.8
  5.1 0.0 copy-start.3
  5.1 0.0 copy-start.5
  5.1 0.0 copy-start.9
  5.1 0.0 copy-start.10
  5.2 5.2 %conv_stats.1 = (bf16[768,1024]{1,0:T(8,128)(2,1)S(1)}, f32[16,40,128]{2,1,0:T(8,128)}) custom-call(bf16[12,49,512]{2,1,0:T(8,128)(2,1)S(1)} %copy-done.4, bf16[12,49,1024]{2,1,0:T(8,128)(2,1)S(1)} %copy-done.2, f32[12,1024]{1,0:T(8,128)S(1)} %copy-done.8, bf16[512,1024]{1,0:T(8,128)(2,1)S(1)} %copy-done), custom_call_target="tpu_custom_call" | custom-call | tf_op jit(solution)/shard_map/conv_stats/pallas_call | solution.py:261
  10.3 0.0 copy-start.6
  10.3 1.2 copy-done.6
  11.5 11.8 %all-to-all-start = ((f32[16,40,128]{2,1,0:T(8,128)}), f32[16,40,128]{2,1,0:T(8,128)S(1)}, u32[]{:S(2)}, u32[]{:S(2)}) async-start(f32[16,40,128]{2,1,0:T(8,128)} %get-tuple-element.17), calls=%async_computation | async-start | bytes 655360 | tf_op jit(solution)/shard_map/all_to_all | solution.py:279
  23.3 0.1 pad_add_fusion.place_ref
  23.4 13.0 %all-to-all-done.stat_ref = f32[16,40,128]{2,1,0:T(8,128)S(1)} async-done(((f32[16,40,128]{2,1,0:T(8,128)}), f32[16,40,128]{2,1,0:T(8,128)S(1)}, u32[]{:S(2)}, u32[]{:S(2)}) %all-to-all-start) | async-done | bytes 327712 | tf_op jit(solution)/shard_map/all_to_all | solution.py:279
  36.4 0.0 copy-done.3
  36.4 0.0 copy-done.5
  36.4 0.0 copy-done.9
  36.4 0.0 copy-done.10
  36.4 0.0 copy-start.7
  36.4 1.4 %copy-done.7 = bf16[768,1024]{1,0:T(8,128)(2,1)S(1)} copy-done((bf16[768,1024]{1,0:T(8,128)(2,1)S(1)}, bf16[768,1024]{1,0:T(8,128)(2,1)}, u32[]{:S(2)}) %copy-start.7) | copy-done | bytes 1572888
  37.8 2.7 %conv_grad.1 = (bf16[768,1024]{1,0:T(8,128)(2,1)S(1)}, f32[256,1024]{1,0:T(8,128)S(1)}, bf16[256,1024]{1,0:T(8,128)(2,1)S(1)}, f32[8,128]{1,0:T(8,128)S(1)}) custom-call(s32[4]{0:T(128)S(1)} %pad_add_fusion.place_ref, f32[16,40,128]{2,1,0:T(8,128)S(1)} %all-to-all-done.stat_ref, bf16[768,1024]{1,0:T(8,128)(2,1)S(1)} %copy-done.7, ...), custom_call_target="tpu_custom_call" | custom-call | tf_op jit(solution)/shard_map/conv_grad/pallas_call | solution.py:280
  40.5 1.9 %collective-permute-start = (bf16[256,1024]{1,0:T(8,128)(2,1)S(1)}, bf16[256,1024]{1,0:T(8,128)(2,1)S(1)}, u32[]{:S(2)}, u32[]{:S(2)}) collective-permute-start(bf16[256,1024]{1,0:T(8,128)(2,1)S(1)} %get-tuple-element.21), channel_id=1, source_target_pairs={{0,1},{1,0},{2,3},{3,2},{4,5},{5,4},{6,7},{7,6},{8,9},{9,8},{10,11... | collective-permute-start | bytes 1572872 | tf_op jit(solution)/shard_map/ppermute | solution.py:295
  42.4 1.9 %collective-permute-done.got_ref = bf16[256,1024]{1,0:T(8,128)(2,1)S(1)} collective-permute-done((bf16[256,1024]{1,0:T(8,128)(2,1)S(1)}, bf16[256,1024]{1,0:T(8,128)(2,1)S(1)}, u32[]{:S(2)}, u32[]{:S(2)}) %collective-permute-start) | collective-permute-done | bytes 524320 | tf_op jit(solution)/shard_map/ppermute | solution.py:295
  44.3 0.0 copy-start.11
  44.3 0.0 copy-start.12
  44.3 0.2 pair_sum.1
  44.5 32.8 %all_to_all.20.got_ref = bf16[256,8,128]{2,1,0:T(8,128)(2,1)S(1)} all-to-all(bf16[256,8,128]{2,1,0:T(8,128)(2,1)S(1)} %bitcast.5), channel_id=1, replica_groups=mesh['x'=4,'y'=8,'z'=8,'core'=2] {'x','y','z'}, dimensions={0} | all-to-all | bytes 1048576 | tf_op jit(solution)/shard_map/all_to_all | solution.py:313
  77.3 0.0 copy-done.11
  77.3 0.0 copy-done.12
  77.3 0.3 block_sum.1
  77.6 14.6 %all_to_all.21.got_ref = bf16[32,24,128]{2,1,0:T(8,128)(2,1)S(1)} all-to-all(bf16[32,24,128]{2,1,0:T(8,128)(2,1)S(1)} %block_sum.1), channel_id=1, replica_groups=mesh['x'=4,'y'=8,'z'=8,'core'=2] {'x','y'}, dimensions={0} | all-to-all | bytes 393216 | tf_op jit(solution)/shard_map/all_to_all | solution.py:329
  92.2 0.2 layer_join.1
  92.3 0.0 copy-start.1
  92.3 27.8 %all_to_all.22.mine_ref = bf16[8,528,128]{2,1,0:T(8,128)(2,1)S(1)} all-to-all(bf16[8,528,128]{2,1,0:T(8,128)(2,1)S(1)} %layer_join.1), channel_id=1, replica_groups=mesh['x'=4,'y'=8,'z'=8,'core'=2] {'z'}, dimensions={0} | all-to-all | bytes 2162688 | tf_op jit(solution)/shard_map/all_to_all | solution.py:330
  120.1 7.2 %collective-permute-start.1 = (bf16[8,528,128]{2,1,0:T(8,128)(2,1)S(1)}, bf16[8,528,128]{2,1,0:T(8,128)(2,1)S(1)}, u32[]{:S(2)}, u32[]{:S(2)}) collective-permute-start(bf16[8,528,128]{2,1,0:T(8,128)(2,1)S(1)} %all_to_all.22.mine_ref), channel_id=1, source_target_pairs={{0,1},{1,0},{2,3},{3,2},{4,5},{5,4},{6,7},{7,6},{8,9},{9,8},{10,11... | collective-permute-start | bytes 3244040 | tf_op jit(solution)/shard_map/ppermute | solution.py:331
  127.3 0.0 copy-done.1
  127.3 0.0 copy-start.13
  127.3 1.9 %input_grad.1 = bf16[12,49,512]{2,1,0:T(8,128)(2,1)} custom-call(bf16[768,1024]{1,0:T(8,128)(2,1)S(1)} %get-tuple-element.19.cg_ref, bf16[512,1024]{1,0:T(8,128)(2,1)S(1)} %copy-done.1), custom_call_target="tpu_custom_call" | custom-call | flops 805306368 | bytes 4194304 | tf_op jit(solution)/shard_map/input_grad/pallas_call | solution.py:296
  129.2 0.4 collective-permute-done.1.other_ref
  129.6 0.0 copy-done.13
  129.6 3.1 %update.1 = (f32[16,64]{1,0:T(8,128)}, f32[16,64]{1,0:T(8,128)}, bf16[512,1024]{1,0:T(8,128)(2,1)}, f32[2,1024]{1,0:T(2,128)}, f32[2,1024]{1,0:T(2,128)}) custom-call(s32[4]{0:T(128)S(1)} %pad_add_fusion.place_ref, bf16[8,528,128]{2,1,0:T(8,128)(2,1)S(1)} %all_to_all.22.mine_ref, bf16[8,528,128]{2,1,0:T(8,128)(2,1)S(1)} %collective-permute-done.1.other_ref, ...), custom_call_target="tpu_custom_call" | custom-call | tf_op jit(solution)/shard_map/update/pallas_call | solution.py:332
Async XLA Ops:
  0.6 1.2 copy-start
  1.9 1.3 %copy-start.2 = (bf16[12,49,1024]{2,1,0:T(8,128)(2,1)S(1)}, bf16[12,49,1024]{2,1,0:T(8,128)(2,1)}, u32[]{:S(2)}) copy-start(bf16[12,49,1024]{2,1,0:T(8,128)(2,1)} %pre_ref.1) | copy-start | bytes 3612676
  3.2 1.1 copy-start.4
  4.3 0.8 copy-start.8
  5.1 31.3 %copy-start.3 = (bf16[12,49,1024]{2,1,0:T(8,128)(2,1)S(1)}, bf16[12,49,1024]{2,1,0:T(8,128)(2,1)}, u32[]{:S(2)}) copy-start(bf16[12,49,1024]{2,1,0:T(8,128)(2,1)} %pre_ref.1) | copy-start | bytes 3612676
  5.1 31.3 %copy-start.5 = (bf16[12,49,512]{2,1,0:T(8,128)(2,1)S(1)}, bf16[12,49,512]{2,1,0:T(8,128)(2,1)}, u32[]{:S(2)}) copy-start(bf16[12,49,512]{2,1,0:T(8,128)(2,1)} %act_ref.1) | copy-start | bytes 1806340
  5.1 31.3 %copy-start.9 = (f32[12,1024]{1,0:T(8,128)S(1)}, f32[12,1024]{1,0:T(8,128)}, u32[]{:S(2)}) copy-start(f32[12,1024]{1,0:T(8,128)} %pool_ref.1) | copy-start | bytes 147460
  5.1 31.3 %copy-start.10 = (f32[2,1024]{1,0:T(2,128)S(1)}, f32[2,1024]{1,0:T(2,128)}, u32[]{:S(2)}) copy-start(f32[2,1024]{1,0:T(2,128)} %bn_ref.3) | copy-start | bytes 24580
  10.3 1.2 copy-start.6
  11.5 24.9 %all-to-all-start = ((f32[16,40,128]{2,1,0:T(8,128)}), f32[16,40,128]{2,1,0:T(8,128)S(1)}, u32[]{:S(2)}, u32[]{:S(2)}) async-start(f32[16,40,128]{2,1,0:T(8,128)} %get-tuple-element.17), calls=%async_computation | async-start | bytes 655360 | tf_op jit(solution)/shard_map/all_to_all | solution.py:279
  36.4 1.4 %copy-start.7 = (bf16[768,1024]{1,0:T(8,128)(2,1)S(1)}, bf16[768,1024]{1,0:T(8,128)(2,1)}, u32[]{:S(2)}) copy-start(bf16[768,1024]{1,0:T(8,128)(2,1)} %copy-done.6) | copy-start | bytes 4718596
  40.5 3.8 %collective-permute-start = (bf16[256,1024]{1,0:T(8,128)(2,1)S(1)}, bf16[256,1024]{1,0:T(8,128)(2,1)S(1)}, u32[]{:S(2)}, u32[]{:S(2)}) collective-permute-start(bf16[256,1024]{1,0:T(8,128)(2,1)S(1)} %get-tuple-element.21), channel_id=1, source_target_pairs={{0,1},{1,0},{2,3},{3,2},{4,5},{5,4},{6,7},{7,6},{8,9},{9,8},{10,11... | collective-permute-start | bytes 1572872 | tf_op jit(solution)/shard_map/ppermute | solution.py:295
  44.3 33.0 %copy-start.11 = (f32[16,64]{1,0:T(8,128)S(1)}, f32[16,64]{1,0:T(8,128)}, u32[]{:S(2)}) copy-start(f32[16,64]{1,0:T(8,128)} %master_ref.3) | copy-start | bytes 12292
  44.3 33.0 %copy-start.12 = (f32[16,64]{1,0:T(8,128)S(1)}, f32[16,64]{1,0:T(8,128)}, u32[]{:S(2)}) copy-start(f32[16,64]{1,0:T(8,128)} %vel_ref.3) | copy-start | bytes 12292
  92.3 34.9 %copy-start.1 = (bf16[512,1024]{1,0:T(8,128)(2,1)S(1)}, bf16[512,1024]{1,0:T(8,128)(2,1)}, u32[]{:S(2)}) copy-start(bf16[512,1024]{1,0:T(8,128)(2,1)} %w_ref.3) | copy-start | bytes 3145732
  120.1 9.5 %collective-permute-start.1 = (bf16[8,528,128]{2,1,0:T(8,128)(2,1)S(1)}, bf16[8,528,128]{2,1,0:T(8,128)(2,1)S(1)}, u32[]{:S(2)}, u32[]{:S(2)}) collective-permute-start(bf16[8,528,128]{2,1,0:T(8,128)(2,1)S(1)} %all_to_all.22.mine_ref), channel_id=1, source_target_pairs={{0,1},{1,0},{2,3},{3,2},{4,5},{5,4},{6,7},{7,6},{8,9},{9,8},{10,11... | collective-permute-start | bytes 3244040 | tf_op jit(solution)/shard_map/ppermute | solution.py:331
  127.3 2.3 %copy-start.13 = (f32[2,1024]{1,0:T(2,128)S(1)}, f32[2,1024]{1,0:T(2,128)}, u32[]{:S(2)}) copy-start(f32[2,1024]{1,0:T(2,128)} %bnv_ref.1) | copy-start | bytes 24580

commit v3 on v2

--- a/solution.py
+++ b/solution.py
@@ -53,7 +53,7 @@
     return block
 
 
-def stats_kernel(act_hbm, pre_hbm, pool_hbm, w_hbm, conv_hbm, msg_ref, act, pre, pool, w, actp, conv, sem_in, sem_out):
+def stats_kernel(act_hbm, pre_hbm, pool_hbm, w_hbm, msg_ref, act, pre, pool, w, actp, conv, sem_in):
     step = IMG // PARTS
     loads = []
     for k in range(PARTS):
@@ -74,12 +74,7 @@
         copy.wait()
     for i in range(IMG):
         actp[STRIDE * i : STRIDE * i + PIX, :] = act[i]
-    stores = []
-    for k in range(2):
-        strip = pl.ds(ROWS // 2 * k, ROWS // 2)
-        conv[strip, :] = jnp.dot(actp[strip, :], w[...], preferred_element_type=f32).astype(bf16)
-        stores.append(pltpu.make_async_copy(conv.at[strip], conv_hbm.at[strip], sem_out.at[k]))
-        stores[-1].start()
+    conv[...] = jnp.dot(actp[...], w[...], preferred_element_type=f32).astype(bf16)
     for copy in later:
         copy.wait()
     total = jnp.zeros((1, COUT), f32)
@@ -100,12 +95,10 @@
     )
     for p in range(N_COL):
         msg_ref[p] = msg
-    for copy in stores:
-        copy.wait()
 
 
 def grad_kernel(
-    place_ref, stat_ref, conv_ref, act_ref, pre_ref, pool_ref, bn_ref, cg_ref, keep_ref, send_ref, line_ref, actp, lines
+    place_ref, stat_ref, w_ref, act_ref, pre_ref, pool_ref, bn_ref, cg_ref, keep_ref, send_ref, line_ref, actp, conv_ref, lines
 ):
     core, layer = place_ref[0], place_ref[3]
     sums = jnp.sum(stat_ref[...], axis=0)
@@ -126,6 +119,7 @@
     actp[...] = jnp.zeros_like(actp)
     for i in range(IMG):
         actp[STRIDE * i : STRIDE * i + PIX, :] = act_ref[i]
+    conv_ref[...] = jnp.dot(actp[...], w_ref[...], preferred_element_type=f32).astype(bf16)
     cg_ref[...] = jnp.zeros_like(cg_ref)
     cg_total = jnp.zeros((1, COUT), f32)
     for i in range(IMG):
@@ -258,11 +252,11 @@
     layer = lax.axis_index("z").astype(jnp.int32)
     row = (lax.axis_index("x") * 8 + lax.axis_index("y")).astype(jnp.int32)
     place = jnp.stack([core, row, layer * 2 + core, layer])
-    conv, msg = pl.pallas_call(
+    msg = pl.pallas_call(
         stats_kernel,
-        out_shape=(shape((ROWS, COUT), bf16), shape((N_COL, STAT_ROWS, 128), f32)),
+        out_shape=shape((N_COL, STAT_ROWS, 128), f32),
         in_specs=[HBM] * 4,
-        out_specs=(HBM, VMEM),
+        out_specs=VMEM,
         scratch_shapes=[
             pltpu.VMEM((IMG, PIX, CIN), bf16),
             pltpu.VMEM((IMG, PIX, COUT), bf16),
@@ -271,9 +265,8 @@
             pltpu.VMEM((ROWS, CIN), bf16),
             pltpu.VMEM((ROWS, COUT), bf16),
             pltpu.SemaphoreType.DMA((4, PARTS)),
-            pltpu.SemaphoreType.DMA((2,)),
         ],
-        compiler_params=params(),
+        compiler_params=params(60),
         name="conv_stats",
     )(activations, pre_activation, pooled_grad, weights)
     stats = lax.all_to_all(msg, GROUP, 0, 0)
@@ -287,10 +280,10 @@
         ),
         in_specs=[SMEM] + [VMEM] * 6,
         out_specs=(VMEM,) * 4,
-        scratch_shapes=[pltpu.VMEM((ROWS, CIN), bf16), pltpu.VMEM((16, 128), f32)],
+        scratch_shapes=[pltpu.VMEM((ROWS, CIN), bf16), pltpu.VMEM((ROWS, COUT), bf16), pltpu.VMEM((16, 128), f32)],
         compiler_params=params(),
         name="conv_grad",
-    )(place, stats, conv, activations, pre_activation, pooled_grad, bn_params)
+    )(place, stats, weights, activations, pre_activation, pooled_grad, bn_params)
     swap = [(0, 1), (1, 0)]
     got = lax.ppermute(send, "core", swap)
     input_grad = pl.pallas_call(

time: 133 us -> 126 us (0.947)
  local copies, waits for them, and re-layouts: 7.1 us -> 0.04 us
    unnamed x28 -> x16, local copies, waits for them, and re-layouts: 7.1 us -> 0.04 us
where the time goes in v3:
time: 126 us
  blocking collectives  75 us (60%)
  starting transfers between devices  21 us (17%)
  waiting for transfers between devices  15.3 us (12%)
  Pallas kernels  13.5 us (11%)
    all_to_all x1, blocking collectives, body(): arrived = lax.all_to_all(blocks.reshape(256, 8, 128), PEERS, 0, 0)  32.8 us
    all_to_all x1, blocking collectives, body(): mine = lax.all_to_all(wide, 'z', 0, 0)  27.6 us
    all_to_all x1, blocking collectives, body(): lax.all_to_all(block, LAYER, 0, 0)  14.6 us
    all_to_all x1, waiting for transfers between devices, body(): stats = lax.all_to_all(msg, GROUP, 0, 0)  13 us
    all_to_all x1, starting transfers between devices, body(): stats = lax.all_to_all(msg, GROUP, 0, 0)  12 us
    ppermute x1, starting transfers between devices, body(): other = lax.ppermute(mine, 'core', swap)  7.15 us
    pallas_call x1, Pallas kernels, body(): pl.pallas_call(stats_kernel, out_shape=shape((N_COL, STAT_ROWS, 128), f32...  4.96 us
    pallas_call x1, Pallas kernels, body(): pl.pallas_call(update_kernel, out_shape=(shape((16, 64), f32), shape((16,...  3.09 us
  transfers between devices with their start and end apart: 3, of which 3 were waited for; matrix products, arithmetic and copies ran while one was open for 0% of the time, Pallas kernels for 1%

profile of v3, /device:TPU:1, one launch (start us, length us, event | category | flops | bytes accessed | tf_op | source)
XLA Modules:
  0.0 125.7 jit_solution(1276230161552023947)
XLA Ops:
  0.6 0.0 copy-start.3
  0.6 0.0 copy-start.4
  0.7 0.0 copy-start
  0.7 0.0 copy-start.1
  0.7 5.0 %conv_stats.1 = f32[16,40,128]{2,1,0:T(8,128)} custom-call(bf16[12,49,512]{2,1,0:T(8,128)(2,1)} %act_ref.1, bf16[12,49,1024]{2,1,0:T(8,128)(2,1)} %pre_ref.1, f32[12,1024]{1,0:T(8,128)} %pool_ref.1, bf16[512,1024]{1,0:T(8,128)(2,1)} %w_ref.5), custom_call_target="tpu_custom_call" | custom-call | tf_op jit(solution)/shard_map/conv_stats/pallas_call | solution.py:255
  5.6 0.0 copy-start.2
  5.7 12.0 %all-to-all-start = ((f32[16,40,128]{2,1,0:T(8,128)}), f32[16,40,128]{2,1,0:T(8,128)S(1)}, u32[]{:S(2)}, u32[]{:S(2)}) async-start(f32[16,40,128]{2,1,0:T(8,128)} %conv_stats.1), calls=%async_computation | async-start | bytes 655360 | tf_op jit(solution)/shard_map/all_to_all | solution.py:272
  17.6 0.1 pad_add_fusion.place_ref
  17.7 13.0 %all-to-all-done.stat_ref = f32[16,40,128]{2,1,0:T(8,128)S(1)} async-done(((f32[16,40,128]{2,1,0:T(8,128)}), f32[16,40,128]{2,1,0:T(8,128)S(1)}, u32[]{:S(2)}, u32[]{:S(2)}) %all-to-all-start) | async-done | bytes 327712 | tf_op jit(solution)/shard_map/all_to_all | solution.py:272
  30.7 0.0 copy-done.3
  30.7 0.0 copy-done.4
  30.7 0.0 copy-done
  30.7 0.0 copy-done.1
  30.7 0.0 copy-done.2
  30.7 3.0 %conv_grad.1 = (bf16[768,1024]{1,0:T(8,128)(2,1)S(1)}, f32[256,1024]{1,0:T(8,128)S(1)}, bf16[256,1024]{1,0:T(8,128)(2,1)S(1)}, f32[8,128]{1,0:T(8,128)S(1)}) custom-call(s32[4]{0:T(128)S(1)} %pad_add_fusion.place_ref, f32[16,40,128]{2,1,0:T(8,128)S(1)} %all-to-all-done.stat_ref, bf16[512,1024]{1,0:T(8,128)(2,1)S(1)} %copy-done, ...), custom_call_target="tpu_custom_call" | custom-call | tf_op jit(solution)/shard_map/conv_grad/pallas_call | solution.py:273
  33.7 1.9 %collective-permute-start = (bf16[256,1024]{1,0:T(8,128)(2,1)S(1)}, bf16[256,1024]{1,0:T(8,128)(2,1)S(1)}, u32[]{:S(2)}, u32[]{:S(2)}) collective-permute-start(bf16[256,1024]{1,0:T(8,128)(2,1)S(1)} %get-tuple-element.17), channel_id=1, source_target_pairs={{0,1},{1,0},{2,3},{3,2},{4,5},{5,4},{6,7},{7,6},{8,9},{9,8},{10,11... | collective-permute-start | bytes 1572872 | tf_op jit(solution)/shard_map/ppermute | solution.py:288
  35.6 1.9 %collective-permute-done.got_ref = bf16[256,1024]{1,0:T(8,128)(2,1)S(1)} collective-permute-done((bf16[256,1024]{1,0:T(8,128)(2,1)S(1)}, bf16[256,1024]{1,0:T(8,128)(2,1)S(1)}, u32[]{:S(2)}, u32[]{:S(2)}) %collective-permute-start) | collective-permute-done | bytes 524320 | tf_op jit(solution)/shard_map/ppermute | solution.py:288
  37.5 0.0 copy-start.5
  37.5 0.0 copy-start.6
  37.5 0.2 pair_sum.1
  37.7 32.8 %all_to_all.20.got_ref = bf16[256,8,128]{2,1,0:T(8,128)(2,1)S(1)} all-to-all(bf16[256,8,128]{2,1,0:T(8,128)(2,1)S(1)} %bitcast.5), channel_id=1, replica_groups=mesh['x'=4,'y'=8,'z'=8,'core'=2] {'x','y','z'}, dimensions={0} | all-to-all | bytes 1048576 | tf_op jit(solution)/shard_map/all_to_all | solution.py:306
  70.5 0.0 copy-done.5
  70.5 0.0 copy-done.6
  70.5 0.3 block_sum.1
  70.8 14.6 %all_to_all.21.got_ref = bf16[32,24,128]{2,1,0:T(8,128)(2,1)S(1)} all-to-all(bf16[32,24,128]{2,1,0:T(8,128)(2,1)S(1)} %block_sum.1), channel_id=1, replica_groups=mesh['x'=4,'y'=8,'z'=8,'core'=2] {'x','y'}, dimensions={0} | all-to-all | bytes 393216 | tf_op jit(solution)/shard_map/all_to_all | solution.py:322
  85.4 0.2 layer_join.1
  85.5 27.6 %all_to_all.22.mine_ref = bf16[8,528,128]{2,1,0:T(8,128)(2,1)S(1)} all-to-all(bf16[8,528,128]{2,1,0:T(8,128)(2,1)S(1)} %layer_join.1), channel_id=1, replica_groups=mesh['x'=4,'y'=8,'z'=8,'core'=2] {'z'}, dimensions={0} | all-to-all | bytes 2162688 | tf_op jit(solution)/shard_map/all_to_all | solution.py:323
  113.2 7.2 %collective-permute-start.1 = (bf16[8,528,128]{2,1,0:T(8,128)(2,1)S(1)}, bf16[8,528,128]{2,1,0:T(8,128)(2,1)S(1)}, u32[]{:S(2)}, u32[]{:S(2)}) collective-permute-start(bf16[8,528,128]{2,1,0:T(8,128)(2,1)S(1)} %all_to_all.22.mine_ref), channel_id=1, source_target_pairs={{0,1},{1,0},{2,3},{3,2},{4,5},{5,4},{6,7},{7,6},{8,9},{9,8},{10,11... | collective-permute-start | bytes 3244040 | tf_op jit(solution)/shard_map/ppermute | solution.py:324
  120.3 0.0 copy-start.7
  120.3 1.9 %input_grad.1 = bf16[12,49,512]{2,1,0:T(8,128)(2,1)} custom-call(bf16[768,1024]{1,0:T(8,128)(2,1)S(1)} %get-tuple-element.15.cg_ref, bf16[512,1024]{1,0:T(8,128)(2,1)S(1)} %copy-done), custom_call_target="tpu_custom_call" | custom-call | flops 805306368 | bytes 4194304 | tf_op jit(solution)/shard_map/input_grad/pallas_call | solution.py:289
  122.2 0.4 collective-permute-done.1.other_ref
  122.6 0.0 copy-done.7
  122.6 3.1 %update.1 = (f32[16,64]{1,0:T(8,128)}, f32[16,64]{1,0:T(8,128)}, bf16[512,1024]{1,0:T(8,128)(2,1)}, f32[2,1024]{1,0:T(2,128)}, f32[2,1024]{1,0:T(2,128)}) custom-call(s32[4]{0:T(128)S(1)} %pad_add_fusion.place_ref, bf16[8,528,128]{2,1,0:T(8,128)(2,1)S(1)} %all_to_all.22.mine_ref, bf16[8,528,128]{2,1,0:T(8,128)(2,1)S(1)} %collective-permute-done.1.other_ref, ...), custom_call_target="tpu_custom_call" | custom-call | tf_op jit(solution)/shard_map/update/pallas_call | solution.py:325
Async XLA Ops:
  0.6 30.1 %copy-start.3 = (f32[12,1024]{1,0:T(8,128)S(1)}, f32[12,1024]{1,0:T(8,128)}, u32[]{:S(2)}) copy-start(f32[12,1024]{1,0:T(8,128)} %pool_ref.1) | copy-start | bytes 147460
  0.6 30.1 %copy-start.4 = (f32[2,1024]{1,0:T(2,128)S(1)}, f32[2,1024]{1,0:T(2,128)}, u32[]{:S(2)}) copy-start(f32[2,1024]{1,0:T(2,128)} %bn_ref.3) | copy-start | bytes 24580
  0.7 30.1 %copy-start = (bf16[512,1024]{1,0:T(8,128)(2,1)S(1)}, bf16[512,1024]{1,0:T(8,128)(2,1)}, u32[]{:S(2)}) copy-start(bf16[512,1024]{1,0:T(8,128)(2,1)} %w_ref.5) | copy-start | bytes 3145732
  0.7 30.0 %copy-start.1 = (bf16[12,49,1024]{2,1,0:T(8,128)(2,1)S(1)}, bf16[12,49,1024]{2,1,0:T(8,128)(2,1)}, u32[]{:S(2)}) copy-start(bf16[12,49,1024]{2,1,0:T(8,128)(2,1)} %pre_ref.1) | copy-start | bytes 3612676
  5.6 25.1 %copy-start.2 = (bf16[12,49,512]{2,1,0:T(8,128)(2,1)S(1)}, bf16[12,49,512]{2,1,0:T(8,128)(2,1)}, u32[]{:S(2)}) copy-start(bf16[12,49,512]{2,1,0:T(8,128)(2,1)} %act_ref.1) | copy-start | bytes 1806340
  5.7 25.0 %all-to-all-start = ((f32[16,40,128]{2,1,0:T(8,128)}), f32[16,40,128]{2,1,0:T(8,128)S(1)}, u32[]{:S(2)}, u32[]{:S(2)}) async-start(f32[16,40,128]{2,1,0:T(8,128)} %conv_stats.1), calls=%async_computation | async-start | bytes 655360 | tf_op jit(solution)/shard_map/all_to_all | solution.py:272
  33.7 3.8 %collective-permute-start = (bf16[256,1024]{1,0:T(8,128)(2,1)S(1)}, bf16[256,1024]{1,0:T(8,128)(2,1)S(1)}, u32[]{:S(2)}, u32[]{:S(2)}) collective-permute-start(bf16[256,1024]{1,0:T(8,128)(2,1)S(1)} %get-tuple-element.17), channel_id=1, source_target_pairs={{0,1},{1,0},{2,3},{3,2},{4,5},{5,4},{6,7},{7,6},{8,9},{9,8},{10,11... | collective-permute-start | bytes 1572872 | tf_op jit(solution)/shard_map/ppermute | solution.py:288
  37.5 33.0 %copy-start.5 = (f32[16,64]{1,0:T(8,128)S(1)}, f32[16,64]{1,0:T(8,128)}, u32[]{:S(2)}) copy-start(f32[16,64]{1,0:T(8,128)} %master_ref.3) | copy-start | bytes 12292
  37.5 33.0 %copy-start.6 = (f32[16,64]{1,0:T(8,128)S(1)}, f32[16,64]{1,0:T(8,128)}, u32[]{:S(2)}) copy-start(f32[16,64]{1,0:T(8,128)} %vel_ref.3) | copy-start | bytes 12292
  113.2 9.5 %collective-permute-start.1 = (bf16[8,528,128]{2,1,0:T(8,128)(2,1)S(1)}, bf16[8,528,128]{2,1,0:T(8,128)(2,1)S(1)}, u32[]{:S(2)}, u32[]{:S(2)}) collective-permute-start(bf16[8,528,128]{2,1,0:T(8,128)(2,1)S(1)} %all_to_all.22.mine_ref), channel_id=1, source_target_pairs={{0,1},{1,0},{2,3},{3,2},{4,5},{5,4},{6,7},{7,6},{8,9},{9,8},{10,11... | collective-permute-start | bytes 3244040 | tf_op jit(solution)/shard_map/ppermute | solution.py:324
  120.3 2.3 %copy-start.7 = (f32[2,1024]{1,0:T(2,128)S(1)}, f32[2,1024]{1,0:T(2,128)}, u32[]{:S(2)}) copy-start(f32[2,1024]{1,0:T(2,128)} %bnv_ref.1) | copy-start | bytes 24580

commit v4 on v3

--- a/solution.py
+++ b/solution.py
@@ -15,15 +15,17 @@
 CIN, COUT = 512, 1024
 ROWS = IMG * STRIDE
 HALF = CIN // 2
-N_ROW, N_COL, N_Z = 32, 16, 8
+N_ROW, N_COL = 32, 16
+N_X, N_Y, N_Z = 4, 8, 8
 M = PIX * IMG * N_COL
 BATCH = IMG * N_ROW * N_COL
 CHUNKS = COUT // 128
-GROUP, LAYER, PEERS, ALL = ("z", "core"), ("x", "y"), ("x", "y", "z"), ("x", "y", "z", "core")
+GROUP, PLANE, ALL = ("z", "core"), ("y", "z"), ("x", "y", "z", "core")
 STAT_ROWS = 40
 SIDE_ROWS = 24
-WIDE_ROWS = 528
-PARTS = 4
+WIDE_ROWS = 1056
+PARTS = 2
+STRIP = 512
 bf16, f32 = jnp.bfloat16, jnp.float32
 
 
@@ -74,25 +76,30 @@
         copy.wait()
     for i in range(IMG):
         actp[STRIDE * i : STRIDE * i + PIX, :] = act[i]
-    conv[...] = jnp.dot(actp[...], w[...], preferred_element_type=f32).astype(bf16)
+    act_total = jnp.sum(actp[...].astype(f32), axis=0, keepdims=True)
+    strips = [slice(STRIP * k, STRIP * k + STRIP) for k in range(COUT // STRIP)]
+    lines = []
+    for strip in strips:
+        value = jnp.dot(actp[...], w[:, strip], preferred_element_type=f32).astype(bf16)
+        conv[:, strip] = value
+        value = value.astype(f32)
+        total = jnp.sum(value, axis=0, keepdims=True)
+        square = jnp.sum(value * value, axis=0, keepdims=True)
+        lines.append([total, square])
     for copy in later:
         copy.wait()
-    total = jnp.zeros((1, COUT), f32)
-    square = jnp.zeros((1, COUT), f32)
-    up = jnp.zeros((1, COUT), f32)
-    up_conv = jnp.zeros((1, COUT), f32)
-    for i in range(IMG):
-        value = conv[STRIDE * i : STRIDE * i + STRIDE, :].astype(f32)
-        total += jnp.sum(value, axis=0, keepdims=True)
-        square += jnp.sum(value * value, axis=0, keepdims=True)
-        passed = pre[i].astype(f32) > 0
-        share = pool[i : i + 1, :] / PIX
-        up += share * jnp.sum(jnp.where(passed, 1.0, 0.0), axis=0, keepdims=True)
-        up_conv += share * jnp.sum(jnp.where(passed, value[:PIX], 0.0), axis=0, keepdims=True)
-    act_total = jnp.sum(actp[...].astype(f32), axis=0, keepdims=True)
-    msg = jnp.concatenate(
-        [fold(total), fold(square), fold(up), fold(up_conv), fold(act_total), jnp.zeros((4, 128), f32)], axis=0
-    )
+    for k, strip in enumerate(strips):
+        up = jnp.zeros((1, STRIP), f32)
+        up_conv = jnp.zeros((1, STRIP), f32)
+        for i in range(IMG):
+            value = conv[STRIDE * i : STRIDE * i + STRIDE, strip].astype(f32)[:PIX]
+            passed = pre[i, :, strip].astype(f32) > 0
+            share = pool[i : i + 1, strip] / PIX
+            up += share * jnp.sum(jnp.where(passed, 1.0, 0.0), axis=0, keepdims=True)
+            up_conv += share * jnp.sum(jnp.where(passed, value, 0.0), axis=0, keepdims=True)
+        lines[k] += [up, up_conv]
+    sums = [fold(jnp.concatenate([line[q] for line in lines], axis=1)) for q in range(4)]
+    msg = jnp.concatenate(sums + [fold(act_total), jnp.zeros((4, 128), f32)], axis=0)
     for p in range(N_COL):
         msg_ref[p] = msg
 
@@ -147,9 +154,13 @@
 
 
 def pair_kernel(keep_ref, got_ref, out_ref):
-    both = (keep_ref[...] + got_ref[...].astype(f32)).reshape(HALF // 8, 8, COUT)
-    for j in range(CHUNKS):
-        out_ref[:, j] = both[:, :, 128 * j : 128 * j + 128].astype(bf16)
+    out_ref[...] = (keep_ref[...] + got_ref[...].astype(f32)).astype(bf16)
+
+
+def line_kernel(got_ref, out_ref):
+    total = jnp.sum(got_ref[...].astype(f32), axis=0).reshape(N_Z, 8, COUT)
+    for y in range(N_Y):
+        out_ref[y] = total[:, :, 128 * y : 128 * y + 128].astype(bf16)
 
 
 def block_kernel(got_ref, line_ref, master_ref, vel_ref, out_ref):
@@ -163,54 +174,62 @@
     out_ref[...] = jnp.broadcast_to(block[None], out_ref.shape)
 
 
-def layer_kernel(got_ref, out_ref):
-    extra = jnp.sum(got_ref[:, 16:24, :].astype(f32), axis=0)
-    line = extra[0:1] + extra[1:2] + extra[2:3]
-    norm = extra[3:4] + extra[4:5] + extra[5:6]
-    extra = rows_of(6, split(line) + split(norm), (16, 128)).astype(bf16)
-    grad = got_ref[:, 0:8, :].astype(f32).reshape(HALF, 128).astype(bf16)
-    decayed = got_ref[:, 8:16, :].astype(f32).reshape(HALF, 128).astype(bf16)
-    for p in range(N_Z):
-        out_ref[p, 0:256, :] = grad
-        out_ref[p, 256:512, :] = decayed
-        out_ref[p, 512:528, :] = extra
+def plane_kernel(got_ref, out_ref):
+    extra = jnp.sum(got_ref[:, 16:24, :].astype(f32).reshape(N_Y, N_Z, 8, 128), axis=0)
+    lines = []
+    norm = jnp.zeros((1, 128), f32)
+    for z in range(N_Z):
+        lines += split(extra[z, 0:1] + extra[z, 1:2] + extra[z, 2:3])
+        norm += extra[z, 3:4] + extra[z, 4:5] + extra[z, 5:6]
+    lines += split(norm)
+    extra = jnp.concatenate(lines + [jnp.zeros((5, 128), f32)], axis=0).astype(bf16)
+    grad = got_ref[:, 0:8, :].astype(f32).reshape(512, 128).astype(bf16)
+    decayed = got_ref[:, 8:16, :].astype(f32).reshape(512, 128).astype(bf16)
+    for p in range(N_X):
+        out_ref[p, 0:512, :] = grad
+        out_ref[p, 512:1024, :] = decayed
+        out_ref[p, 1024:1056, :] = extra
 
 
 def update_kernel(
     place_ref, mine_ref, other_ref, w_ref, master_ref, vel_ref, bn_ref, bnv_ref,
     new_master_ref, new_vel_ref, new_w_hbm, new_bn_ref, new_bnv_ref, new_w, sems,
 ):
-    core, row, col = place_ref[0], place_ref[1], place_ref[2]
+    core, row, layer = place_ref[0], place_ref[1], place_ref[3]
 
     def run(parts):
         square = jnp.zeros((8, 128), f32)
         norm = jnp.zeros((1, 128), f32)
         totals = []
         for part in parts:
-            line = []
-            for z in range(N_Z):
-                block = part[z, 0:256, :].astype(f32)
-                square += jnp.sum((block * block).reshape(32, 8, 128), axis=0)
-                extra = part[z, 512:528, :].astype(f32)
-                line.append(extra[0:1] + extra[1:2] + extra[2:3])
-                norm += extra[3:4] + extra[4:5] + extra[5:6]
+            extra = jnp.zeros((32, 128), f32)
+            for x in range(N_X):
+                block = part[x, 0:512, :].astype(f32)
+                square += jnp.sum((block * block).reshape(64, 8, 128), axis=0)
+                extra += part[x, 1024:1056, :].astype(f32)
+            line = [extra[3 * z : 3 * z + 1] + extra[3 * z + 1 : 3 * z + 2] + extra[3 * z + 2 : 3 * z + 3] for z in range(N_Z)]
+            norm += extra[24:25] + extra[25:26] + extra[26:27]
             totals.append(jnp.concatenate(line, axis=1))
         grad_total = jnp.sum(jnp.sum(square, axis=1, keepdims=True), axis=0, keepdims=True)
         wnorm = jnp.sqrt(norm[:, 0:1])
         gnorm = jnp.sqrt(grad_total)
         rate = learn_rate * (trust_coef * wnorm / (gnorm + weight_decay * wnorm))
         stores = []
-        for z in range(N_Z):
-            even, odd = [part[z, 256:512, :].astype(f32).reshape(32, 8, 128) for part in parts]
-            top = jnp.concatenate([even[:, :, :64], odd[:, :, :64]], axis=2)
-            bottom = jnp.concatenate([even[:, :, 64:], odd[:, :, 64:]], axis=2)
-            decayed = jnp.stack([top, bottom], axis=1).reshape(CIN, 128)
-            columns = slice(128 * z, 128 * z + 128)
-            for h in range(2):
-                rows = slice(HALF * h, HALF * h + HALF)
-                step = parts[h][z, 0:256, :].astype(f32) + weight_decay * w_ref[rows, columns].astype(f32)
-                new_w[rows, columns] = (decayed[rows] - rate * step).astype(bf16)
-            stores.append(pltpu.make_async_copy(new_w.at[:, columns], new_w_hbm.at[:, columns], sems.at[z]))
+        for x in range(N_X):
+            tiles = [part[x, 512:1024, :].astype(f32).reshape(N_Y, N_Z, 8, 128) for part in parts]
+            rows = slice(128 * x, 128 * x + 128)
+            h, strip = x // 2, x % 2 * 2
+            for z in range(N_Z):
+                columns = slice(128 * z, 128 * z + 128)
+                even, odd = [tile[:, z] for tile in tiles]
+                top = jnp.concatenate([even[:, :, :64], odd[:, :, :64]], axis=2)
+                bottom = jnp.concatenate([even[:, :, 64:], odd[:, :, 64:]], axis=2)
+                decayed = jnp.stack([top, bottom], axis=1).reshape(128, 128)
+                lines = slice(64 * z, 64 * z + 64)
+                step = jnp.concatenate([parts[h][strip, lines, :], parts[h][strip + 1, lines, :]], axis=0).astype(f32)
+                step += weight_decay * w_ref[rows, columns].astype(f32)
+                new_w[rows, columns] = (decayed - rate * step).astype(bf16)
+            stores.append(pltpu.make_async_copy(new_w.at[rows], new_w_hbm.at[rows], sems.at[x]))
             stores[-1].start()
         bn_grad = jnp.concatenate([totals[1], totals[0]], axis=0) * (1.0 / BATCH)
         new_bnv = momentum * bnv_ref[...] + learn_rate * bn_grad
@@ -220,7 +239,8 @@
 
             @pl.when(row // 16 == h)
             def _():
-                pair = parts[h][col // 2, pl.ds(pl.multiple_of(row % 16 * 16, 16), 16), :].astype(f32)
+                start = pl.multiple_of(layer * 64 + row % 4 * 16, 16)
+                pair = parts[h][row % 16 // 4, pl.ds(start, 16), :].astype(f32)
                 own = jnp.where(core == 0, pair[:, :64], pair[:, 64:])
                 new_vel = momentum * vel_ref[...] + rate * (own + weight_decay * master_ref[...])
                 new_vel_ref[...] = new_vel
@@ -295,32 +315,41 @@
         cost_estimate=pl.CostEstimate(flops=2 * ROWS * CIN * COUT, bytes_accessed=4 << 20, transcendentals=0),
         name="input_grad",
     )(conv_grad, weights)
-    blocks = pl.pallas_call(
+    halves = pl.pallas_call(
         pair_kernel,
-        out_shape=shape((HALF // 8, CHUNKS, 8, 128), bf16),
+        out_shape=shape((HALF, COUT), bf16),
         in_specs=[VMEM] * 2,
         out_specs=VMEM,
         compiler_params=params(),
         name="pair_sum",
     )(keep, got)
-    arrived = lax.all_to_all(blocks.reshape(256, 8, 128), PEERS, 0, 0)
+    arrived = lax.all_to_all(halves.reshape(N_X, HALF // N_X, COUT), "x", 0, 0)
+    lines = pl.pallas_call(
+        line_kernel,
+        out_shape=shape((N_Y, N_Z, 8, 128), bf16),
+        in_specs=[VMEM],
+        out_specs=VMEM,
+        compiler_params=params(),
+        name="line_sum",
+    )(arrived)
+    arrived = lax.all_to_all(lines.reshape(N_Y * N_Z, 8, 128), PLANE, 0, 0)
     block = pl.pallas_call(
         block_kernel,
-        out_shape=shape((N_ROW, SIDE_ROWS, 128), bf16),
+        out_shape=shape((N_Y * N_Z, SIDE_ROWS, 128), bf16),
         in_specs=[VMEM] * 4,
         out_specs=VMEM,
         compiler_params=params(),
         name="block_sum",
     )(arrived, line, master, velocity)
     wide = pl.pallas_call(
-        layer_kernel,
-        out_shape=shape((N_Z, WIDE_ROWS, 128), bf16),
+        plane_kernel,
+        out_shape=shape((N_X, WIDE_ROWS, 128), bf16),
         in_specs=[VMEM],
         out_specs=VMEM,
         compiler_params=params(),
-        name="layer_join",
-    )(lax.all_to_all(block, LAYER, 0, 0))
-    mine = lax.all_to_all(wide, "z", 0, 0)
+        name="plane_join",
+    )(lax.all_to_all(block, PLANE, 0, 0))
+    mine = lax.all_to_all(wide, "x", 0, 0)
     other = lax.ppermute(mine, "core", swap)
     new_master, new_velocity, new_weights, new_bn, new_bn_velocity = pl.pallas_call(
         update_kernel,
@@ -333,7 +362,7 @@
         ),
         in_specs=[SMEM] + [VMEM] * 7,
         out_specs=(VMEM, VMEM, HBM, VMEM, VMEM),
-        scratch_shapes=[pltpu.VMEM((CIN, COUT), bf16), pltpu.SemaphoreType.DMA((N_Z,))],
+        scratch_shapes=[pltpu.VMEM((CIN, COUT), bf16), pltpu.SemaphoreType.DMA((N_X,))],
         compiler_params=params(),
         name="update",
     )(place, mine, other, weights, master, velocity, bn_params, bn_velocity)

time: 126 us -> 114 us (0.905)
  blocking collectives: 75 us -> 62.9 us
    all_to_all x3 -> x4, blocking collectives: 75 us -> 62.9 us  [the longest x1 19.3 us: body(): arrived = lax.all_to_all(lines.reshape(N_Y * N_Z, 8, 128), PLANE, 0, 0)]
  transfers between devices with their start and end apart: 3 -> 3, of which waited for: 3 -> 3; matrix products, arithmetic and copies ran while one was open for 0% -> 0% of each run, Pallas kernels for 1% -> 2%
where the time goes in v4:
time: 114 us; the launch traced here: 113 us
  blocking collectives  62.9 us (55%)
  starting transfers between devices  21.4 us (19%)
  waiting for transfers between devices  15.3 us (13%)
  Pallas kernels  12.9 us (11%)
    all_to_all x1, blocking collectives, body(): arrived = lax.all_to_all(lines.reshape(N_Y * N_Z, 8, 128), PLANE, 0, 0)  19.3 us
    all_to_all x1, blocking collectives, body(): lax.all_to_all(block, PLANE, 0, 0)  17.4 us
    all_to_all x1, blocking collectives, body(): mine = lax.all_to_all(wide, 'x', 0, 0)  13.2 us
    all_to_all x1, waiting for transfers between devices, body(): stats = lax.all_to_all(msg, GROUP, 0, 0)  13 us
    all_to_all x1, blocking collectives, body(): arrived = lax.all_to_all(halves.reshape(N_X, HALF // N_X, COUT), 'x', 0, 0)  13 us
    all_to_all x1, starting transfers between devices, body(): stats = lax.all_to_all(msg, GROUP, 0, 0)  12 us
    ppermute x1, starting transfers between devices, body(): other = lax.ppermute(mine, 'core', swap)  7.53 us
    pallas_call x1, Pallas kernels, body(): pl.pallas_call(stats_kernel, out_shape=shape((N_COL, STAT_ROWS, 128), f32...  4.43 us
  transfers between devices with their start and end apart: 3, of which 3 were waited for; matrix products, arithmetic and copies ran while one was open for 0% of the time, Pallas kernels for 2%

profile of v4, /device:TPU:1, one launch (start us, length us, event | category | flops | bytes accessed | tf_op | source)
XLA Modules:
  0.0 113.3 jit_solution(16065865274909516320)
XLA Ops:
  0.6 0.0 copy-start.3
  0.6 0.0 copy-start.4
  0.7 0.0 copy-start
  0.7 0.0 copy-start.1
  0.7 4.4 %conv_stats.1 = f32[16,40,128]{2,1,0:T(8,128)} custom-call(bf16[12,49,512]{2,1,0:T(8,128)(2,1)} %act_ref.1, bf16[12,49,1024]{2,1,0:T(8,128)(2,1)} %pre_ref.1, f32[12,1024]{1,0:T(8,128)} %pool_ref.1, bf16[512,1024]{1,0:T(8,128)(2,1)} %w_ref.5), custom_call_target="tpu_custom_call" | custom-call | tf_op jit(solution)/shard_map/conv_stats/pallas_call | solution.py:275
  5.1 0.0 copy-start.2
  5.1 12.0 %all-to-all-start = ((f32[16,40,128]{2,1,0:T(8,128)}), f32[16,40,128]{2,1,0:T(8,128)S(1)}, u32[]{:S(2)}, u32[]{:S(2)}) async-start(f32[16,40,128]{2,1,0:T(8,128)} %conv_stats.1), calls=%async_computation | async-start | bytes 655360 | tf_op jit(solution)/shard_map/all_to_all | solution.py:292
  17.1 0.1 pad_add_fusion.place_ref
  17.2 13.0 %all-to-all-done.stat_ref = f32[16,40,128]{2,1,0:T(8,128)S(1)} async-done(((f32[16,40,128]{2,1,0:T(8,128)}), f32[16,40,128]{2,1,0:T(8,128)S(1)}, u32[]{:S(2)}, u32[]{:S(2)}) %all-to-all-start) | async-done | bytes 327712 | tf_op jit(solution)/shard_map/all_to_all | solution.py:292
  30.2 0.0 copy-done.3
  30.2 0.0 copy-done.4
  30.2 0.0 copy-done
  30.2 0.0 copy-done.1
  30.2 0.0 copy-done.2
  30.2 3.0 %conv_grad.1 = (bf16[768,1024]{1,0:T(8,128)(2,1)S(1)}, f32[256,1024]{1,0:T(8,128)S(1)}, bf16[256,1024]{1,0:T(8,128)(2,1)S(1)}, f32[8,128]{1,0:T(8,128)S(1)}) custom-call(s32[4]{0:T(128)S(1)} %pad_add_fusion.place_ref, f32[16,40,128]{2,1,0:T(8,128)S(1)} %all-to-all-done.stat_ref, bf16[512,1024]{1,0:T(8,128)(2,1)S(1)} %copy-done, ...), custom_call_target="tpu_custom_call" | custom-call | tf_op jit(solution)/shard_map/conv_grad/pallas_call | solution.py:293
  33.2 1.9 %collective-permute-start = (bf16[256,1024]{1,0:T(8,128)(2,1)S(1)}, bf16[256,1024]{1,0:T(8,128)(2,1)S(1)}, u32[]{:S(2)}, u32[]{:S(2)}) collective-permute-start(bf16[256,1024]{1,0:T(8,128)(2,1)S(1)} %get-tuple-element.17), channel_id=1, source_target_pairs={{0,1},{1,0},{2,3},{3,2},{4,5},{5,4},{6,7},{7,6},{8,9},{9,8},{10,11... | collective-permute-start | bytes 1572872 | tf_op jit(solution)/shard_map/ppermute | solution.py:308
  35.1 1.9 %collective-permute-done.got_ref = bf16[256,1024]{1,0:T(8,128)(2,1)S(1)} collective-permute-done((bf16[256,1024]{1,0:T(8,128)(2,1)S(1)}, bf16[256,1024]{1,0:T(8,128)(2,1)S(1)}, u32[]{:S(2)}, u32[]{:S(2)}) %collective-permute-start) | collective-permute-done | bytes 524320 | tf_op jit(solution)/shard_map/ppermute | solution.py:308
  37.0 0.1 pair_sum.1
  37.1 0.0 copy-start.5
  37.1 0.0 copy-start.6
  37.1 13.0 %all_to_all.25.got_ref = bf16[4,64,1024]{2,1,0:T(8,128)(2,1)S(1)} all-to-all(bf16[4,64,1024]{2,1,0:T(8,128)(2,1)S(1)} %bitcast.6), channel_id=1, replica_groups=mesh['x'=4,'y'=8,'z'=8,'core'=2] {'x'}, dimensions={0} | all-to-all | bytes 1048576 | tf_op jit(solution)/shard_map/all_to_all | solution.py:326
  50.1 0.1 line_sum.1
  50.2 19.3 %all_to_all.26.got_ref = bf16[64,8,128]{2,1,0:T(8,128)(2,1)S(1)} all-to-all(bf16[64,8,128]{2,1,0:T(8,128)(2,1)S(1)} %bitcast.7), channel_id=1, replica_groups=mesh['x'=4,'y'=8,'z'=8,'core'=2] {'y','z'}, dimensions={0} | all-to-all | bytes 262144 | tf_op jit(solution)/shard_map/all_to_all | solution.py:335
  69.5 0.0 copy-done.5
  69.5 0.0 copy-done.6
  69.5 0.1 block_sum.1
  69.6 17.4 %all_to_all.27.got_ref = bf16[64,24,128]{2,1,0:T(8,128)(2,1)S(1)} all-to-all(bf16[64,24,128]{2,1,0:T(8,128)(2,1)S(1)} %block_sum.1), channel_id=1, replica_groups=mesh['x'=4,'y'=8,'z'=8,'core'=2] {'y','z'}, dimensions={0} | all-to-all | bytes 786432 | tf_op jit(solution)/shard_map/all_to_all | solution.py:351
  87.0 0.2 plane_join.1
  87.2 13.2 %all_to_all.28.mine_ref = bf16[4,1056,128]{2,1,0:T(8,128)(2,1)S(1)} all-to-all(bf16[4,1056,128]{2,1,0:T(8,128)(2,1)S(1)} %plane_join.1), channel_id=1, replica_groups=mesh['x'=4,'y'=8,'z'=8,'core'=2] {'x'}, dimensions={0} | all-to-all | bytes 2162688 | tf_op jit(solution)/shard_map/all_to_all | solution.py:352
  100.3 7.5 %collective-permute-start.1 = (bf16[4,1056,128]{2,1,0:T(8,128)(2,1)S(1)}, bf16[4,1056,128]{2,1,0:T(8,128)(2,1)S(1)}, u32[]{:S(2)}, u32[]{:S(2)}) collective-permute-start(bf16[4,1056,128]{2,1,0:T(8,128)(2,1)S(1)} %all_to_all.28.mine_ref), channel_id=1, source_target_pairs={{0,1},{1,0},{2,3},{3,2},{4,5},{5,4},{6,7},{7,6},{8,9},{9,8},{10,11... | collective-permute-start | bytes 3244040 | tf_op jit(solution)/shard_map/ppermute | solution.py:353
  107.9 0.0 copy-start.7
  107.9 1.9 %input_grad.1 = bf16[12,49,512]{2,1,0:T(8,128)(2,1)} custom-call(bf16[768,1024]{1,0:T(8,128)(2,1)S(1)} %get-tuple-element.15.cg_ref, bf16[512,1024]{1,0:T(8,128)(2,1)S(1)} %copy-done), custom_call_target="tpu_custom_call" | custom-call | flops 805306368 | bytes 4194304 | tf_op jit(solution)/shard_map/input_grad/pallas_call | solution.py:309
  109.7 0.4 collective-permute-done.1.other_ref
  110.2 0.0 copy-done.7
  110.2 3.2 %update.1 = (f32[16,64]{1,0:T(8,128)}, f32[16,64]{1,0:T(8,128)}, bf16[512,1024]{1,0:T(8,128)(2,1)}, f32[2,1024]{1,0:T(2,128)}, f32[2,1024]{1,0:T(2,128)}) custom-call(s32[4]{0:T(128)S(1)} %pad_add_fusion.place_ref, bf16[4,1056,128]{2,1,0:T(8,128)(2,1)S(1)} %all_to_all.28.mine_ref, bf16[4,1056,128]{2,1,0:T(8,128)(2,1)S(1)} %collective-permute-done.1.other_ref, ...), custom_call_target="tpu_custom_call" | custom-call | tf_op jit(solution)/shard_map/update/pallas_call | solution.py:354
Async XLA Ops:
  0.6 29.5 %copy-start.3 = (f32[12,1024]{1,0:T(8,128)S(1)}, f32[12,1024]{1,0:T(8,128)}, u32[]{:S(2)}) copy-start(f32[12,1024]{1,0:T(8,128)} %pool_ref.1) | copy-start | bytes 147460
  0.6 29.5 %copy-start.4 = (f32[2,1024]{1,0:T(2,128)S(1)}, f32[2,1024]{1,0:T(2,128)}, u32[]{:S(2)}) copy-start(f32[2,1024]{1,0:T(2,128)} %bn_ref.3) | copy-start | bytes 24580
  0.7 29.5 %copy-start = (bf16[512,1024]{1,0:T(8,128)(2,1)S(1)}, bf16[512,1024]{1,0:T(8,128)(2,1)}, u32[]{:S(2)}) copy-start(bf16[512,1024]{1,0:T(8,128)(2,1)} %w_ref.5) | copy-start | bytes 3145732
  0.7 29.5 %copy-start.1 = (bf16[12,49,1024]{2,1,0:T(8,128)(2,1)S(1)}, bf16[12,49,1024]{2,1,0:T(8,128)(2,1)}, u32[]{:S(2)}) copy-start(bf16[12,49,1024]{2,1,0:T(8,128)(2,1)} %pre_ref.1) | copy-start | bytes 3612676
  5.1 25.1 %copy-start.2 = (bf16[12,49,512]{2,1,0:T(8,128)(2,1)S(1)}, bf16[12,49,512]{2,1,0:T(8,128)(2,1)}, u32[]{:S(2)}) copy-start(bf16[12,49,512]{2,1,0:T(8,128)(2,1)} %act_ref.1) | copy-start | bytes 1806340
  5.1 25.0 %all-to-all-start = ((f32[16,40,128]{2,1,0:T(8,128)}), f32[16,40,128]{2,1,0:T(8,128)S(1)}, u32[]{:S(2)}, u32[]{:S(2)}) async-start(f32[16,40,128]{2,1,0:T(8,128)} %conv_stats.1), calls=%async_computation | async-start | bytes 655360 | tf_op jit(solution)/shard_map/all_to_all | solution.py:292
  33.2 3.8 %collective-permute-start = (bf16[256,1024]{1,0:T(8,128)(2,1)S(1)}, bf16[256,1024]{1,0:T(8,128)(2,1)S(1)}, u32[]{:S(2)}, u32[]{:S(2)}) collective-permute-start(bf16[256,1024]{1,0:T(8,128)(2,1)S(1)} %get-tuple-element.17), channel_id=1, source_target_pairs={{0,1},{1,0},{2,3},{3,2},{4,5},{5,4},{6,7},{7,6},{8,9},{9,8},{10,11... | collective-permute-start | bytes 1572872 | tf_op jit(solution)/shard_map/ppermute | solution.py:308
  37.1 32.4 %copy-start.5 = (f32[16,64]{1,0:T(8,128)S(1)}, f32[16,64]{1,0:T(8,128)}, u32[]{:S(2)}) copy-start(f32[16,64]{1,0:T(8,128)} %master_ref.3) | copy-start | bytes 12292
  37.1 32.4 %copy-start.6 = (f32[16,64]{1,0:T(8,128)S(1)}, f32[16,64]{1,0:T(8,128)}, u32[]{:S(2)}) copy-start(f32[16,64]{1,0:T(8,128)} %vel_ref.3) | copy-start | bytes 12292
  100.3 9.9 %collective-permute-start.1 = (bf16[4,1056,128]{2,1,0:T(8,128)(2,1)S(1)}, bf16[4,1056,128]{2,1,0:T(8,128)(2,1)S(1)}, u32[]{:S(2)}, u32[]{:S(2)}) collective-permute-start(bf16[4,1056,128]{2,1,0:T(8,128)(2,1)S(1)} %all_to_all.28.mine_ref), channel_id=1, source_target_pairs={{0,1},{1,0},{2,3},{3,2},{4,5},{5,4},{6,7},{7,6},{8,9},{9,8},{10,11... | collective-permute-start | bytes 3244040 | tf_op jit(solution)/shard_map/ppermute | solution.py:353
  107.9 2.3 %copy-start.7 = (f32[2,1024]{1,0:T(2,128)S(1)}, f32[2,1024]{1,0:T(2,128)}, u32[]{:S(2)}) copy-start(f32[2,1024]{1,0:T(2,128)} %bnv_ref.1) | copy-start | bytes 24580

commit v5 on v4

--- a/solution.py
+++ b/solution.py
@@ -20,7 +20,7 @@
 M = PIX * IMG * N_COL
 BATCH = IMG * N_ROW * N_COL
 CHUNKS = COUT // 128
-GROUP, PLANE, ALL = ("z", "core"), ("y", "z"), ("x", "y", "z", "core")
+PLANE, ALL = ("y", "z"), ("x", "y", "z", "core")
 STAT_ROWS = 40
 SIDE_ROWS = 24
 WIDE_ROWS = 1056
@@ -100,12 +100,15 @@
         lines[k] += [up, up_conv]
     sums = [fold(jnp.concatenate([line[q] for line in lines], axis=1)) for q in range(4)]
     msg = jnp.concatenate(sums + [fold(act_total), jnp.zeros((4, 128), f32)], axis=0)
-    for p in range(N_COL):
-        msg_ref[p] = msg
+    msg_ref[...] = msg
+
+
+def chip_kernel(got_ref, out_ref):
+    out_ref[...] = jnp.broadcast_to((got_ref[0] + got_ref[1])[None], out_ref.shape)
 
 
 def grad_kernel(
-    place_ref, stat_ref, w_ref, act_ref, pre_ref, pool_ref, bn_ref, cg_ref, keep_ref, send_ref, line_ref, actp, conv_ref, lines
+    place_ref, stat_ref, w_ref, act_ref, pre_ref, pool_ref, bn_ref, cg_ref, actp, send_ref, line_ref, conv_ref, lines
 ):
     core, layer = place_ref[0], place_ref[3]
     sums = jnp.sum(stat_ref[...], axis=0)
@@ -141,10 +144,16 @@
     high, middle, rest = split(cg_total)
     edge = cg_ref[48:64, :].astype(f32)
     cg_ref[48:64, :] = (edge + rows_of(4, [jnp.zeros_like(high), high, middle, rest], edge.shape)).astype(bf16)
-    for half, out_ref in ((1 - core, send_ref), (core, keep_ref)):
-        columns = actp[:, pl.ds(pl.multiple_of(half * HALF, HALF), HALF)]
-        part = lax.dot_general(columns, cg_ref[...], (((0,), (0,)), ((), ())), preferred_element_type=f32)
-        out_ref[...] = part.astype(out_ref.dtype)
+    send_ref[...] = half_grad(actp, cg_ref, 1 - core).astype(bf16)
+
+
+def half_grad(actp, cg_ref, half):
+    columns = actp[:, pl.ds(pl.multiple_of(half * HALF, HALF), HALF)]
+    return lax.dot_general(columns, cg_ref[...], (((0,), (0,)), ((), ())), preferred_element_type=f32)
+
+
+def keep_kernel(place_ref, actp, cg_ref, keep_ref):
+    keep_ref[...] = half_grad(actp, cg_ref, place_ref[0])
 
 
 def back_kernel(cg_ref, w_ref, out_ref):
@@ -169,7 +178,9 @@
     decayed = master - momentum * vel_ref[...]
     decayed = jnp.concatenate([decayed[:8], decayed[8:]], axis=1)
     norm = jnp.sum(jnp.sum(master * master, axis=1, keepdims=True), axis=0, keepdims=True)
-    extra = rows_of(6, split(line_ref[...]) + split(jnp.broadcast_to(norm, (8, 128))), (8, 128))
+    square = jnp.sum(jnp.sum(total * total, axis=1, keepdims=True), axis=0, keepdims=True)
+    norms = split(jnp.broadcast_to(norm, (8, 128))) + split(jnp.broadcast_to(square, (8, 128)))[:2]
+    extra = rows_of(8, split(line_ref[...]) + norms, (8, 128))
     block = jnp.concatenate([total, decayed, extra], axis=0).astype(bf16)
     out_ref[...] = jnp.broadcast_to(block[None], out_ref.shape)
 
@@ -178,11 +189,13 @@
     extra = jnp.sum(got_ref[:, 16:24, :].astype(f32).reshape(N_Y, N_Z, 8, 128), axis=0)
     lines = []
     norm = jnp.zeros((1, 128), f32)
+    square = jnp.zeros((1, 128), f32)
     for z in range(N_Z):
         lines += split(extra[z, 0:1] + extra[z, 1:2] + extra[z, 2:3])
         norm += extra[z, 3:4] + extra[z, 4:5] + extra[z, 5:6]
-    lines += split(norm)
-    extra = jnp.concatenate(lines + [jnp.zeros((5, 128), f32)], axis=0).astype(bf16)
+        square += extra[z, 6:7] + extra[z, 7:8]
+    lines += split(norm) + split(square)
+    extra = jnp.concatenate(lines + [jnp.zeros((2, 128), f32)], axis=0).astype(bf16)
     grad = got_ref[:, 0:8, :].astype(f32).reshape(512, 128).astype(bf16)
     decayed = got_ref[:, 8:16, :].astype(f32).reshape(512, 128).astype(bf16)
     for p in range(N_X):
@@ -198,21 +211,19 @@
     core, row, layer = place_ref[0], place_ref[1], place_ref[3]
 
     def run(parts):
-        square = jnp.zeros((8, 128), f32)
+        square = jnp.zeros((1, 128), f32)
         norm = jnp.zeros((1, 128), f32)
         totals = []
         for part in parts:
             extra = jnp.zeros((32, 128), f32)
             for x in range(N_X):
-                block = part[x, 0:512, :].astype(f32)
-                square += jnp.sum((block * block).reshape(64, 8, 128), axis=0)
                 extra += part[x, 1024:1056, :].astype(f32)
             line = [extra[3 * z : 3 * z + 1] + extra[3 * z + 1 : 3 * z + 2] + extra[3 * z + 2 : 3 * z + 3] for z in range(N_Z)]
             norm += extra[24:25] + extra[25:26] + extra[26:27]
+            square += extra[27:28] + extra[28:29] + extra[29:30]
             totals.append(jnp.concatenate(line, axis=1))
-        grad_total = jnp.sum(jnp.sum(square, axis=1, keepdims=True), axis=0, keepdims=True)
         wnorm = jnp.sqrt(norm[:, 0:1])
-        gnorm = jnp.sqrt(grad_total)
+        gnorm = jnp.sqrt(square[:, 0:1])
         rate = learn_rate * (trust_coef * wnorm / (gnorm + weight_decay * wnorm))
         stores = []
         for x in range(N_X):
@@ -274,7 +285,7 @@
     place = jnp.stack([core, row, layer * 2 + core, layer])
     msg = pl.pallas_call(
         stats_kernel,
-        out_shape=shape((N_COL, STAT_ROWS, 128), f32),
+        out_shape=shape((STAT_ROWS, 128), f32),
         in_specs=[HBM] * 4,
         out_specs=VMEM,
         scratch_shapes=[
@@ -289,23 +300,40 @@
         compiler_params=params(60),
         name="conv_stats",
     )(activations, pre_activation, pooled_grad, weights)
-    stats = lax.all_to_all(msg, GROUP, 0, 0)
-    conv_grad, keep, send, line = pl.pallas_call(
+    chip = pl.pallas_call(
+        chip_kernel,
+        out_shape=shape((N_Z, STAT_ROWS, 128), f32),
+        in_specs=[VMEM],
+        out_specs=VMEM,
+        compiler_params=params(),
+        name="chip_stats",
+    )(lax.all_gather(msg, "core"))
+    stats = lax.all_to_all(chip, "z", 0, 0)
+    conv_grad, act, send, line = pl.pallas_call(
         grad_kernel,
         out_shape=(
             shape((ROWS, COUT), bf16),
-            shape((HALF, COUT), f32),
+            shape((ROWS, CIN), bf16),
             shape((HALF, COUT), bf16),
             shape((8, 128), f32),
         ),
         in_specs=[SMEM] + [VMEM] * 6,
         out_specs=(VMEM,) * 4,
-        scratch_shapes=[pltpu.VMEM((ROWS, CIN), bf16), pltpu.VMEM((ROWS, COUT), bf16), pltpu.VMEM((16, 128), f32)],
+        scratch_shapes=[pltpu.VMEM((ROWS, COUT), bf16), pltpu.VMEM((16, 128), f32)],
         compiler_params=params(),
         name="conv_grad",
     )(place, stats, weights, activations, pre_activation, pooled_grad, bn_params)
     swap = [(0, 1), (1, 0)]
     got = lax.ppermute(send, "core", swap)
+    keep = pl.pallas_call(
+        keep_kernel,
+        out_shape=shape((HALF, COUT), f32),
+        in_specs=[SMEM] + [VMEM] * 2,
+        out_specs=VMEM,
+        compiler_params=params(),
+        cost_estimate=pl.CostEstimate(flops=2 * ROWS * HALF * COUT, bytes_accessed=4 << 20, transcendentals=0),
+        name="keep_grad",
+    )(place, act, conv_grad)
     input_grad = pl.pallas_call(
         back_kernel,
         out_shape=shape((IMG, PIX, CIN), bf16),

time: 114 us -> 112 us (0.982)
  blocking collectives: 62.9 us -> 70.7 us
  waiting for transfers between devices: 15.3 us -> 9.39 us
  starting transfers between devices: 21.4 us -> 16.3 us
    all_gather x0 -> x1, blocking collectives: none -> 8.58 us  [body(): lax.all_gather(msg, 'core')]
    all_to_all x1, starting transfers between devices: 12 us -> 4.67 us  [body(): stats = lax.all_to_all(chip, 'z', 0, 0)]
    all_to_all x1, waiting for transfers between devices: 13 us -> 8.58 us  [body(): stats = lax.all_to_all(chip, 'z', 0, 0)]
    ppermute x1, starting transfers between devices: 1.92 us -> 3.95 us  [body(): got = lax.ppermute(send, 'core', swap)]
    pallas_call x1 -> x3, Pallas kernels: 4.43 us -> 6.13 us  [the longest x1 4.31 us: body(): pl.pallas_call(stats_kernel, out_shape=shape((STAT_ROWS, 128), f32), in_s...]
    ppermute x1, waiting for transfers between devices: 1.88 us -> 0.36 us  [body(): got = lax.ppermute(send, 'core', swap)]
  transfers between devices with their start and end apart: 3 -> 3, of which waited for: 3 -> 3; matrix products, arithmetic and copies ran while one was open for 0% -> 0% of each run, Pallas kernels for 2% -> 3%
where the time goes in v5:
time: 112 us; the launch traced here: 111 us
  blocking collectives  70.7 us (63%)
  starting transfers between devices  16.3 us (15%)
  Pallas kernels  13.8 us (12%)
  waiting for transfers between devices  9.39 us (8%)
    all_to_all x1, blocking collectives, body(): arrived = lax.all_to_all(lines.reshape(N_Y * N_Z, 8, 128), PLANE, 0, 0)  19.1 us
    all_to_all x1, blocking collectives, body(): lax.all_to_all(block, PLANE, 0, 0)  17.4 us
    all_to_all x1, blocking collectives, body(): mine = lax.all_to_all(wide, 'x', 0, 0)  13.2 us
    all_to_all x1, blocking collectives, body(): arrived = lax.all_to_all(halves.reshape(N_X, HALF // N_X, COUT), 'x', 0, 0)  12.4 us
    all_gather x1, blocking collectives, body(): lax.all_gather(msg, 'core')  8.58 us
    all_to_all x1, waiting for transfers between devices, body(): stats = lax.all_to_all(chip, 'z', 0, 0)  8.58 us
    ppermute x1, starting transfers between devices, body(): other = lax.ppermute(mine, 'core', swap)  7.66 us
    all_to_all x1, starting transfers between devices, body(): stats = lax.all_to_all(chip, 'z', 0, 0)  4.67 us
  transfers between devices with their start and end apart: 3, of which 3 were waited for; matrix products, arithmetic and copies ran while one was open for 0% of the time, Pallas kernels for 3%

profile of v5, /device:TPU:1, one launch (start us, length us, event | category | flops | bytes accessed | tf_op | source)
XLA Modules:
  0.0 111.1 jit_solution(6867608815613992953)
XLA Ops:
  0.6 0.0 copy-start.3
  0.6 0.0 copy-start.4
  0.7 0.0 copy-start
  0.7 0.0 copy-start.1
  0.7 0.0 copy-start.2
  0.7 4.3 %conv_stats.1 = f32[40,128]{1,0:T(8,128)} custom-call(bf16[12,49,512]{2,1,0:T(8,128)(2,1)} %act_ref.1, bf16[12,49,1024]{2,1,0:T(8,128)(2,1)} %pre_ref.1, f32[12,1024]{1,0:T(8,128)} %pool_ref.1, bf16[512,1024]{1,0:T(8,128)(2,1)} %w_ref.5), custom_call_target="tpu_custom_call" | custom-call | tf_op jit(solution)/shard_map/conv_stats/pallas_call | solution.py:286
  5.0 8.6 %all-gather = f32[80,128]{1,0:T(8,128)S(1)} all-gather(f32[40,128]{1,0:T(8,128)} %conv_stats.1), channel_id=2, replica_groups=mesh['x'=4,'y'=8,'z'=8,'core'=2] {'core'}, dimensions={0}, use_global_device_ids=true | all-gather | bytes 61440 | tf_op jit(solution)/shard_map/all_gather | solution.py:310
  13.6 0.7 chip_stats.1
  14.3 4.7 %all-to-all-start = ((f32[8,40,128]{2,1,0:T(8,128)}), f32[8,40,128]{2,1,0:T(8,128)S(1)}, u32[]{:S(2)}, u32[]{:S(2)}) async-start(f32[8,40,128]{2,1,0:T(8,128)} %chip_stats.1), calls=%async_computation | async-start | bytes 327680 | tf_op jit(solution)/shard_map/all_to_all | solution.py:311
  18.9 0.1 pad_add_fusion.place_ref
  19.0 8.6 %all-to-all-done.stat_ref = f32[8,40,128]{2,1,0:T(8,128)S(1)} async-done(((f32[8,40,128]{2,1,0:T(8,128)}), f32[8,40,128]{2,1,0:T(8,128)S(1)}, u32[]{:S(2)}, u32[]{:S(2)}) %all-to-all-start) | async-done | bytes 163872 | tf_op jit(solution)/shard_map/all_to_all | solution.py:311
  27.6 0.0 copy-done.3
  27.6 0.0 copy-done.4
  27.6 0.0 copy-done
  27.6 0.0 copy-done.1
  27.6 0.0 copy-done.2
  27.6 2.6 %conv_grad.1 = (bf16[768,1024]{1,0:T(8,128)(2,1)S(1)}, bf16[768,512]{1,0:T(8,128)(2,1)S(1)}, bf16[256,1024]{1,0:T(8,128)(2,1)S(1)}, f32[8,128]{1,0:T(8,128)S(1)}) custom-call(s32[4]{0:T(128)S(1)} %pad_add_fusion.place_ref, f32[8,40,128]{2,1,0:T(8,128)S(1)} %all-to-all-done.stat_ref, bf16[512,1024]{1,0:T(8,128)(2,1)S(1)} %copy-done, ...), custom_call_target="tpu_custom_call" | custom-call | tf_op jit(solution)/shard_map/conv_grad/pallas_call | solution.py:312
  30.2 4.0 %collective-permute-start = (bf16[256,1024]{1,0:T(8,128)(2,1)S(1)}, bf16[256,1024]{1,0:T(8,128)(2,1)S(1)}, u32[]{:S(2)}, u32[]{:S(2)}) collective-permute-start(bf16[256,1024]{1,0:T(8,128)(2,1)S(1)} %get-tuple-element.17), channel_id=1, source_target_pairs={{0,1},{1,0},{2,3},{3,2},{4,5},{5,4},{6,7},{7,6},{8,9},{9,8},{10,11... | collective-permute-start | bytes 1572872 | tf_op jit(solution)/shard_map/ppermute | solution.py:327
  34.1 1.1 %keep_grad.1.keep_ref = f32[256,1024]{1,0:T(8,128)S(1)} custom-call(s32[4]{0:T(128)S(1)} %pad_add_fusion.place_ref, bf16[768,512]{1,0:T(8,128)(2,1)S(1)} %get-tuple-element.16.actp, bf16[768,1024]{1,0:T(8,128)(2,1)S(1)} %get-tuple-element.15.cg_ref), custom_call_target="tpu_custom_call" | custom-call | flops 402653184 | bytes 4194304 | tf_op jit(solution)/shard_map/keep_grad/pallas_call | solution.py:328
  35.3 0.4 collective-permute-done.got_ref
  35.6 0.1 pair_sum.1
  35.7 0.0 copy-start.5
  35.8 0.0 copy-start.6
  35.8 12.4 %all_to_all.25.got_ref = bf16[4,64,1024]{2,1,0:T(8,128)(2,1)S(1)} all-to-all(bf16[4,64,1024]{2,1,0:T(8,128)(2,1)S(1)} %bitcast.7), channel_id=1, replica_groups=mesh['x'=4,'y'=8,'z'=8,'core'=2] {'x'}, dimensions={0} | all-to-all | bytes 1048576 | tf_op jit(solution)/shard_map/all_to_all | solution.py:354
  48.2 0.1 line_sum.1
  48.3 19.1 %all_to_all.26.got_ref = bf16[64,8,128]{2,1,0:T(8,128)(2,1)S(1)} all-to-all(bf16[64,8,128]{2,1,0:T(8,128)(2,1)S(1)} %bitcast.8), channel_id=1, replica_groups=mesh['x'=4,'y'=8,'z'=8,'core'=2] {'y','z'}, dimensions={0} | all-to-all | bytes 262144 | tf_op jit(solution)/shard_map/all_to_all | solution.py:363
  67.4 0.0 copy-done.5
  67.4 0.0 copy-done.6
  67.4 0.2 block_sum.1
  67.6 17.4 %all_to_all.27.got_ref = bf16[64,24,128]{2,1,0:T(8,128)(2,1)S(1)} all-to-all(bf16[64,24,128]{2,1,0:T(8,128)(2,1)S(1)} %block_sum.1), channel_id=1, replica_groups=mesh['x'=4,'y'=8,'z'=8,'core'=2] {'y','z'}, dimensions={0} | all-to-all | bytes 786432 | tf_op jit(solution)/shard_map/all_to_all | solution.py:379
  85.0 0.2 plane_join.1
  85.2 13.2 %all_to_all.28.mine_ref = bf16[4,1056,128]{2,1,0:T(8,128)(2,1)S(1)} all-to-all(bf16[4,1056,128]{2,1,0:T(8,128)(2,1)S(1)} %plane_join.1), channel_id=1, replica_groups=mesh['x'=4,'y'=8,'z'=8,'core'=2] {'x'}, dimensions={0} | all-to-all | bytes 2162688 | tf_op jit(solution)/shard_map/all_to_all | solution.py:380
  98.4 0.0 copy-start.7
  98.4 7.7 %collective-permute-start.1 = (bf16[4,1056,128]{2,1,0:T(8,128)(2,1)S(1)}, bf16[4,1056,128]{2,1,0:T(8,128)(2,1)S(1)}, u32[]{:S(2)}, u32[]{:S(2)}) collective-permute-start(bf16[4,1056,128]{2,1,0:T(8,128)(2,1)S(1)} %all_to_all.28.mine_ref), channel_id=1, source_target_pairs={{0,1},{1,0},{2,3},{3,2},{4,5},{5,4},{6,7},{7,6},{8,9},{9,8},{10,11... | collective-permute-start | bytes 3244040 | tf_op jit(solution)/shard_map/ppermute | solution.py:381
  106.0 1.9 %input_grad.1 = bf16[12,49,512]{2,1,0:T(8,128)(2,1)} custom-call(bf16[768,1024]{1,0:T(8,128)(2,1)S(1)} %get-tuple-element.15.cg_ref, bf16[512,1024]{1,0:T(8,128)(2,1)S(1)} %copy-done), custom_call_target="tpu_custom_call" | custom-call | flops 805306368 | bytes 4194304 | tf_op jit(solution)/shard_map/input_grad/pallas_call | solution.py:337
  107.9 0.4 collective-permute-done.1.other_ref
  108.3 0.0 copy-done.7
  108.3 2.7 %update.1 = (f32[16,64]{1,0:T(8,128)}, f32[16,64]{1,0:T(8,128)}, bf16[512,1024]{1,0:T(8,128)(2,1)}, f32[2,1024]{1,0:T(2,128)}, f32[2,1024]{1,0:T(2,128)}) custom-call(s32[4]{0:T(128)S(1)} %pad_add_fusion.place_ref, bf16[4,1056,128]{2,1,0:T(8,128)(2,1)S(1)} %all_to_all.28.mine_ref, bf16[4,1056,128]{2,1,0:T(8,128)(2,1)S(1)} %collective-permute-done.1.other_ref, ...), custom_call_target="tpu_custom_call" | custom-call | tf_op jit(solution)/shard_map/update/pallas_call | solution.py:382
Async XLA Ops:
  0.6 27.0 %copy-start.3 = (f32[12,1024]{1,0:T(8,128)S(1)}, f32[12,1024]{1,0:T(8,128)}, u32[]{:S(2)}) copy-start(f32[12,1024]{1,0:T(8,128)} %pool_ref.1) | copy-start | bytes 147460
  0.6 26.9 %copy-start.4 = (f32[2,1024]{1,0:T(2,128)S(1)}, f32[2,1024]{1,0:T(2,128)}, u32[]{:S(2)}) copy-start(f32[2,1024]{1,0:T(2,128)} %bn_ref.3) | copy-start | bytes 24580
  0.7 26.9 %copy-start = (bf16[512,1024]{1,0:T(8,128)(2,1)S(1)}, bf16[512,1024]{1,0:T(8,128)(2,1)}, u32[]{:S(2)}) copy-start(bf16[512,1024]{1,0:T(8,128)(2,1)} %w_ref.5) | copy-start | bytes 3145732
  0.7 26.9 %copy-start.1 = (bf16[12,49,1024]{2,1,0:T(8,128)(2,1)S(1)}, bf16[12,49,1024]{2,1,0:T(8,128)(2,1)}, u32[]{:S(2)}) copy-start(bf16[12,49,1024]{2,1,0:T(8,128)(2,1)} %pre_ref.1) | copy-start | bytes 3612676
  0.7 26.9 %copy-start.2 = (bf16[12,49,512]{2,1,0:T(8,128)(2,1)S(1)}, bf16[12,49,512]{2,1,0:T(8,128)(2,1)}, u32[]{:S(2)}) copy-start(bf16[12,49,512]{2,1,0:T(8,128)(2,1)} %act_ref.1) | copy-start | bytes 1806340
  14.3 13.3 %all-to-all-start = ((f32[8,40,128]{2,1,0:T(8,128)}), f32[8,40,128]{2,1,0:T(8,128)S(1)}, u32[]{:S(2)}, u32[]{:S(2)}) async-start(f32[8,40,128]{2,1,0:T(8,128)} %chip_stats.1), calls=%async_computation | async-start | bytes 327680 | tf_op jit(solution)/shard_map/all_to_all | solution.py:311
  30.2 5.5 %collective-permute-start = (bf16[256,1024]{1,0:T(8,128)(2,1)S(1)}, bf16[256,1024]{1,0:T(8,128)(2,1)S(1)}, u32[]{:S(2)}, u32[]{:S(2)}) collective-permute-start(bf16[256,1024]{1,0:T(8,128)(2,1)S(1)} %get-tuple-element.17), channel_id=1, source_target_pairs={{0,1},{1,0},{2,3},{3,2},{4,5},{5,4},{6,7},{7,6},{8,9},{9,8},{10,11... | collective-permute-start | bytes 1572872 | tf_op jit(solution)/shard_map/ppermute | solution.py:327
  35.7 31.7 %copy-start.5 = (f32[16,64]{1,0:T(8,128)S(1)}, f32[16,64]{1,0:T(8,128)}, u32[]{:S(2)}) copy-start(f32[16,64]{1,0:T(8,128)} %master_ref.3) | copy-start | bytes 12292
  35.8 31.7 %copy-start.6 = (f32[16,64]{1,0:T(8,128)S(1)}, f32[16,64]{1,0:T(8,128)}, u32[]{:S(2)}) copy-start(f32[16,64]{1,0:T(8,128)} %vel_ref.3) | copy-start | bytes 12292
  98.4 10.0 %copy-start.7 = (f32[2,1024]{1,0:T(2,128)S(1)}, f32[2,1024]{1,0:T(2,128)}, u32[]{:S(2)}) copy-start(f32[2,1024]{1,0:T(2,128)} %bnv_ref.1) | copy-start | bytes 24580
  98.4 10.0 %collective-permute-start.1 = (bf16[4,1056,128]{2,1,0:T(8,128)(2,1)S(1)}, bf16[4,1056,128]{2,1,0:T(8,128)(2,1)S(1)}, u32[]{:S(2)}, u32[]{:S(2)}) collective-permute-start(bf16[4,1056,128]{2,1,0:T(8,128)(2,1)S(1)} %all_to_all.28.mine_ref), channel_id=1, source_target_pairs={{0,1},{1,0},{2,3},{3,2},{4,5},{5,4},{6,7},{7,6},{8,9},{9,8},{10,11... | collective-permute-start | bytes 3244040 | tf_op jit(solution)/shard_map/ppermute | solution.py:381

commit v6 on v5

--- a/solution.py
+++ b/solution.py
@@ -108,9 +108,9 @@
 
 
 def grad_kernel(
-    place_ref, stat_ref, w_ref, act_ref, pre_ref, pool_ref, bn_ref, cg_ref, actp, send_ref, line_ref, conv_ref, lines
+    stat_ref, w_ref, act_ref, pre_ref, pool_ref, bn_ref, cg_ref, actp, send_ref, line_ref, conv_ref, lines
 ):
-    core, layer = place_ref[0], place_ref[3]
+    core, layer = core_of(), lax.axis_index("z").astype(jnp.int32)
     sums = jnp.sum(stat_ref[...], axis=0)
     sum_up = sums[16:24]
     act_mean = (unfold(sums[32:36]) / M).astype(bf16).astype(f32)
@@ -147,13 +147,17 @@
     send_ref[...] = half_grad(actp, cg_ref, 1 - core).astype(bf16)
 
 
+def core_of():
+    return lax.axis_index("core").astype(jnp.int32)
+
+
 def half_grad(actp, cg_ref, half):
     columns = actp[:, pl.ds(pl.multiple_of(half * HALF, HALF), HALF)]
     return lax.dot_general(columns, cg_ref[...], (((0,), (0,)), ((), ())), preferred_element_type=f32)
 
 
-def keep_kernel(place_ref, actp, cg_ref, keep_ref):
-    keep_ref[...] = half_grad(actp, cg_ref, place_ref[0])
+def keep_kernel(actp, cg_ref, keep_ref):
+    keep_ref[...] = half_grad(actp, cg_ref, core_of())
 
 
 def back_kernel(cg_ref, w_ref, out_ref):
@@ -205,10 +209,11 @@
 
 
 def update_kernel(
-    place_ref, mine_ref, other_ref, w_ref, master_ref, vel_ref, bn_ref, bnv_ref,
+    mine_ref, other_ref, w_ref, master_ref, vel_ref, bn_ref, bnv_ref,
     new_master_ref, new_vel_ref, new_w_hbm, new_bn_ref, new_bnv_ref, new_w, sems,
 ):
-    core, row, layer = place_ref[0], place_ref[1], place_ref[3]
+    core, layer = core_of(), lax.axis_index("z").astype(jnp.int32)
+    row = (lax.axis_index("x") * N_Y + lax.axis_index("y")).astype(jnp.int32)
 
     def run(parts):
         square = jnp.zeros((1, 128), f32)
@@ -273,16 +278,11 @@
     return jax.ShapeDtypeStruct(dims, kind)
 
 
-SMEM = pl.BlockSpec(memory_space=pltpu.SMEM)
 VMEM = pl.BlockSpec(memory_space=pltpu.VMEM)
 HBM = pl.BlockSpec(memory_space=pltpu.HBM)
 
 
 def body(activations, pre_activation, pooled_grad, weights, master, velocity, bn_params, bn_velocity):
-    core = lax.axis_index("core").astype(jnp.int32)
-    layer = lax.axis_index("z").astype(jnp.int32)
-    row = (lax.axis_index("x") * 8 + lax.axis_index("y")).astype(jnp.int32)
-    place = jnp.stack([core, row, layer * 2 + core, layer])
     msg = pl.pallas_call(
         stats_kernel,
         out_shape=shape((STAT_ROWS, 128), f32),
@@ -317,23 +317,23 @@
             shape((HALF, COUT), bf16),
             shape((8, 128), f32),
         ),
-        in_specs=[SMEM] + [VMEM] * 6,
+        in_specs=[VMEM] * 6,
         out_specs=(VMEM,) * 4,
         scratch_shapes=[pltpu.VMEM((ROWS, COUT), bf16), pltpu.VMEM((16, 128), f32)],
         compiler_params=params(),
         name="conv_grad",
-    )(place, stats, weights, activations, pre_activation, pooled_grad, bn_params)
+    )(stats, weights, activations, pre_activation, pooled_grad, bn_params)
     swap = [(0, 1), (1, 0)]
     got = lax.ppermute(send, "core", swap)
     keep = pl.pallas_call(
         keep_kernel,
         out_shape=shape((HALF, COUT), f32),
-        in_specs=[SMEM] + [VMEM] * 2,
+        in_specs=[VMEM] * 2,
         out_specs=VMEM,
         compiler_params=params(),
         cost_estimate=pl.CostEstimate(flops=2 * ROWS * HALF * COUT, bytes_accessed=4 << 20, transcendentals=0),
         name="keep_grad",
-    )(place, act, conv_grad)
+    )(act, conv_grad)
     input_grad = pl.pallas_call(
         back_kernel,
         out_shape=shape((IMG, PIX, CIN), bf16),
@@ -388,12 +388,12 @@
             shape((2, COUT), f32),
             shape((2, COUT), f32),
         ),
-        in_specs=[SMEM] + [VMEM] * 7,
+        in_specs=[VMEM] * 7,
         out_specs=(VMEM, VMEM, HBM, VMEM, VMEM),
         scratch_shapes=[pltpu.VMEM((CIN, COUT), bf16), pltpu.SemaphoreType.DMA((N_X,))],
         compiler_params=params(),
         name="update",
-    )(place, mine, other, weights, master, velocity, bn_params, bn_velocity)
+    )(mine, other, weights, master, velocity, bn_params, bn_velocity)
     return input_grad, new_master, new_velocity, new_weights, new_bn, new_bn_velocity
 
 

time: 112 us -> 109 us (0.973)
  blocking collectives: 70.7 us -> 83.8 us
  waiting for transfers between devices: 9.39 us -> 1.34 us
  starting transfers between devices: 16.3 us -> 11.6 us
  Pallas kernels: 13.8 us -> 11.4 us
    all_to_all x0 -> x1, blocking collectives: none -> 13.1 us  [body(): stats = lax.all_to_all(chip, 'z', 0, 0)]
    all_to_all x1 -> x0, waiting for transfers between devices: 8.58 us -> none  [body(): stats = lax.all_to_all(chip, 'z', 0, 0)]
    all_to_all x1 -> x0, starting transfers between devices: 4.67 us -> none  [body(): stats = lax.all_to_all(chip, 'z', 0, 0)]
  transfers between devices with their start and end apart: 3 -> 2, of which waited for: 3 -> 2; matrix products, arithmetic and copies ran while one was open for 0% -> 0% of each run, Pallas kernels for 3% -> 2%
where the time goes in v6:
time: 109 us
  blocking collectives  83.8 us (77%)
  starting transfers between devices  11.6 us (11%)
  Pallas kernels  11.4 us (10%)
  waiting for transfers between devices  1.34 us (1%)
    all_to_all x1, blocking collectives, body(): arrived = lax.all_to_all(lines.reshape(N_Y * N_Z, 8, 128), PLANE, 0, 0)  19.1 us
    all_to_all x1, blocking collectives, body(): lax.all_to_all(block, PLANE, 0, 0)  17.4 us
    all_to_all x1, blocking collectives, body(): mine = lax.all_to_all(wide, 'x', 0, 0)  13.2 us
    all_to_all x1, blocking collectives, body(): stats = lax.all_to_all(chip, 'z', 0, 0)  13.1 us
    all_to_all x1, blocking collectives, body(): arrived = lax.all_to_all(halves.reshape(N_X, HALF // N_X, COUT), 'x', 0, 0)  12.4 us
    all_gather x1, blocking collectives, body(): lax.all_gather(msg, 'core')  8.58 us
    ppermute x1, starting transfers between devices, body(): other = lax.ppermute(mine, 'core', swap)  7.66 us
    pallas_call x1, Pallas kernels, body(): pl.pallas_call(stats_kernel, out_shape=shape((STAT_ROWS, 128), f32), in_s...  4.31 us
  transfers between devices with their start and end apart: 2, of which 2 were waited for; matrix products, arithmetic and copies ran while one was open for 0% of the time, Pallas kernels for 2%

profile of v6, /device:TPU:1, one launch (start us, length us, event | category | flops | bytes accessed | tf_op | source)
XLA Modules:
  0.0 109.1 jit_solution(7222362855941507551)
XLA Ops:
  0.6 0.0 copy-start.3
  0.6 0.0 copy-start.2
  0.7 0.0 copy-start.4
  0.7 0.0 copy-start
  0.7 0.0 copy-start.1
  0.7 4.3 %conv_stats.1 = f32[40,128]{1,0:T(8,128)} custom-call(bf16[12,49,512]{2,1,0:T(8,128)(2,1)} %act_ref.1, bf16[12,49,1024]{2,1,0:T(8,128)(2,1)} %pre_ref.1, f32[12,1024]{1,0:T(8,128)} %pool_ref.1, bf16[512,1024]{1,0:T(8,128)(2,1)} %w_ref.5), custom_call_target="tpu_custom_call" | custom-call | tf_op jit(solution)/shard_map/conv_stats/pallas_call | solution.py:286
  5.0 8.6 %all-gather = f32[80,128]{1,0:T(8,128)S(1)} all-gather(f32[40,128]{1,0:T(8,128)} %conv_stats.1), channel_id=2, replica_groups=mesh['x'=4,'y'=8,'z'=8,'core'=2] {'core'}, dimensions={0}, use_global_device_ids=true | all-gather | bytes 61440 | tf_op jit(solution)/shard_map/all_gather | solution.py:310
  13.6 13.1 %all_to_all.25.stat_ref = f32[8,40,128]{2,1,0:T(8,128)S(1)} all-to-all(f32[8,40,128]{2,1,0:T(8,128)S(1)} %chip_stats.1), channel_id=1, replica_groups=mesh['x'=4,'y'=8,'z'=8,'core'=2] {'z'}, dimensions={0} | all-to-all | bytes 327680 | tf_op jit(solution)/shard_map/all_to_all | solution.py:311
  26.7 0.0 copy-done.3
  26.7 0.0 copy-done.2
  26.7 0.0 copy-done.4
  26.7 0.0 copy-done
  26.7 0.0 copy-done.1
  26.7 1.9 %conv_grad.1 = (bf16[768,1024]{1,0:T(8,128)(2,1)S(1)}, bf16[768,512]{1,0:T(8,128)(2,1)S(1)}, bf16[256,1024]{1,0:T(8,128)(2,1)S(1)}, f32[8,128]{1,0:T(8,128)S(1)}) custom-call(f32[8,40,128]{2,1,0:T(8,128)S(1)} %all_to_all.25.stat_ref, bf16[512,1024]{1,0:T(8,128)(2,1)S(1)} %copy-done, bf16[12,49,512]{2,1,0:T(8,128)(2,1)S(1)} %copy-done.2, ...), custom_call_target="tpu_custom_call" | custom-call | tf_op jit(solution)/shard_map/conv_grad/pallas_call | solution.py:312
  28.7 4.0 %collective-permute-start = (bf16[256,1024]{1,0:T(8,128)(2,1)S(1)}, bf16[256,1024]{1,0:T(8,128)(2,1)S(1)}, u32[]{:S(2)}, u32[]{:S(2)}) collective-permute-start(bf16[256,1024]{1,0:T(8,128)(2,1)S(1)} %get-tuple-element.17), channel_id=1, source_target_pairs={{0,1},{1,0},{2,3},{3,2},{4,5},{5,4},{6,7},{7,6},{8,9},{9,8},{10,11... | collective-permute-start | bytes 1572872 | tf_op jit(solution)/shard_map/ppermute | solution.py:327
  32.7 0.6 keep_grad.1.keep_ref
  33.3 0.9 collective-permute-done.got_ref
  34.2 0.1 pair_sum.1
  34.3 0.0 copy-start.5
  34.3 0.0 copy-start.6
  34.3 12.4 %all_to_all.26.got_ref = bf16[4,64,1024]{2,1,0:T(8,128)(2,1)S(1)} all-to-all(bf16[4,64,1024]{2,1,0:T(8,128)(2,1)S(1)} %bitcast.3), channel_id=1, replica_groups=mesh['x'=4,'y'=8,'z'=8,'core'=2] {'x'}, dimensions={0} | all-to-all | bytes 1048576 | tf_op jit(solution)/shard_map/all_to_all | solution.py:354
  46.8 0.1 line_sum.1
  46.8 19.1 %all_to_all.27.got_ref = bf16[64,8,128]{2,1,0:T(8,128)(2,1)S(1)} all-to-all(bf16[64,8,128]{2,1,0:T(8,128)(2,1)S(1)} %bitcast.4), channel_id=1, replica_groups=mesh['x'=4,'y'=8,'z'=8,'core'=2] {'y','z'}, dimensions={0} | all-to-all | bytes 262144 | tf_op jit(solution)/shard_map/all_to_all | solution.py:363
  66.0 0.0 copy-done.5
  66.0 0.0 copy-done.6
  66.0 0.2 block_sum.1
  66.1 17.4 %all_to_all.28.got_ref = bf16[64,24,128]{2,1,0:T(8,128)(2,1)S(1)} all-to-all(bf16[64,24,128]{2,1,0:T(8,128)(2,1)S(1)} %block_sum.1), channel_id=1, replica_groups=mesh['x'=4,'y'=8,'z'=8,'core'=2] {'y','z'}, dimensions={0} | all-to-all | bytes 786432 | tf_op jit(solution)/shard_map/all_to_all | solution.py:379
  83.6 0.2 plane_join.1
  83.7 13.2 %all_to_all.29.mine_ref = bf16[4,1056,128]{2,1,0:T(8,128)(2,1)S(1)} all-to-all(bf16[4,1056,128]{2,1,0:T(8,128)(2,1)S(1)} %plane_join.1), channel_id=1, replica_groups=mesh['x'=4,'y'=8,'z'=8,'core'=2] {'x'}, dimensions={0} | all-to-all | bytes 2162688 | tf_op jit(solution)/shard_map/all_to_all | solution.py:380
  96.9 0.0 copy-start.7
  96.9 7.7 %collective-permute-start.1 = (bf16[4,1056,128]{2,1,0:T(8,128)(2,1)S(1)}, bf16[4,1056,128]{2,1,0:T(8,128)(2,1)S(1)}, u32[]{:S(2)}, u32[]{:S(2)}) collective-permute-start(bf16[4,1056,128]{2,1,0:T(8,128)(2,1)S(1)} %all_to_all.29.mine_ref), channel_id=1, source_target_pairs={{0,1},{1,0},{2,3},{3,2},{4,5},{5,4},{6,7},{7,6},{8,9},{9,8},{10,11... | collective-permute-start | bytes 3244040 | tf_op jit(solution)/shard_map/ppermute | solution.py:381
  104.6 1.9 %input_grad.1 = bf16[12,49,512]{2,1,0:T(8,128)(2,1)} custom-call(bf16[768,1024]{1,0:T(8,128)(2,1)S(1)} %get-tuple-element.15.cg_ref, bf16[512,1024]{1,0:T(8,128)(2,1)S(1)} %copy-done), custom_call_target="tpu_custom_call" | custom-call | flops 805306368 | bytes 4194304 | tf_op jit(solution)/shard_map/input_grad/pallas_call | solution.py:337
  106.4 0.4 collective-permute-done.1.other_ref
  106.9 0.0 copy-done.7
  106.9 2.2 %update.1 = (f32[16,64]{1,0:T(8,128)}, f32[16,64]{1,0:T(8,128)}, bf16[512,1024]{1,0:T(8,128)(2,1)}, f32[2,1024]{1,0:T(2,128)}, f32[2,1024]{1,0:T(2,128)}) custom-call(bf16[4,1056,128]{2,1,0:T(8,128)(2,1)S(1)} %all_to_all.29.mine_ref, bf16[4,1056,128]{2,1,0:T(8,128)(2,1)S(1)} %collective-permute-done.1.other_ref, bf16[512,1024]{1,0:T(8,128)(2,1)S(1)} %copy-done, ...), custom_call_target="tpu_custom_call" | custom-call | tf_op jit(solution)/shard_map/update/pallas_call | solution.py:382
  (1 shorter events, 0.0 us)
Async XLA Ops:
  0.6 26.1 %copy-start.3 = (f32[12,1024]{1,0:T(8,128)S(1)}, f32[12,1024]{1,0:T(8,128)}, u32[]{:S(2)}) copy-start(f32[12,1024]{1,0:T(8,128)} %pool_ref.1) | copy-start | bytes 147460
  0.6 26.1 %copy-start.2 = (bf16[12,49,512]{2,1,0:T(8,128)(2,1)S(1)}, bf16[12,49,512]{2,1,0:T(8,128)(2,1)}, u32[]{:S(2)}) copy-start(bf16[12,49,512]{2,1,0:T(8,128)(2,1)} %act_ref.1) | copy-start | bytes 1806340
  0.7 26.1 %copy-start.4 = (f32[2,1024]{1,0:T(2,128)S(1)}, f32[2,1024]{1,0:T(2,128)}, u32[]{:S(2)}) copy-start(f32[2,1024]{1,0:T(2,128)} %bn_ref.3) | copy-start | bytes 24580
  0.7 26.1 %copy-start = (bf16[512,1024]{1,0:T(8,128)(2,1)S(1)}, bf16[512,1024]{1,0:T(8,128)(2,1)}, u32[]{:S(2)}) copy-start(bf16[512,1024]{1,0:T(8,128)(2,1)} %w_ref.5) | copy-start | bytes 3145732
  0.7 26.1 %copy-start.1 = (bf16[12,49,1024]{2,1,0:T(8,128)(2,1)S(1)}, bf16[12,49,1024]{2,1,0:T(8,128)(2,1)}, u32[]{:S(2)}) copy-start(bf16[12,49,1024]{2,1,0:T(8,128)(2,1)} %pre_ref.1) | copy-start | bytes 3612676
  28.7 5.5 %collective-permute-start = (bf16[256,1024]{1,0:T(8,128)(2,1)S(1)}, bf16[256,1024]{1,0:T(8,128)(2,1)S(1)}, u32[]{:S(2)}, u32[]{:S(2)}) collective-permute-start(bf16[256,1024]{1,0:T(8,128)(2,1)S(1)} %get-tuple-element.17), channel_id=1, source_target_pairs={{0,1},{1,0},{2,3},{3,2},{4,5},{5,4},{6,7},{7,6},{8,9},{9,8},{10,11... | collective-permute-start | bytes 1572872 | tf_op jit(solution)/shard_map/ppermute | solution.py:327
  34.3 31.7 %copy-start.5 = (f32[16,64]{1,0:T(8,128)S(1)}, f32[16,64]{1,0:T(8,128)}, u32[]{:S(2)}) copy-start(f32[16,64]{1,0:T(8,128)} %master_ref.3) | copy-start | bytes 12292
  34.3 31.7 %copy-start.6 = (f32[16,64]{1,0:T(8,128)S(1)}, f32[16,64]{1,0:T(8,128)}, u32[]{:S(2)}) copy-start(f32[16,64]{1,0:T(8,128)} %vel_ref.3) | copy-start | bytes 12292
  96.9 10.0 %copy-start.7 = (f32[2,1024]{1,0:T(2,128)S(1)}, f32[2,1024]{1,0:T(2,128)}, u32[]{:S(2)}) copy-start(f32[2,1024]{1,0:T(2,128)} %bnv_ref.1) | copy-start | bytes 24580
  96.9 10.0 %collective-permute-start.1 = (bf16[4,1056,128]{2,1,0:T(8,128)(2,1)S(1)}, bf16[4,1056,128]{2,1,0:T(8,128)(2,1)S(1)}, u32[]{:S(2)}, u32[]{:S(2)}) collective-permute-start(bf16[4,1056,128]{2,1,0:T(8,128)(2,1)S(1)} %all_to_all.29.mine_ref), channel_id=1, source_target_pairs={{0,1},{1,0},{2,3},{3,2},{4,5},{5,4},{6,7},{7,6},{8,9},{9,8},{10,11... | collective-permute-start | bytes 3244040 | tf_op jit(solution)/shard_map/ppermute | solution.py:381

commit v7 on v6

--- a/solution.py
+++ b/solution.py
@@ -190,7 +190,8 @@
 
 
 def plane_kernel(got_ref, out_ref):
-    extra = jnp.sum(got_ref[:, 16:24, :].astype(f32).reshape(N_Y, N_Z, 8, 128), axis=0)
+    got = got_ref[...].astype(f32)
+    extra = jnp.sum(got[:, 16:24, :].reshape(N_Y, N_Z, 8, 128), axis=0)
     lines = []
     norm = jnp.zeros((1, 128), f32)
     square = jnp.zeros((1, 128), f32)
@@ -200,8 +201,8 @@
         square += extra[z, 6:7] + extra[z, 7:8]
     lines += split(norm) + split(square)
     extra = jnp.concatenate(lines + [jnp.zeros((2, 128), f32)], axis=0).astype(bf16)
-    grad = got_ref[:, 0:8, :].astype(f32).reshape(512, 128).astype(bf16)
-    decayed = got_ref[:, 8:16, :].astype(f32).reshape(512, 128).astype(bf16)
+    grad = got[:, 0:8, :].reshape(512, 128).astype(bf16)
+    decayed = got[:, 8:16, :].reshape(512, 128).astype(bf16)
     for p in range(N_X):
         out_ref[p, 0:512, :] = grad
         out_ref[p, 512:1024, :] = decayed

time: 109 us -> 109 us (level)
  no operation moved by 1% of the time
where the time goes in v7:
time: 109 us
  blocking collectives  83.8 us (77%)
  starting transfers between devices  11.6 us (11%)
  Pallas kernels  11.4 us (10%)
  waiting for transfers between devices  1.34 us (1%)
    all_to_all x1, blocking collectives, body(): arrived = lax.all_to_all(lines.reshape(N_Y * N_Z, 8, 128), PLANE, 0, 0)  19.1 us
    all_to_all x1, blocking collectives, body(): lax.all_to_all(block, PLANE, 0, 0)  17.4 us
    all_to_all x1, blocking collectives, body(): mine = lax.all_to_all(wide, 'x', 0, 0)  13.2 us
    all_to_all x1, blocking collectives, body(): stats = lax.all_to_all(chip, 'z', 0, 0)  13.1 us
    all_to_all x1, blocking collectives, body(): arrived = lax.all_to_all(halves.reshape(N_X, HALF // N_X, COUT), 'x', 0, 0)  12.4 us
    all_gather x1, blocking collectives, body(): lax.all_gather(msg, 'core')  8.58 us
    ppermute x1, starting transfers between devices, body(): other = lax.ppermute(mine, 'core', swap)  7.66 us
    pallas_call x1, Pallas kernels, body(): pl.pallas_call(stats_kernel, out_shape=shape((STAT_ROWS, 128), f32), in_s...  4.31 us
  transfers between devices with their start and end apart: 2, of which 2 were waited for; matrix products, arithmetic and copies ran while one was open for 0% of the time, Pallas kernels for 2%

profile of v7, /device:TPU:1, one launch (start us, length us, event | category | flops | bytes accessed | tf_op | source)
XLA Modules:
  0.0 109.1 jit_solution(7222362855941507551)
XLA Ops:
  0.6 0.0 copy-start.3
  0.6 0.0 copy-start.2
  0.7 0.0 copy-start.4
  0.7 0.0 copy-start
  0.7 0.0 copy-start.1
  0.7 4.3 %conv_stats.1 = f32[40,128]{1,0:T(8,128)} custom-call(bf16[12,49,512]{2,1,0:T(8,128)(2,1)} %act_ref.1, bf16[12,49,1024]{2,1,0:T(8,128)(2,1)} %pre_ref.1, f32[12,1024]{1,0:T(8,128)} %pool_ref.1, bf16[512,1024]{1,0:T(8,128)(2,1)} %w_ref.5), custom_call_target="tpu_custom_call" | custom-call | tf_op jit(solution)/shard_map/conv_stats/pallas_call | solution.py:287
  5.0 8.6 %all-gather = f32[80,128]{1,0:T(8,128)S(1)} all-gather(f32[40,128]{1,0:T(8,128)} %conv_stats.1), channel_id=2, replica_groups=mesh['x'=4,'y'=8,'z'=8,'core'=2] {'core'}, dimensions={0}, use_global_device_ids=true | all-gather | bytes 61440 | tf_op jit(solution)/shard_map/all_gather | solution.py:311
  13.6 13.1 %all_to_all.25.stat_ref = f32[8,40,128]{2,1,0:T(8,128)S(1)} all-to-all(f32[8,40,128]{2,1,0:T(8,128)S(1)} %chip_stats.1), channel_id=1, replica_groups=mesh['x'=4,'y'=8,'z'=8,'core'=2] {'z'}, dimensions={0} | all-to-all | bytes 327680 | tf_op jit(solution)/shard_map/all_to_all | solution.py:312
  26.7 0.0 copy-done.3
  26.7 0.0 copy-done.2
  26.7 0.0 copy-done.4
  26.7 0.0 copy-done
  26.7 0.0 copy-done.1
  26.7 1.9 %conv_grad.1 = (bf16[768,1024]{1,0:T(8,128)(2,1)S(1)}, bf16[768,512]{1,0:T(8,128)(2,1)S(1)}, bf16[256,1024]{1,0:T(8,128)(2,1)S(1)}, f32[8,128]{1,0:T(8,128)S(1)}) custom-call(f32[8,40,128]{2,1,0:T(8,128)S(1)} %all_to_all.25.stat_ref, bf16[512,1024]{1,0:T(8,128)(2,1)S(1)} %copy-done, bf16[12,49,512]{2,1,0:T(8,128)(2,1)S(1)} %copy-done.2, ...), custom_call_target="tpu_custom_call" | custom-call | tf_op jit(solution)/shard_map/conv_grad/pallas_call | solution.py:313
  28.7 4.0 %collective-permute-start = (bf16[256,1024]{1,0:T(8,128)(2,1)S(1)}, bf16[256,1024]{1,0:T(8,128)(2,1)S(1)}, u32[]{:S(2)}, u32[]{:S(2)}) collective-permute-start(bf16[256,1024]{1,0:T(8,128)(2,1)S(1)} %get-tuple-element.17), channel_id=1, source_target_pairs={{0,1},{1,0},{2,3},{3,2},{4,5},{5,4},{6,7},{7,6},{8,9},{9,8},{10,11... | collective-permute-start | bytes 1572872 | tf_op jit(solution)/shard_map/ppermute | solution.py:328
  32.7 0.6 keep_grad.1.keep_ref
  33.3 0.9 collective-permute-done.got_ref
  34.2 0.1 pair_sum.1
  34.3 0.0 copy-start.5
  34.3 0.0 copy-start.6
  34.3 12.4 %all_to_all.26.got_ref = bf16[4,64,1024]{2,1,0:T(8,128)(2,1)S(1)} all-to-all(bf16[4,64,1024]{2,1,0:T(8,128)(2,1)S(1)} %bitcast.3), channel_id=1, replica_groups=mesh['x'=4,'y'=8,'z'=8,'core'=2] {'x'}, dimensions={0} | all-to-all | bytes 1048576 | tf_op jit(solution)/shard_map/all_to_all | solution.py:355
  46.8 0.1 line_sum.1
  46.8 19.1 %all_to_all.27.got_ref = bf16[64,8,128]{2,1,0:T(8,128)(2,1)S(1)} all-to-all(bf16[64,8,128]{2,1,0:T(8,128)(2,1)S(1)} %bitcast.4), channel_id=1, replica_groups=mesh['x'=4,'y'=8,'z'=8,'core'=2] {'y','z'}, dimensions={0} | all-to-all | bytes 262144 | tf_op jit(solution)/shard_map/all_to_all | solution.py:364
  66.0 0.0 copy-done.5
  66.0 0.0 copy-done.6
  66.0 0.2 block_sum.1
  66.1 17.4 %all_to_all.28.got_ref = bf16[64,24,128]{2,1,0:T(8,128)(2,1)S(1)} all-to-all(bf16[64,24,128]{2,1,0:T(8,128)(2,1)S(1)} %block_sum.1), channel_id=1, replica_groups=mesh['x'=4,'y'=8,'z'=8,'core'=2] {'y','z'}, dimensions={0} | all-to-all | bytes 786432 | tf_op jit(solution)/shard_map/all_to_all | solution.py:380
  83.6 0.2 plane_join.1
  83.7 13.2 %all_to_all.29.mine_ref = bf16[4,1056,128]{2,1,0:T(8,128)(2,1)S(1)} all-to-all(bf16[4,1056,128]{2,1,0:T(8,128)(2,1)S(1)} %plane_join.1), channel_id=1, replica_groups=mesh['x'=4,'y'=8,'z'=8,'core'=2] {'x'}, dimensions={0} | all-to-all | bytes 2162688 | tf_op jit(solution)/shard_map/all_to_all | solution.py:381
  96.9 0.0 copy-start.7
  96.9 7.7 %collective-permute-start.1 = (bf16[4,1056,128]{2,1,0:T(8,128)(2,1)S(1)}, bf16[4,1056,128]{2,1,0:T(8,128)(2,1)S(1)}, u32[]{:S(2)}, u32[]{:S(2)}) collective-permute-start(bf16[4,1056,128]{2,1,0:T(8,128)(2,1)S(1)} %all_to_all.29.mine_ref), channel_id=1, source_target_pairs={{0,1},{1,0},{2,3},{3,2},{4,5},{5,4},{6,7},{7,6},{8,9},{9,8},{10,11... | collective-permute-start | bytes 3244040 | tf_op jit(solution)/shard_map/ppermute | solution.py:382
  104.6 1.9 %input_grad.1 = bf16[12,49,512]{2,1,0:T(8,128)(2,1)} custom-call(bf16[768,1024]{1,0:T(8,128)(2,1)S(1)} %get-tuple-element.15.cg_ref, bf16[512,1024]{1,0:T(8,128)(2,1)S(1)} %copy-done), custom_call_target="tpu_custom_call" | custom-call | flops 805306368 | bytes 4194304 | tf_op jit(solution)/shard_map/input_grad/pallas_call | solution.py:338
  106.4 0.4 collective-permute-done.1.other_ref
  106.9 0.0 copy-done.7
  106.9 2.2 %update.1 = (f32[16,64]{1,0:T(8,128)}, f32[16,64]{1,0:T(8,128)}, bf16[512,1024]{1,0:T(8,128)(2,1)}, f32[2,1024]{1,0:T(2,128)}, f32[2,1024]{1,0:T(2,128)}) custom-call(bf16[4,1056,128]{2,1,0:T(8,128)(2,1)S(1)} %all_to_all.29.mine_ref, bf16[4,1056,128]{2,1,0:T(8,128)(2,1)S(1)} %collective-permute-done.1.other_ref, bf16[512,1024]{1,0:T(8,128)(2,1)S(1)} %copy-done, ...), custom_call_target="tpu_custom_call" | custom-call | tf_op jit(solution)/shard_map/update/pallas_call | solution.py:383
  (1 shorter events, 0.0 us)
Async XLA Ops:
  0.6 26.1 %copy-start.3 = (f32[12,1024]{1,0:T(8,128)S(1)}, f32[12,1024]{1,0:T(8,128)}, u32[]{:S(2)}) copy-start(f32[12,1024]{1,0:T(8,128)} %pool_ref.1) | copy-start | bytes 147460
  0.6 26.1 %copy-start.2 = (bf16[12,49,512]{2,1,0:T(8,128)(2,1)S(1)}, bf16[12,49,512]{2,1,0:T(8,128)(2,1)}, u32[]{:S(2)}) copy-start(bf16[12,49,512]{2,1,0:T(8,128)(2,1)} %act_ref.1) | copy-start | bytes 1806340
  0.7 26.1 %copy-start.4 = (f32[2,1024]{1,0:T(2,128)S(1)}, f32[2,1024]{1,0:T(2,128)}, u32[]{:S(2)}) copy-start(f32[2,1024]{1,0:T(2,128)} %bn_ref.3) | copy-start | bytes 24580
  0.7 26.1 %copy-start = (bf16[512,1024]{1,0:T(8,128)(2,1)S(1)}, bf16[512,1024]{1,0:T(8,128)(2,1)}, u32[]{:S(2)}) copy-start(bf16[512,1024]{1,0:T(8,128)(2,1)} %w_ref.5) | copy-start | bytes 3145732
  0.7 26.1 %copy-start.1 = (bf16[12,49,1024]{2,1,0:T(8,128)(2,1)S(1)}, bf16[12,49,1024]{2,1,0:T(8,128)(2,1)}, u32[]{:S(2)}) copy-start(bf16[12,49,1024]{2,1,0:T(8,128)(2,1)} %pre_ref.1) | copy-start | bytes 3612676
  28.7 5.5 %collective-permute-start = (bf16[256,1024]{1,0:T(8,128)(2,1)S(1)}, bf16[256,1024]{1,0:T(8,128)(2,1)S(1)}, u32[]{:S(2)}, u32[]{:S(2)}) collective-permute-start(bf16[256,1024]{1,0:T(8,128)(2,1)S(1)} %get-tuple-element.17), channel_id=1, source_target_pairs={{0,1},{1,0},{2,3},{3,2},{4,5},{5,4},{6,7},{7,6},{8,9},{9,8},{10,11... | collective-permute-start | bytes 1572872 | tf_op jit(solution)/shard_map/ppermute | solution.py:328
  34.3 31.7 %copy-start.5 = (f32[16,64]{1,0:T(8,128)S(1)}, f32[16,64]{1,0:T(8,128)}, u32[]{:S(2)}) copy-start(f32[16,64]{1,0:T(8,128)} %master_ref.3) | copy-start | bytes 12292
  34.3 31.7 %copy-start.6 = (f32[16,64]{1,0:T(8,128)S(1)}, f32[16,64]{1,0:T(8,128)}, u32[]{:S(2)}) copy-start(f32[16,64]{1,0:T(8,128)} %vel_ref.3) | copy-start | bytes 12292
  96.9 10.0 %copy-start.7 = (f32[2,1024]{1,0:T(2,128)S(1)}, f32[2,1024]{1,0:T(2,128)}, u32[]{:S(2)}) copy-start(f32[2,1024]{1,0:T(2,128)} %bnv_ref.1) | copy-start | bytes 24580
  96.9 10.0 %collective-permute-start.1 = (bf16[4,1056,128]{2,1,0:T(8,128)(2,1)S(1)}, bf16[4,1056,128]{2,1,0:T(8,128)(2,1)S(1)}, u32[]{:S(2)}, u32[]{:S(2)}) collective-permute-start(bf16[4,1056,128]{2,1,0:T(8,128)(2,1)S(1)} %all_to_all.29.mine_ref), channel_id=1, source_target_pairs={{0,1},{1,0},{2,3},{3,2},{4,5},{5,4},{6,7},{7,6},{8,9},{9,8},{10,11... | collective-permute-start | bytes 3244040 | tf_op jit(solution)/shard_map/ppermute | solution.py:382

commit v8 on v7

--- a/solution.py
+++ b/solution.py
@@ -211,7 +211,8 @@
 
 def update_kernel(
     mine_ref, other_ref, w_ref, master_ref, vel_ref, bn_ref, bnv_ref,
-    new_master_ref, new_vel_ref, new_w_hbm, new_bn_ref, new_bnv_ref, new_w, sems,
+    new_master_hbm, new_vel_hbm, new_w_hbm, new_bn_hbm, new_bnv_hbm,
+    new_master_ref, new_vel_ref, new_w, new_bn_ref, new_bnv_ref, sems, small_sems,
 ):
     core, layer = core_of(), lax.axis_index("z").astype(jnp.int32)
     row = (lax.axis_index("x") * N_Y + lax.axis_index("y")).astype(jnp.int32)
@@ -231,7 +232,30 @@
         wnorm = jnp.sqrt(norm[:, 0:1])
         gnorm = jnp.sqrt(square[:, 0:1])
         rate = learn_rate * (trust_coef * wnorm / (gnorm + weight_decay * wnorm))
-        stores = []
+        bn_grad = jnp.concatenate([totals[1], totals[0]], axis=0) * (1.0 / BATCH)
+        new_bnv = momentum * bnv_ref[...] + learn_rate * bn_grad
+        new_bnv_ref[...] = new_bnv
+        new_bn_ref[...] = bn_ref[...] - new_bnv
+        for h in range(2):
+
+            @pl.when(row // 16 == h)
+            def _():
+                start = pl.multiple_of(layer * 64 + row % 4 * 16, 16)
+                pair = parts[h][row % 16 // 4, pl.ds(start, 16), :].astype(f32)
+                own = jnp.where(core == 0, pair[:, :64], pair[:, 64:])
+                new_vel = momentum * vel_ref[...] + rate * (own + weight_decay * master_ref[...])
+                new_vel_ref[...] = new_vel
+                new_master_ref[...] = master_ref[...] - new_vel
+
+        small_pairs = (
+            (new_master_ref, new_master_hbm),
+            (new_vel_ref, new_vel_hbm),
+            (new_bn_ref, new_bn_hbm),
+            (new_bnv_ref, new_bnv_hbm),
+        )
+        stores = [pltpu.make_async_copy(here, there, small_sems.at[k]) for k, (here, there) in enumerate(small_pairs)]
+        for copy in stores:
+            copy.start()
         for x in range(N_X):
             tiles = [part[x, 512:1024, :].astype(f32).reshape(N_Y, N_Z, 8, 128) for part in parts]
             rows = slice(128 * x, 128 * x + 128)
@@ -248,21 +272,6 @@
                 new_w[rows, columns] = (decayed - rate * step).astype(bf16)
             stores.append(pltpu.make_async_copy(new_w.at[rows], new_w_hbm.at[rows], sems.at[x]))
             stores[-1].start()
-        bn_grad = jnp.concatenate([totals[1], totals[0]], axis=0) * (1.0 / BATCH)
-        new_bnv = momentum * bnv_ref[...] + learn_rate * bn_grad
-        new_bnv_ref[...] = new_bnv
-        new_bn_ref[...] = bn_ref[...] - new_bnv
-        for h in range(2):
-
-            @pl.when(row // 16 == h)
-            def _():
-                start = pl.multiple_of(layer * 64 + row % 4 * 16, 16)
-                pair = parts[h][row % 16 // 4, pl.ds(start, 16), :].astype(f32)
-                own = jnp.where(core == 0, pair[:, :64], pair[:, 64:])
-                new_vel = momentum * vel_ref[...] + rate * (own + weight_decay * master_ref[...])
-                new_vel_ref[...] = new_vel
-                new_master_ref[...] = master_ref[...] - new_vel
-
         for copy in stores:
             copy.wait()
 
@@ -286,7 +295,7 @@
 def body(activations, pre_activation, pooled_grad, weights, master, velocity, bn_params, bn_velocity):
     msg = pl.pallas_call(
         stats_kernel,
-        out_shape=shape((STAT_ROWS, 128), f32),
+        out_shape=pltpu.VMEM((STAT_ROWS, 128), f32),
         in_specs=[HBM] * 4,
         out_specs=VMEM,
         scratch_shapes=[
@@ -390,8 +399,16 @@
             shape((2, COUT), f32),
         ),
         in_specs=[VMEM] * 7,
-        out_specs=(VMEM, VMEM, HBM, VMEM, VMEM),
-        scratch_shapes=[pltpu.VMEM((CIN, COUT), bf16), pltpu.SemaphoreType.DMA((N_X,))],
+        out_specs=(HBM,) * 5,
+        scratch_shapes=[
+            pltpu.VMEM((16, 64), f32),
+            pltpu.VMEM((16, 64), f32),
+            pltpu.VMEM((CIN, COUT), bf16),
+            pltpu.VMEM((2, COUT), f32),
+            pltpu.VMEM((2, COUT), f32),
+            pltpu.SemaphoreType.DMA((N_X,)),
+            pltpu.SemaphoreType.DMA((4,)),
+        ],
         compiler_params=params(),
         name="update",
     )(mine, other, weights, master, velocity, bn_params, bn_velocity)

time: 109 us -> 108 us (level)
  no operation moved by 1% of the time
where the time goes in v8:
time: 108 us
  blocking collectives  83.6 us (77%)
  starting transfers between devices  11.6 us (11%)
  Pallas kernels  10.4 us (10%)
  waiting for transfers between devices  1.35 us (1%)
    all_to_all x1, blocking collectives, body(): arrived = lax.all_to_all(lines.reshape(N_Y * N_Z, 8, 128), PLANE, 0, 0)  19.1 us
    all_to_all x1, blocking collectives, body(): lax.all_to_all(block, PLANE, 0, 0)  17.4 us
    all_to_all x1, blocking collectives, body(): mine = lax.all_to_all(wide, 'x', 0, 0)  13.2 us
    all_to_all x1, blocking collectives, body(): stats = lax.all_to_all(chip, 'z', 0, 0)  13.1 us
    all_to_all x1, blocking collectives, body(): arrived = lax.all_to_all(halves.reshape(N_X, HALF // N_X, COUT), 'x', 0, 0)  12.4 us
    all_gather x1, blocking collectives, body(): lax.all_gather(msg, 'core')  8.38 us
    ppermute x1, starting transfers between devices, body(): other = lax.ppermute(mine, 'core', swap)  7.66 us
    ppermute x1, starting transfers between devices, body(): got = lax.ppermute(send, 'core', swap)  3.98 us
  transfers between devices with their start and end apart: 2, of which 2 were waited for; matrix products, arithmetic and copies ran while one was open for 0% of the time, Pallas kernels for 2%

profile of v8, /device:TPU:1, one launch (start us, length us, event | category | flops | bytes accessed | tf_op | source)
XLA Modules:
  0.0 107.8 jit_solution(15728863944855804146)
XLA Ops:
  0.6 0.0 copy-start.3
  0.6 0.0 copy-start.2
  0.7 0.0 copy-start.4
  0.7 0.0 copy-start
  0.7 0.0 copy-start.1
  0.7 3.7 %conv_stats.1 = f32[40,128]{1,0:T(8,128)S(1)} custom-call(bf16[12,49,512]{2,1,0:T(8,128)(2,1)} %act_ref.1, bf16[12,49,1024]{2,1,0:T(8,128)(2,1)} %pre_ref.1, f32[12,1024]{1,0:T(8,128)} %pool_ref.1, bf16[512,1024]{1,0:T(8,128)(2,1)} %w_ref.5), custom_call_target="tpu_custom_call" | custom-call | tf_op jit(solution)/shard_map/conv_stats/pallas_call | solution.py:296
  4.4 8.4 %all-gather = f32[80,128]{1,0:T(8,128)S(1)} all-gather(f32[40,128]{1,0:T(8,128)S(1)} %conv_stats.1), channel_id=2, replica_groups=mesh['x'=4,'y'=8,'z'=8,'core'=2] {'core'}, dimensions={0}, use_global_device_ids=true | all-gather | bytes 61440 | tf_op jit(solution)/shard_map/all_gather | solution.py:320
  12.8 13.1 %all_to_all.25.stat_ref = f32[8,40,128]{2,1,0:T(8,128)S(1)} all-to-all(f32[8,40,128]{2,1,0:T(8,128)S(1)} %chip_stats.1), channel_id=1, replica_groups=mesh['x'=4,'y'=8,'z'=8,'core'=2] {'z'}, dimensions={0} | all-to-all | bytes 327680 | tf_op jit(solution)/shard_map/all_to_all | solution.py:321
  25.9 0.0 copy-done.3
  25.9 0.0 copy-done.2
  25.9 0.0 copy-done.4
  25.9 0.0 copy-done
  25.9 0.0 copy-done.1
  25.9 2.0 %conv_grad.1 = (bf16[768,1024]{1,0:T(8,128)(2,1)S(1)}, bf16[768,512]{1,0:T(8,128)(2,1)S(1)}, bf16[256,1024]{1,0:T(8,128)(2,1)S(1)}, f32[8,128]{1,0:T(8,128)S(1)}) custom-call(f32[8,40,128]{2,1,0:T(8,128)S(1)} %all_to_all.25.stat_ref, bf16[512,1024]{1,0:T(8,128)(2,1)S(1)} %copy-done, bf16[12,49,512]{2,1,0:T(8,128)(2,1)S(1)} %copy-done.2, ...), custom_call_target="tpu_custom_call" | custom-call | tf_op jit(solution)/shard_map/conv_grad/pallas_call | solution.py:322
  27.9 4.0 %collective-permute-start = (bf16[256,1024]{1,0:T(8,128)(2,1)S(1)}, bf16[256,1024]{1,0:T(8,128)(2,1)S(1)}, u32[]{:S(2)}, u32[]{:S(2)}) collective-permute-start(bf16[256,1024]{1,0:T(8,128)(2,1)S(1)} %get-tuple-element.17), channel_id=1, source_target_pairs={{0,1},{1,0},{2,3},{3,2},{4,5},{5,4},{6,7},{7,6},{8,9},{9,8},{10,11... | collective-permute-start | bytes 1572872 | tf_op jit(solution)/shard_map/ppermute | solution.py:337
  31.9 0.6 keep_grad.1.keep_ref
  32.5 0.9 collective-permute-done.got_ref
  33.4 0.1 pair_sum.1
  33.5 0.0 copy-start.5
  33.5 0.0 copy-start.6
  33.5 12.4 %all_to_all.26.got_ref = bf16[4,64,1024]{2,1,0:T(8,128)(2,1)S(1)} all-to-all(bf16[4,64,1024]{2,1,0:T(8,128)(2,1)S(1)} %bitcast.3), channel_id=1, replica_groups=mesh['x'=4,'y'=8,'z'=8,'core'=2] {'x'}, dimensions={0} | all-to-all | bytes 1048576 | tf_op jit(solution)/shard_map/all_to_all | solution.py:364
  46.0 0.1 line_sum.1
  46.0 19.1 %all_to_all.27.got_ref = bf16[64,8,128]{2,1,0:T(8,128)(2,1)S(1)} all-to-all(bf16[64,8,128]{2,1,0:T(8,128)(2,1)S(1)} %bitcast.4), channel_id=1, replica_groups=mesh['x'=4,'y'=8,'z'=8,'core'=2] {'y','z'}, dimensions={0} | all-to-all | bytes 262144 | tf_op jit(solution)/shard_map/all_to_all | solution.py:373
  65.2 0.0 copy-done.5
  65.2 0.0 copy-done.6
  65.2 0.2 block_sum.1
  65.4 17.4 %all_to_all.28.got_ref = bf16[64,24,128]{2,1,0:T(8,128)(2,1)S(1)} all-to-all(bf16[64,24,128]{2,1,0:T(8,128)(2,1)S(1)} %block_sum.1), channel_id=1, replica_groups=mesh['x'=4,'y'=8,'z'=8,'core'=2] {'y','z'}, dimensions={0} | all-to-all | bytes 786432 | tf_op jit(solution)/shard_map/all_to_all | solution.py:389
  82.8 0.2 plane_join.1
  83.0 13.2 %all_to_all.29.mine_ref = bf16[4,1056,128]{2,1,0:T(8,128)(2,1)S(1)} all-to-all(bf16[4,1056,128]{2,1,0:T(8,128)(2,1)S(1)} %plane_join.1), channel_id=1, replica_groups=mesh['x'=4,'y'=8,'z'=8,'core'=2] {'x'}, dimensions={0} | all-to-all | bytes 2162688 | tf_op jit(solution)/shard_map/all_to_all | solution.py:390
  96.1 0.0 copy-start.7
  96.1 7.7 %collective-permute-start.1 = (bf16[4,1056,128]{2,1,0:T(8,128)(2,1)S(1)}, bf16[4,1056,128]{2,1,0:T(8,128)(2,1)S(1)}, u32[]{:S(2)}, u32[]{:S(2)}) collective-permute-start(bf16[4,1056,128]{2,1,0:T(8,128)(2,1)S(1)} %all_to_all.29.mine_ref), channel_id=1, source_target_pairs={{0,1},{1,0},{2,3},{3,2},{4,5},{5,4},{6,7},{7,6},{8,9},{9,8},{10,11... | collective-permute-start | bytes 3244040 | tf_op jit(solution)/shard_map/ppermute | solution.py:391
  103.8 1.9 %input_grad.1 = bf16[12,49,512]{2,1,0:T(8,128)(2,1)} custom-call(bf16[768,1024]{1,0:T(8,128)(2,1)S(1)} %get-tuple-element.15.cg_ref, bf16[512,1024]{1,0:T(8,128)(2,1)S(1)} %copy-done), custom_call_target="tpu_custom_call" | custom-call | flops 805306368 | bytes 4194304 | tf_op jit(solution)/shard_map/input_grad/pallas_call | solution.py:347
  105.7 0.4 collective-permute-done.1.other_ref
  106.1 0.0 copy-done.7
  106.1 1.7 %update.1 = (f32[16,64]{1,0:T(8,128)}, f32[16,64]{1,0:T(8,128)}, bf16[512,1024]{1,0:T(8,128)(2,1)}, f32[2,1024]{1,0:T(2,128)}, f32[2,1024]{1,0:T(2,128)}) custom-call(bf16[4,1056,128]{2,1,0:T(8,128)(2,1)S(1)} %all_to_all.29.mine_ref, bf16[4,1056,128]{2,1,0:T(8,128)(2,1)S(1)} %collective-permute-done.1.other_ref, bf16[512,1024]{1,0:T(8,128)(2,1)S(1)} %copy-done, ...), custom_call_target="tpu_custom_call" | custom-call | tf_op jit(solution)/shard_map/update/pallas_call | solution.py:392
  (1 shorter events, 0.0 us)
Async XLA Ops:
  0.6 25.3 %copy-start.3 = (f32[12,1024]{1,0:T(8,128)S(1)}, f32[12,1024]{1,0:T(8,128)}, u32[]{:S(2)}) copy-start(f32[12,1024]{1,0:T(8,128)} %pool_ref.1) | copy-start | bytes 147460
  0.6 25.3 %copy-start.2 = (bf16[12,49,512]{2,1,0:T(8,128)(2,1)S(1)}, bf16[12,49,512]{2,1,0:T(8,128)(2,1)}, u32[]{:S(2)}) copy-start(bf16[12,49,512]{2,1,0:T(8,128)(2,1)} %act_ref.1) | copy-start | bytes 1806340
  0.7 25.3 %copy-start.4 = (f32[2,1024]{1,0:T(2,128)S(1)}, f32[2,1024]{1,0:T(2,128)}, u32[]{:S(2)}) copy-start(f32[2,1024]{1,0:T(2,128)} %bn_ref.3) | copy-start | bytes 24580
  0.7 25.2 %copy-start = (bf16[512,1024]{1,0:T(8,128)(2,1)S(1)}, bf16[512,1024]{1,0:T(8,128)(2,1)}, u32[]{:S(2)}) copy-start(bf16[512,1024]{1,0:T(8,128)(2,1)} %w_ref.5) | copy-start | bytes 3145732
  0.7 25.2 %copy-start.1 = (bf16[12,49,1024]{2,1,0:T(8,128)(2,1)S(1)}, bf16[12,49,1024]{2,1,0:T(8,128)(2,1)}, u32[]{:S(2)}) copy-start(bf16[12,49,1024]{2,1,0:T(8,128)(2,1)} %pre_ref.1) | copy-start | bytes 3612676
  27.9 5.5 %collective-permute-start = (bf16[256,1024]{1,0:T(8,128)(2,1)S(1)}, bf16[256,1024]{1,0:T(8,128)(2,1)S(1)}, u32[]{:S(2)}, u32[]{:S(2)}) collective-permute-start(bf16[256,1024]{1,0:T(8,128)(2,1)S(1)} %get-tuple-element.17), channel_id=1, source_target_pairs={{0,1},{1,0},{2,3},{3,2},{4,5},{5,4},{6,7},{7,6},{8,9},{9,8},{10,11... | collective-permute-start | bytes 1572872 | tf_op jit(solution)/shard_map/ppermute | solution.py:337
  33.5 31.7 %copy-start.5 = (f32[16,64]{1,0:T(8,128)S(1)}, f32[16,64]{1,0:T(8,128)}, u32[]{:S(2)}) copy-start(f32[16,64]{1,0:T(8,128)} %master_ref.3) | copy-start | bytes 12292
  33.5 31.7 %copy-start.6 = (f32[16,64]{1,0:T(8,128)S(1)}, f32[16,64]{1,0:T(8,128)}, u32[]{:S(2)}) copy-start(f32[16,64]{1,0:T(8,128)} %vel_ref.3) | copy-start | bytes 12292
  96.1 10.0 %copy-start.7 = (f32[2,1024]{1,0:T(2,128)S(1)}, f32[2,1024]{1,0:T(2,128)}, u32[]{:S(2)}) copy-start(f32[2,1024]{1,0:T(2,128)} %bnv_ref.1) | copy-start | bytes 24580
  96.1 10.0 %collective-permute-start.1 = (bf16[4,1056,128]{2,1,0:T(8,128)(2,1)S(1)}, bf16[4,1056,128]{2,1,0:T(8,128)(2,1)S(1)}, u32[]{:S(2)}, u32[]{:S(2)}) collective-permute-start(bf16[4,1056,128]{2,1,0:T(8,128)(2,1)S(1)} %all_to_all.29.mine_ref), channel_id=1, source_target_pairs={{0,1},{1,0},{2,3},{3,2},{4,5},{5,4},{6,7},{7,6},{8,9},{9,8},{10,11... | collective-permute-start | bytes 3244040 | tf_op jit(solution)/shard_map/ppermute | solution.py:391

commit v9 on v8

--- a/solution.py
+++ b/solution.py
@@ -55,7 +55,7 @@
     return block
 
 
-def stats_kernel(act_hbm, pre_hbm, pool_hbm, w_hbm, msg_ref, act, pre, pool, w, actp, conv, sem_in):
+def stats_kernel(act_hbm, pre_hbm, pool_hbm, w_hbm, msg_ref, conv, actp, pre, pool, act, w, sem_in):
     step = IMG // PARTS
     loads = []
     for k in range(PARTS):
@@ -108,7 +108,7 @@
 
 
 def grad_kernel(
-    stat_ref, w_ref, act_ref, pre_ref, pool_ref, bn_ref, cg_ref, actp, send_ref, line_ref, conv_ref, lines
+    stat_ref, msg_ref, conv_ref, act_ref, pre_ref, pool_ref, bn_ref, cg_ref, actp, send_ref, line_ref, lines
 ):
     core, layer = core_of(), lax.axis_index("z").astype(jnp.int32)
     sums = jnp.sum(stat_ref[...], axis=0)
@@ -122,22 +122,18 @@
     lines[8:16, :] = sum_upx
     line_ref[...] = jnp.broadcast_to(lines[pl.ds(core * 8 + layer, 1), :], (8, 128))
     scale = fold(bn_ref[0:1, :]) * rstd
-    shift = unfold(scale * (sum_up / M))
-    slope = unfold(scale * (sum_upx / M) * rstd)
-    mean = unfold(mean)
-    scale = unfold(scale)
-    actp[...] = jnp.zeros_like(actp)
+    shift = scale * (sum_up / M)
+    slope = scale * (sum_upx / M) * rstd
+    local = IMG * PIX
+    cg_total = unfold(scale * msg_ref[16:24, :] - local * shift - slope * (msg_ref[0:8, :] - local * mean))
+    mean, scale, shift, slope = unfold(mean), unfold(scale), unfold(shift), unfold(slope)
+    actp[...] = act_ref[...]
     for i in range(IMG):
-        actp[STRIDE * i : STRIDE * i + PIX, :] = act_ref[i]
-    conv_ref[...] = jnp.dot(actp[...], w_ref[...], preferred_element_type=f32).astype(bf16)
-    cg_ref[...] = jnp.zeros_like(cg_ref)
-    cg_total = jnp.zeros((1, COUT), f32)
-    for i in range(IMG):
+        cg_ref[STRIDE * i + 48 : STRIDE * i + 64, :] = jnp.zeros((16, COUT), bf16)
         conv = conv_ref[STRIDE * i : STRIDE * i + STRIDE, :].astype(f32)[:PIX]
         on = scale * (pool_ref[i : i + 1, :] / PIX) - shift
-        low = (jnp.where(pre_ref[i].astype(f32) > 0, on, -shift) - slope * (conv - mean)).astype(bf16)
-        cg_ref[STRIDE * i : STRIDE * i + PIX, :] = low
-        cg_total += jnp.sum(low.astype(f32), axis=0, keepdims=True)
+        cg = jnp.where(pre_ref[i].astype(f32) > 0, on, -shift) - slope * (conv - mean)
+        cg_ref[STRIDE * i : STRIDE * i + PIX, :] = cg.astype(bf16)
     edge = actp[48:64, :].astype(f32)
     row = lax.broadcasted_iota(jnp.int32, edge.shape, 0)
     actp[48:64, :] = jnp.where((row >= 1) & (row < 4), -act_mean, edge).astype(bf16)
@@ -293,18 +289,20 @@
 
 
 def body(activations, pre_activation, pooled_grad, weights, master, velocity, bn_params, bn_velocity):
-    msg = pl.pallas_call(
+    msg, conv, act, pre, pool = pl.pallas_call(
         stats_kernel,
-        out_shape=pltpu.VMEM((STAT_ROWS, 128), f32),
+        out_shape=(
+            pltpu.VMEM((STAT_ROWS, 128), f32),
+            pltpu.VMEM((ROWS, COUT), bf16),
+            pltpu.VMEM((ROWS, CIN), bf16),
+            pltpu.VMEM((IMG, PIX, COUT), bf16),
+            pltpu.VMEM((IMG, COUT), f32),
+        ),
         in_specs=[HBM] * 4,
-        out_specs=VMEM,
+        out_specs=(VMEM,) * 5,
         scratch_shapes=[
             pltpu.VMEM((IMG, PIX, CIN), bf16),
-            pltpu.VMEM((IMG, PIX, COUT), bf16),
-            pltpu.VMEM((IMG, COUT), f32),
             pltpu.VMEM((CIN, COUT), bf16),
-            pltpu.VMEM((ROWS, CIN), bf16),
-            pltpu.VMEM((ROWS, COUT), bf16),
             pltpu.SemaphoreType.DMA((4, PARTS)),
         ],
         compiler_params=params(60),
@@ -327,12 +325,12 @@
             shape((HALF, COUT), bf16),
             shape((8, 128), f32),
         ),
-        in_specs=[VMEM] * 6,
+        in_specs=[VMEM] * 7,
         out_specs=(VMEM,) * 4,
-        scratch_shapes=[pltpu.VMEM((ROWS, COUT), bf16), pltpu.VMEM((16, 128), f32)],
+        scratch_shapes=[pltpu.VMEM((16, 128), f32)],
         compiler_params=params(),
         name="conv_grad",
-    )(stats, weights, activations, pre_activation, pooled_grad, bn_params)
+    )(stats, msg, conv, act, pre, pool, bn_params)
     swap = [(0, 1), (1, 0)]
     got = lax.ppermute(send, "core", swap)
     keep = pl.pallas_call(

time: 108 us -> 108 us (level)
  no operation moved by 1% of the time
where the time goes in v9:
time: 108 us; the launch traced here: 107 us
  blocking collectives  83.8 us (78%)
  starting transfers between devices  11.6 us (11%)
  Pallas kernels  9.79 us (9%)
  waiting for transfers between devices  1.34 us (1%)
    all_to_all x1, blocking collectives, body(): arrived = lax.all_to_all(lines.reshape(N_Y * N_Z, 8, 128), PLANE, 0, 0)  19.1 us
    all_to_all x1, blocking collectives, body(): lax.all_to_all(block, PLANE, 0, 0)  17.4 us
    all_to_all x1, blocking collectives, body(): mine = lax.all_to_all(wide, 'x', 0, 0)  13.3 us
    all_to_all x1, blocking collectives, body(): stats = lax.all_to_all(chip, 'z', 0, 0)  13.1 us
    all_to_all x1, blocking collectives, body(): arrived = lax.all_to_all(halves.reshape(N_X, HALF // N_X, COUT), 'x', 0, 0)  12.4 us
    all_gather x1, blocking collectives, body(): lax.all_gather(msg, 'core')  8.38 us
    ppermute x1, starting transfers between devices, body(): other = lax.ppermute(mine, 'core', swap)  7.66 us
    ppermute x1, starting transfers between devices, body(): got = lax.ppermute(send, 'core', swap)  3.98 us
  transfers between devices with their start and end apart: 2, of which 2 were waited for; matrix products, arithmetic and copies ran while one was open for 0% of the time, Pallas kernels for 2%

profile of v9, /device:TPU:1, one launch (start us, length us, event | category | flops | bytes accessed | tf_op | source)
XLA Modules:
  0.0 107.3 jit_solution(15651242803013976507)
XLA Ops:
  0.6 0.0 copy-start.1
  0.6 3.8 %conv_stats.1 = (f32[40,128]{1,0:T(8,128)S(1)}, bf16[768,1024]{1,0:T(8,128)(2,1)S(1)}, bf16[768,512]{1,0:T(8,128)(2,1)S(1)}, bf16[12,49,1024]{2,1,0:T(8,128)(2,1)S(1)}, f32[12,1024]{1,0:T(8,128)S(1)}) custom-call(bf16[12,49,512]{2,1,0:T(8,128)(2,1)} %act_hbm.1, bf16[12,49,1024]{2,1,0:T(8,128)(2,1)} %pre_hbm.1, f32[12,1024]{1,0:T(8,128)} %pool_hbm.1, ...), custom_call_target="tpu_custom_call" | custom-call | tf_op jit(solution)/shard_map/conv_stats/pallas_call | solution.py:292
  4.4 8.4 %all-gather = f32[80,128]{1,0:T(8,128)S(1)} all-gather(f32[40,128]{1,0:T(8,128)S(1)} %get-tuple-element.20.msg_ref), channel_id=2, replica_groups=mesh['x'=4,'y'=8,'z'=8,'core'=2] {'core'}, dimensions={0}, use_global_device_ids=true | all-gather | bytes 61440 | tf_op jit(solution)/shard_map/all_gather | solution.py:318
  12.8 13.1 %all_to_all.25.stat_ref = f32[8,40,128]{2,1,0:T(8,128)S(1)} all-to-all(f32[8,40,128]{2,1,0:T(8,128)S(1)} %chip_stats.1), channel_id=1, replica_groups=mesh['x'=4,'y'=8,'z'=8,'core'=2] {'z'}, dimensions={0} | all-to-all | bytes 327680 | tf_op jit(solution)/shard_map/all_to_all | solution.py:319
  25.9 0.0 copy-done.1
  25.9 1.3 %conv_grad.1 = (bf16[768,1024]{1,0:T(8,128)(2,1)S(1)}, bf16[768,512]{1,0:T(8,128)(2,1)S(1)}, bf16[256,1024]{1,0:T(8,128)(2,1)S(1)}, f32[8,128]{1,0:T(8,128)S(1)}) custom-call(f32[8,40,128]{2,1,0:T(8,128)S(1)} %all_to_all.25.stat_ref, f32[40,128]{1,0:T(8,128)S(1)} %get-tuple-element.20.msg_ref, bf16[768,1024]{1,0:T(8,128)(2,1)S(1)} %get-tuple-element.21.conv_ref, ...), custom_call_target="tpu_custom_call" | custom-call | tf_op jit(solution)/shard_map/conv_grad/pallas_call | solution.py:320
  27.2 4.0 %collective-permute-start = (bf16[256,1024]{1,0:T(8,128)(2,1)S(1)}, bf16[256,1024]{1,0:T(8,128)(2,1)S(1)}, u32[]{:S(2)}, u32[]{:S(2)}) collective-permute-start(bf16[256,1024]{1,0:T(8,128)(2,1)S(1)} %get-tuple-element.27), channel_id=1, source_target_pairs={{0,1},{1,0},{2,3},{3,2},{4,5},{5,4},{6,7},{7,6},{8,9},{9,8},{10,11... | collective-permute-start | bytes 1572872 | tf_op jit(solution)/shard_map/ppermute | solution.py:335
  31.2 0.6 keep_grad.1.keep_ref
  31.8 0.9 collective-permute-done.got_ref
  32.7 0.1 pair_sum.1
  32.8 0.0 copy-start.2
  32.8 0.0 copy-start.3
  32.9 12.4 %all_to_all.26.got_ref = bf16[4,64,1024]{2,1,0:T(8,128)(2,1)S(1)} all-to-all(bf16[4,64,1024]{2,1,0:T(8,128)(2,1)S(1)} %bitcast.3), channel_id=1, replica_groups=mesh['x'=4,'y'=8,'z'=8,'core'=2] {'x'}, dimensions={0} | all-to-all | bytes 1048576 | tf_op jit(solution)/shard_map/all_to_all | solution.py:362
  45.3 0.1 line_sum.1
  45.4 19.1 %all_to_all.27.got_ref = bf16[64,8,128]{2,1,0:T(8,128)(2,1)S(1)} all-to-all(bf16[64,8,128]{2,1,0:T(8,128)(2,1)S(1)} %bitcast.4), channel_id=1, replica_groups=mesh['x'=4,'y'=8,'z'=8,'core'=2] {'y','z'}, dimensions={0} | all-to-all | bytes 262144 | tf_op jit(solution)/shard_map/all_to_all | solution.py:371
  64.5 0.0 copy-done.2
  64.5 0.0 copy-done.3
  64.5 0.2 block_sum.1
  64.7 17.4 %all_to_all.28.got_ref = bf16[64,24,128]{2,1,0:T(8,128)(2,1)S(1)} all-to-all(bf16[64,24,128]{2,1,0:T(8,128)(2,1)S(1)} %block_sum.1), channel_id=1, replica_groups=mesh['x'=4,'y'=8,'z'=8,'core'=2] {'y','z'}, dimensions={0} | all-to-all | bytes 786432 | tf_op jit(solution)/shard_map/all_to_all | solution.py:387
  82.1 0.2 plane_join.1
  82.3 0.0 copy-start
  82.3 13.3 %all_to_all.29.mine_ref = bf16[4,1056,128]{2,1,0:T(8,128)(2,1)S(1)} all-to-all(bf16[4,1056,128]{2,1,0:T(8,128)(2,1)S(1)} %plane_join.1), channel_id=1, replica_groups=mesh['x'=4,'y'=8,'z'=8,'core'=2] {'x'}, dimensions={0} | all-to-all | bytes 2162688 | tf_op jit(solution)/shard_map/all_to_all | solution.py:388
  95.6 0.0 copy-start.4
  95.6 7.7 %collective-permute-start.1 = (bf16[4,1056,128]{2,1,0:T(8,128)(2,1)S(1)}, bf16[4,1056,128]{2,1,0:T(8,128)(2,1)S(1)}, u32[]{:S(2)}, u32[]{:S(2)}) collective-permute-start(bf16[4,1056,128]{2,1,0:T(8,128)(2,1)S(1)} %all_to_all.29.mine_ref), channel_id=1, source_target_pairs={{0,1},{1,0},{2,3},{3,2},{4,5},{5,4},{6,7},{7,6},{8,9},{9,8},{10,11... | collective-permute-start | bytes 3244040 | tf_op jit(solution)/shard_map/ppermute | solution.py:389
  103.3 0.0 copy-done
  103.3 1.9 %input_grad.1 = bf16[12,49,512]{2,1,0:T(8,128)(2,1)} custom-call(bf16[768,1024]{1,0:T(8,128)(2,1)S(1)} %get-tuple-element.25.cg_ref, bf16[512,1024]{1,0:T(8,128)(2,1)S(1)} %copy-done), custom_call_target="tpu_custom_call" | custom-call | flops 805306368 | bytes 4194304 | tf_op jit(solution)/shard_map/input_grad/pallas_call | solution.py:345
  105.2 0.4 collective-permute-done.1.other_ref
  105.6 0.0 copy-done.4
  105.6 1.7 %update.1 = (f32[16,64]{1,0:T(8,128)}, f32[16,64]{1,0:T(8,128)}, bf16[512,1024]{1,0:T(8,128)(2,1)}, f32[2,1024]{1,0:T(2,128)}, f32[2,1024]{1,0:T(2,128)}) custom-call(bf16[4,1056,128]{2,1,0:T(8,128)(2,1)S(1)} %all_to_all.29.mine_ref, bf16[4,1056,128]{2,1,0:T(8,128)(2,1)S(1)} %collective-permute-done.1.other_ref, bf16[512,1024]{1,0:T(8,128)(2,1)S(1)} %copy-done, ...), custom_call_target="tpu_custom_call" | custom-call | tf_op jit(solution)/shard_map/update/pallas_call | solution.py:390
  (1 shorter events, 0.0 us)
Async XLA Ops:
  0.6 25.3 %copy-start.1 = (f32[2,1024]{1,0:T(2,128)S(1)}, f32[2,1024]{1,0:T(2,128)}, u32[]{:S(2)}) copy-start(f32[2,1024]{1,0:T(2,128)} %bn_ref.3) | copy-start | bytes 24580
  27.2 5.5 %collective-permute-start = (bf16[256,1024]{1,0:T(8,128)(2,1)S(1)}, bf16[256,1024]{1,0:T(8,128)(2,1)S(1)}, u32[]{:S(2)}, u32[]{:S(2)}) collective-permute-start(bf16[256,1024]{1,0:T(8,128)(2,1)S(1)} %get-tuple-element.27), channel_id=1, source_target_pairs={{0,1},{1,0},{2,3},{3,2},{4,5},{5,4},{6,7},{7,6},{8,9},{9,8},{10,11... | collective-permute-start | bytes 1572872 | tf_op jit(solution)/shard_map/ppermute | solution.py:335
  32.8 31.7 %copy-start.2 = (f32[16,64]{1,0:T(8,128)S(1)}, f32[16,64]{1,0:T(8,128)}, u32[]{:S(2)}) copy-start(f32[16,64]{1,0:T(8,128)} %master_ref.3) | copy-start | bytes 12292
  32.8 31.7 %copy-start.3 = (f32[16,64]{1,0:T(8,128)S(1)}, f32[16,64]{1,0:T(8,128)}, u32[]{:S(2)}) copy-start(f32[16,64]{1,0:T(8,128)} %vel_ref.3) | copy-start | bytes 12292
  82.3 21.0 %copy-start = (bf16[512,1024]{1,0:T(8,128)(2,1)S(1)}, bf16[512,1024]{1,0:T(8,128)(2,1)}, u32[]{:S(2)}) copy-start(bf16[512,1024]{1,0:T(8,128)(2,1)} %w_ref.3) | copy-start | bytes 3145732
  95.6 10.0 %copy-start.4 = (f32[2,1024]{1,0:T(2,128)S(1)}, f32[2,1024]{1,0:T(2,128)}, u32[]{:S(2)}) copy-start(f32[2,1024]{1,0:T(2,128)} %bnv_ref.1) | copy-start | bytes 24580
  95.6 10.0 %collective-permute-start.1 = (bf16[4,1056,128]{2,1,0:T(8,128)(2,1)S(1)}, bf16[4,1056,128]{2,1,0:T(8,128)(2,1)S(1)}, u32[]{:S(2)}, u32[]{:S(2)}) collective-permute-start(bf16[4,1056,128]{2,1,0:T(8,128)(2,1)S(1)} %all_to_all.29.mine_ref), channel_id=1, source_target_pairs={{0,1},{1,0},{2,3},{3,2},{4,5},{5,4},{6,7},{7,6},{8,9},{9,8},{10,11... | collective-permute-start | bytes 3244040 | tf_op jit(solution)/shard_map/ppermute | solution.py:389

commit v10 on v9

--- a/solution.py
+++ b/solution.py
@@ -25,7 +25,7 @@
 SIDE_ROWS = 24
 WIDE_ROWS = 1056
 PARTS = 2
-STRIP = 512
+STRIP = 256
 bf16, f32 = jnp.bfloat16, jnp.float32
 
 
@@ -82,21 +82,28 @@
     for strip in strips:
         value = jnp.dot(actp[...], w[:, strip], preferred_element_type=f32).astype(bf16)
         conv[:, strip] = value
-        value = value.astype(f32)
-        total = jnp.sum(value, axis=0, keepdims=True)
-        square = jnp.sum(value * value, axis=0, keepdims=True)
+        value = value.astype(f32).reshape(IMG, STRIDE, STRIP)[:, :56]
+        total = jnp.sum(jnp.sum(value, axis=0), axis=0, keepdims=True)
+        square = jnp.sum(jnp.sum(value * value, axis=0), axis=0, keepdims=True)
         lines.append([total, square])
     for copy in later:
         copy.wait()
     for k, strip in enumerate(strips):
-        up = jnp.zeros((1, STRIP), f32)
-        up_conv = jnp.zeros((1, STRIP), f32)
+        wide, last = (8, STRIP), (1, STRIP)
+        up, up_conv = jnp.zeros(wide, f32), jnp.zeros(wide, f32)
+        up_last, up_conv_last = jnp.zeros(last, f32), jnp.zeros(last, f32)
         for i in range(IMG):
             value = conv[STRIDE * i : STRIDE * i + STRIDE, strip].astype(f32)[:PIX]
             passed = pre[i, :, strip].astype(f32) > 0
             share = pool[i : i + 1, strip] / PIX
-            up += share * jnp.sum(jnp.where(passed, 1.0, 0.0), axis=0, keepdims=True)
-            up_conv += share * jnp.sum(jnp.where(passed, value, 0.0), axis=0, keepdims=True)
+            ones = jnp.where(passed, 1.0, 0.0)
+            value = jnp.where(passed, value, 0.0)
+            up += share * jnp.sum(ones[:48].reshape(6, 8, STRIP), axis=0)
+            up_conv += share * jnp.sum(value[:48].reshape(6, 8, STRIP), axis=0)
+            up_last += share * ones[48:49]
+            up_conv_last += share * value[48:49]
+        up = jnp.sum(up, axis=0, keepdims=True) + up_last
+        up_conv = jnp.sum(up_conv, axis=0, keepdims=True) + up_conv_last
         lines[k] += [up, up_conv]
     sums = [fold(jnp.concatenate([line[q] for line in lines], axis=1)) for q in range(4)]
     msg = jnp.concatenate(sums + [fold(act_total), jnp.zeros((4, 128), f32)], axis=0)

time: 108 us -> 108 us (level)
  no operation moved by 1% of the time
where the time goes in v10:
time: 108 us; the launch traced here: 107 us
  blocking collectives  83.8 us (78%)
  starting transfers between devices  11.6 us (11%)
  Pallas kernels  9.57 us (9%)
  waiting for transfers between devices  1.34 us (1%)
    all_to_all x1, blocking collectives, body(): arrived = lax.all_to_all(lines.reshape(N_Y * N_Z, 8, 128), PLANE, 0, 0)  19.1 us
    all_to_all x1, blocking collectives, body(): lax.all_to_all(block, PLANE, 0, 0)  17.4 us
    all_to_all x1, blocking collectives, body(): mine = lax.all_to_all(wide, 'x', 0, 0)  13.3 us
    all_to_all x1, blocking collectives, body(): stats = lax.all_to_all(chip, 'z', 0, 0)  13.1 us
    all_to_all x1, blocking collectives, body(): arrived = lax.all_to_all(halves.reshape(N_X, HALF // N_X, COUT), 'x', 0, 0)  12.4 us
    all_gather x1, blocking collectives, body(): lax.all_gather(msg, 'core')  8.38 us
    ppermute x1, starting transfers between devices, body(): other = lax.ppermute(mine, 'core', swap)  7.66 us
    ppermute x1, starting transfers between devices, body(): got = lax.ppermute(send, 'core', swap)  3.99 us
  transfers between devices with their start and end apart: 2, of which 2 were waited for; matrix products, arithmetic and copies ran while one was open for 0% of the time, Pallas kernels for 2%

profile of v10, /device:TPU:1, one launch (start us, length us, event | category | flops | bytes accessed | tf_op | source)
XLA Modules:
  0.0 107.1 jit_solution(13579338747724493614)
XLA Ops:
  0.6 0.0 copy-start.1
  0.6 3.6 %conv_stats.1 = (f32[40,128]{1,0:T(8,128)S(1)}, bf16[768,1024]{1,0:T(8,128)(2,1)S(1)}, bf16[768,512]{1,0:T(8,128)(2,1)S(1)}, bf16[12,49,1024]{2,1,0:T(8,128)(2,1)S(1)}, f32[12,1024]{1,0:T(8,128)S(1)}) custom-call(bf16[12,49,512]{2,1,0:T(8,128)(2,1)} %act_hbm.1, bf16[12,49,1024]{2,1,0:T(8,128)(2,1)} %pre_hbm.1, f32[12,1024]{1,0:T(8,128)} %pool_hbm.1, ...), custom_call_target="tpu_custom_call" | custom-call | tf_op jit(solution)/shard_map/conv_stats/pallas_call | solution.py:299
  4.2 8.4 %all-gather = f32[80,128]{1,0:T(8,128)S(1)} all-gather(f32[40,128]{1,0:T(8,128)S(1)} %get-tuple-element.20.msg_ref), channel_id=2, replica_groups=mesh['x'=4,'y'=8,'z'=8,'core'=2] {'core'}, dimensions={0}, use_global_device_ids=true | all-gather | bytes 61440 | tf_op jit(solution)/shard_map/all_gather | solution.py:325
  12.6 13.1 %all_to_all.25.stat_ref = f32[8,40,128]{2,1,0:T(8,128)S(1)} all-to-all(f32[8,40,128]{2,1,0:T(8,128)S(1)} %chip_stats.1), channel_id=1, replica_groups=mesh['x'=4,'y'=8,'z'=8,'core'=2] {'z'}, dimensions={0} | all-to-all | bytes 327680 | tf_op jit(solution)/shard_map/all_to_all | solution.py:326
  25.7 0.0 copy-done.1
  25.7 1.3 %conv_grad.1 = (bf16[768,1024]{1,0:T(8,128)(2,1)S(1)}, bf16[768,512]{1,0:T(8,128)(2,1)S(1)}, bf16[256,1024]{1,0:T(8,128)(2,1)S(1)}, f32[8,128]{1,0:T(8,128)S(1)}) custom-call(f32[8,40,128]{2,1,0:T(8,128)S(1)} %all_to_all.25.stat_ref, f32[40,128]{1,0:T(8,128)S(1)} %get-tuple-element.20.msg_ref, bf16[768,1024]{1,0:T(8,128)(2,1)S(1)} %get-tuple-element.21.conv_ref, ...), custom_call_target="tpu_custom_call" | custom-call | tf_op jit(solution)/shard_map/conv_grad/pallas_call | solution.py:327
  27.0 4.0 %collective-permute-start = (bf16[256,1024]{1,0:T(8,128)(2,1)S(1)}, bf16[256,1024]{1,0:T(8,128)(2,1)S(1)}, u32[]{:S(2)}, u32[]{:S(2)}) collective-permute-start(bf16[256,1024]{1,0:T(8,128)(2,1)S(1)} %get-tuple-element.27), channel_id=1, source_target_pairs={{0,1},{1,0},{2,3},{3,2},{4,5},{5,4},{6,7},{7,6},{8,9},{9,8},{10,11... | collective-permute-start | bytes 1572872 | tf_op jit(solution)/shard_map/ppermute | solution.py:342
  31.0 0.6 keep_grad.1.keep_ref
  31.6 0.9 collective-permute-done.got_ref
  32.5 0.1 pair_sum.1
  32.6 0.0 copy-start.2
  32.6 0.0 copy-start.3
  32.7 12.4 %all_to_all.26.got_ref = bf16[4,64,1024]{2,1,0:T(8,128)(2,1)S(1)} all-to-all(bf16[4,64,1024]{2,1,0:T(8,128)(2,1)S(1)} %bitcast.3), channel_id=1, replica_groups=mesh['x'=4,'y'=8,'z'=8,'core'=2] {'x'}, dimensions={0} | all-to-all | bytes 1048576 | tf_op jit(solution)/shard_map/all_to_all | solution.py:369
  45.1 0.1 line_sum.1
  45.2 19.1 %all_to_all.27.got_ref = bf16[64,8,128]{2,1,0:T(8,128)(2,1)S(1)} all-to-all(bf16[64,8,128]{2,1,0:T(8,128)(2,1)S(1)} %bitcast.4), channel_id=1, replica_groups=mesh['x'=4,'y'=8,'z'=8,'core'=2] {'y','z'}, dimensions={0} | all-to-all | bytes 262144 | tf_op jit(solution)/shard_map/all_to_all | solution.py:378
  64.3 0.0 copy-done.2
  64.3 0.0 copy-done.3
  64.3 0.2 block_sum.1
  64.5 17.4 %all_to_all.28.got_ref = bf16[64,24,128]{2,1,0:T(8,128)(2,1)S(1)} all-to-all(bf16[64,24,128]{2,1,0:T(8,128)(2,1)S(1)} %block_sum.1), channel_id=1, replica_groups=mesh['x'=4,'y'=8,'z'=8,'core'=2] {'y','z'}, dimensions={0} | all-to-all | bytes 786432 | tf_op jit(solution)/shard_map/all_to_all | solution.py:394
  81.9 0.2 plane_join.1
  82.1 0.0 copy-start
  82.1 13.3 %all_to_all.29.mine_ref = bf16[4,1056,128]{2,1,0:T(8,128)(2,1)S(1)} all-to-all(bf16[4,1056,128]{2,1,0:T(8,128)(2,1)S(1)} %plane_join.1), channel_id=1, replica_groups=mesh['x'=4,'y'=8,'z'=8,'core'=2] {'x'}, dimensions={0} | all-to-all | bytes 2162688 | tf_op jit(solution)/shard_map/all_to_all | solution.py:395
  95.4 0.0 copy-start.4
  95.4 7.7 %collective-permute-start.1 = (bf16[4,1056,128]{2,1,0:T(8,128)(2,1)S(1)}, bf16[4,1056,128]{2,1,0:T(8,128)(2,1)S(1)}, u32[]{:S(2)}, u32[]{:S(2)}) collective-permute-start(bf16[4,1056,128]{2,1,0:T(8,128)(2,1)S(1)} %all_to_all.29.mine_ref), channel_id=1, source_target_pairs={{0,1},{1,0},{2,3},{3,2},{4,5},{5,4},{6,7},{7,6},{8,9},{9,8},{10,11... | collective-permute-start | bytes 3244040 | tf_op jit(solution)/shard_map/ppermute | solution.py:396
  103.1 0.0 copy-done
  103.1 1.9 %input_grad.1 = bf16[12,49,512]{2,1,0:T(8,128)(2,1)} custom-call(bf16[768,1024]{1,0:T(8,128)(2,1)S(1)} %get-tuple-element.25.cg_ref, bf16[512,1024]{1,0:T(8,128)(2,1)S(1)} %copy-done), custom_call_target="tpu_custom_call" | custom-call | flops 805306368 | bytes 4194304 | tf_op jit(solution)/shard_map/input_grad/pallas_call | solution.py:352
  104.9 0.4 collective-permute-done.1.other_ref
  105.4 0.0 copy-done.4
  105.4 1.7 %update.1 = (f32[16,64]{1,0:T(8,128)}, f32[16,64]{1,0:T(8,128)}, bf16[512,1024]{1,0:T(8,128)(2,1)}, f32[2,1024]{1,0:T(2,128)}, f32[2,1024]{1,0:T(2,128)}) custom-call(bf16[4,1056,128]{2,1,0:T(8,128)(2,1)S(1)} %all_to_all.29.mine_ref, bf16[4,1056,128]{2,1,0:T(8,128)(2,1)S(1)} %collective-permute-done.1.other_ref, bf16[512,1024]{1,0:T(8,128)(2,1)S(1)} %copy-done, ...), custom_call_target="tpu_custom_call" | custom-call | tf_op jit(solution)/shard_map/update/pallas_call | solution.py:397
  (1 shorter events, 0.0 us)
Async XLA Ops:
  0.6 25.1 %copy-start.1 = (f32[2,1024]{1,0:T(2,128)S(1)}, f32[2,1024]{1,0:T(2,128)}, u32[]{:S(2)}) copy-start(f32[2,1024]{1,0:T(2,128)} %bn_ref.3) | copy-start | bytes 24580
  27.0 5.5 %collective-permute-start = (bf16[256,1024]{1,0:T(8,128)(2,1)S(1)}, bf16[256,1024]{1,0:T(8,128)(2,1)S(1)}, u32[]{:S(2)}, u32[]{:S(2)}) collective-permute-start(bf16[256,1024]{1,0:T(8,128)(2,1)S(1)} %get-tuple-element.27), channel_id=1, source_target_pairs={{0,1},{1,0},{2,3},{3,2},{4,5},{5,4},{6,7},{7,6},{8,9},{9,8},{10,11... | collective-permute-start | bytes 1572872 | tf_op jit(solution)/shard_map/ppermute | solution.py:342
  32.6 31.7 %copy-start.2 = (f32[16,64]{1,0:T(8,128)S(1)}, f32[16,64]{1,0:T(8,128)}, u32[]{:S(2)}) copy-start(f32[16,64]{1,0:T(8,128)} %master_ref.3) | copy-start | bytes 12292
  32.6 31.7 %copy-start.3 = (f32[16,64]{1,0:T(8,128)S(1)}, f32[16,64]{1,0:T(8,128)}, u32[]{:S(2)}) copy-start(f32[16,64]{1,0:T(8,128)} %vel_ref.3) | copy-start | bytes 12292
  82.1 21.0 %copy-start = (bf16[512,1024]{1,0:T(8,128)(2,1)S(1)}, bf16[512,1024]{1,0:T(8,128)(2,1)}, u32[]{:S(2)}) copy-start(bf16[512,1024]{1,0:T(8,128)(2,1)} %w_ref.3) | copy-start | bytes 3145732
  95.4 10.0 %copy-start.4 = (f32[2,1024]{1,0:T(2,128)S(1)}, f32[2,1024]{1,0:T(2,128)}, u32[]{:S(2)}) copy-start(f32[2,1024]{1,0:T(2,128)} %bnv_ref.1) | copy-start | bytes 24580
  95.4 10.0 %collective-permute-start.1 = (bf16[4,1056,128]{2,1,0:T(8,128)(2,1)S(1)}, bf16[4,1056,128]{2,1,0:T(8,128)(2,1)S(1)}, u32[]{:S(2)}, u32[]{:S(2)}) collective-permute-start(bf16[4,1056,128]{2,1,0:T(8,128)(2,1)S(1)} %all_to_all.29.mine_ref), channel_id=1, source_target_pairs={{0,1},{1,0},{2,3},{3,2},{4,5},{5,4},{6,7},{7,6},{8,9},{9,8},{10,11... | collective-permute-start | bytes 3244040 | tf_op jit(solution)/shard_map/ppermute | solution.py:396

commit v11 on v10

--- a/solution.py
+++ b/solution.py
@@ -14,7 +14,7 @@
 IMG, PIX, STRIDE = 12, 49, 64
 CIN, COUT = 512, 1024
 ROWS = IMG * STRIDE
-HALF = CIN // 2
+WIDE = COUT // 2
 N_ROW, N_COL = 32, 16
 N_X, N_Y, N_Z = 4, 8, 8
 M = PIX * IMG * N_COL
@@ -114,8 +114,32 @@
     out_ref[...] = jnp.broadcast_to((got_ref[0] + got_ref[1])[None], out_ref.shape)
 
 
+def fill(vectors, half, conv_ref, pre_ref, pool_ref, cg_ref):
+    columns = pl.ds(pl.multiple_of(half * WIDE, WIDE), WIDE)
+    mean, scale, shift, slope, cg_total = [
+        unfold(jnp.where(half == 0, vectors[8 * k : 8 * k + 4], vectors[8 * k + 4 : 8 * k + 8])) for k in range(5)
+    ]
+    for i in range(IMG):
+        cg_ref[STRIDE * i + 48 : STRIDE * i + 64, :] = jnp.zeros((16, WIDE), bf16)
+        conv = conv_ref[STRIDE * i : STRIDE * i + STRIDE, columns].astype(f32)[:PIX]
+        on = scale * (pool_ref[i : i + 1, columns] / PIX) - shift
+        cg = jnp.where(pre_ref[i, :, columns].astype(f32) > 0, on, -shift) - slope * (conv - mean)
+        cg_ref[STRIDE * i : STRIDE * i + PIX, :] = cg.astype(bf16)
+    high, middle, rest = split(cg_total)
+    edge = cg_ref[48:64, :].astype(f32)
+    cg_ref[48:64, :] = (edge + rows_of(4, [jnp.zeros_like(high), high, middle, rest], edge.shape)).astype(bf16)
+
+
+def product(actp, cg_ref):
+    return lax.dot_general(actp[...], cg_ref[...], (((0,), (0,)), ((), ())), preferred_element_type=f32)
+
+
+def core_of():
+    return lax.axis_index("core").astype(jnp.int32)
+
+
 def grad_kernel(
-    stat_ref, msg_ref, conv_ref, act_ref, pre_ref, pool_ref, bn_ref, cg_ref, actp, send_ref, line_ref, lines
+    stat_ref, msg_ref, conv_ref, act_ref, pre_ref, pool_ref, bn_ref, cg_ref, actp, send_ref, line_ref, vec_ref, lines
 ):
     core, layer = core_of(), lax.axis_index("z").astype(jnp.int32)
     sums = jnp.sum(stat_ref[...], axis=0)
@@ -132,39 +156,28 @@
     shift = scale * (sum_up / M)
     slope = scale * (sum_upx / M) * rstd
     local = IMG * PIX
-    cg_total = unfold(scale * msg_ref[16:24, :] - local * shift - slope * (msg_ref[0:8, :] - local * mean))
-    mean, scale, shift, slope = unfold(mean), unfold(scale), unfold(shift), unfold(slope)
+    cg_total = scale * msg_ref[16:24, :] - local * shift - slope * (msg_ref[0:8, :] - local * mean)
+    vectors = jnp.concatenate([mean, scale, shift, slope, cg_total], axis=0)
+    vec_ref[...] = vectors
     actp[...] = act_ref[...]
-    for i in range(IMG):
-        cg_ref[STRIDE * i + 48 : STRIDE * i + 64, :] = jnp.zeros((16, COUT), bf16)
-        conv = conv_ref[STRIDE * i : STRIDE * i + STRIDE, :].astype(f32)[:PIX]
-        on = scale * (pool_ref[i : i + 1, :] / PIX) - shift
-        cg = jnp.where(pre_ref[i].astype(f32) > 0, on, -shift) - slope * (conv - mean)
-        cg_ref[STRIDE * i : STRIDE * i + PIX, :] = cg.astype(bf16)
     edge = actp[48:64, :].astype(f32)
     row = lax.broadcasted_iota(jnp.int32, edge.shape, 0)
     actp[48:64, :] = jnp.where((row >= 1) & (row < 4), -act_mean, edge).astype(bf16)
-    high, middle, rest = split(cg_total)
-    edge = cg_ref[48:64, :].astype(f32)
-    cg_ref[48:64, :] = (edge + rows_of(4, [jnp.zeros_like(high), high, middle, rest], edge.shape)).astype(bf16)
-    send_ref[...] = half_grad(actp, cg_ref, 1 - core).astype(bf16)
-
-
-def core_of():
-    return lax.axis_index("core").astype(jnp.int32)
-
-
-def half_grad(actp, cg_ref, half):
-    columns = actp[:, pl.ds(pl.multiple_of(half * HALF, HALF), HALF)]
-    return lax.dot_general(columns, cg_ref[...], (((0,), (0,)), ((), ())), preferred_element_type=f32)
-
-
-def keep_kernel(actp, cg_ref, keep_ref):
-    keep_ref[...] = half_grad(actp, cg_ref, core_of())
-
-
-def back_kernel(cg_ref, w_ref, out_ref):
-    back = lax.dot_general(cg_ref[...], w_ref[...], (((1,), (1,)), ((), ())), preferred_element_type=f32)
+    fill(vectors, 1 - core, conv_ref, pre_ref, pool_ref, cg_ref)
+    send_ref[...] = product(actp, cg_ref).astype(bf16)
+
+
+def keep_kernel(vec_ref, conv_ref, pre_ref, pool_ref, actp, cg_ref, keep_ref):
+    fill(vec_ref[...], core_of(), conv_ref, pre_ref, pool_ref, cg_ref)
+    keep_ref[...] = product(actp, cg_ref)
+
+
+def back_kernel(sent_ref, kept_ref, w_ref, out_ref):
+    core = core_of()
+    back = jnp.zeros((ROWS, CIN), f32)
+    for half, cg_ref in ((1 - core, sent_ref), (core, kept_ref)):
+        w = w_ref[:, pl.ds(pl.multiple_of(half * WIDE, WIDE), WIDE)]
+        back += lax.dot_general(cg_ref[...], w, (((1,), (1,)), ((), ())), preferred_element_type=f32)
     for i in range(IMG):
         out_ref[i] = back[STRIDE * i : STRIDE * i + PIX].astype(bf16)
 
@@ -174,9 +187,9 @@
 
 
 def line_kernel(got_ref, out_ref):
-    total = jnp.sum(got_ref[...].astype(f32), axis=0).reshape(N_Z, 8, COUT)
-    for y in range(N_Y):
-        out_ref[y] = total[:, :, 128 * y : 128 * y + 128].astype(bf16)
+    total = jnp.sum(got_ref[...].astype(f32), axis=0).reshape(16, 8, WIDE)
+    for j in range(4):
+        out_ref[j] = total[:, :, 128 * j : 128 * j + 128].astype(bf16)
 
 
 def block_kernel(got_ref, line_ref, master_ref, vel_ref, out_ref):
@@ -241,10 +254,10 @@
         new_bn_ref[...] = bn_ref[...] - new_bnv
         for h in range(2):
 
-            @pl.when(row // 16 == h)
+            @pl.when(layer // 4 == h)
             def _():
-                start = pl.multiple_of(layer * 64 + row % 4 * 16, 16)
-                pair = parts[h][row % 16 // 4, pl.ds(start, 16), :].astype(f32)
+                start = pl.multiple_of(layer % 4 * 128 + row % 8 * 16, 16)
+                pair = parts[h][row // 8, pl.ds(start, 16), :].astype(f32)
                 own = jnp.where(core == 0, pair[:, :64], pair[:, 64:])
                 new_vel = momentum * vel_ref[...] + rate * (own + weight_decay * master_ref[...])
                 new_vel_ref[...] = new_vel
@@ -262,15 +275,14 @@
         for x in range(N_X):
             tiles = [part[x, 512:1024, :].astype(f32).reshape(N_Y, N_Z, 8, 128) for part in parts]
             rows = slice(128 * x, 128 * x + 128)
-            h, strip = x // 2, x % 2 * 2
             for z in range(N_Z):
                 columns = slice(128 * z, 128 * z + 128)
                 even, odd = [tile[:, z] for tile in tiles]
                 top = jnp.concatenate([even[:, :, :64], odd[:, :, :64]], axis=2)
                 bottom = jnp.concatenate([even[:, :, 64:], odd[:, :, 64:]], axis=2)
                 decayed = jnp.stack([top, bottom], axis=1).reshape(128, 128)
-                lines = slice(64 * z, 64 * z + 64)
-                step = jnp.concatenate([parts[h][strip, lines, :], parts[h][strip + 1, lines, :]], axis=0).astype(f32)
+                lines = slice(128 * (z % 4), 128 * (z % 4) + 128)
+                step = parts[z // 4][x, lines, :].astype(f32)
                 step += weight_decay * w_ref[rows, columns].astype(f32)
                 new_w[rows, columns] = (decayed - rate * step).astype(bf16)
             stores.append(pltpu.make_async_copy(new_w.at[rows], new_w_hbm.at[rows], sems.at[x]))
@@ -312,7 +324,7 @@
             pltpu.VMEM((CIN, COUT), bf16),
             pltpu.SemaphoreType.DMA((4, PARTS)),
         ],
-        compiler_params=params(60),
+        compiler_params=params(56),
         name="conv_stats",
     )(activations, pre_activation, pooled_grad, weights)
     chip = pl.pallas_call(
@@ -324,52 +336,53 @@
         name="chip_stats",
     )(lax.all_gather(msg, "core"))
     stats = lax.all_to_all(chip, "z", 0, 0)
-    conv_grad, act, send, line = pl.pallas_call(
+    sent, act, send, line, vectors = pl.pallas_call(
         grad_kernel,
         out_shape=(
-            shape((ROWS, COUT), bf16),
+            shape((ROWS, WIDE), bf16),
             shape((ROWS, CIN), bf16),
-            shape((HALF, COUT), bf16),
+            shape((CIN, WIDE), bf16),
             shape((8, 128), f32),
+            shape((40, 128), f32),
         ),
         in_specs=[VMEM] * 7,
-        out_specs=(VMEM,) * 4,
+        out_specs=(VMEM,) * 5,
         scratch_shapes=[pltpu.VMEM((16, 128), f32)],
         compiler_params=params(),
         name="conv_grad",
     )(stats, msg, conv, act, pre, pool, bn_params)
     swap = [(0, 1), (1, 0)]
     got = lax.ppermute(send, "core", swap)
-    keep = pl.pallas_call(
+    kept, keep = pl.pallas_call(
         keep_kernel,
-        out_shape=shape((HALF, COUT), f32),
-        in_specs=[VMEM] * 2,
-        out_specs=VMEM,
-        compiler_params=params(),
-        cost_estimate=pl.CostEstimate(flops=2 * ROWS * HALF * COUT, bytes_accessed=4 << 20, transcendentals=0),
+        out_shape=(shape((ROWS, WIDE), bf16), shape((CIN, WIDE), f32)),
+        in_specs=[VMEM] * 5,
+        out_specs=(VMEM,) * 2,
+        compiler_params=params(),
+        cost_estimate=pl.CostEstimate(flops=2 * ROWS * CIN * WIDE, bytes_accessed=4 << 20, transcendentals=0),
         name="keep_grad",
-    )(act, conv_grad)
+    )(vectors, conv, pre, pool, act)
     input_grad = pl.pallas_call(
         back_kernel,
         out_shape=shape((IMG, PIX, CIN), bf16),
-        in_specs=[VMEM] * 2,
+        in_specs=[VMEM] * 3,
         out_specs=VMEM,
         compiler_params=params(),
         cost_estimate=pl.CostEstimate(flops=2 * ROWS * CIN * COUT, bytes_accessed=4 << 20, transcendentals=0),
         name="input_grad",
-    )(conv_grad, weights)
+    )(sent, kept, weights)
     halves = pl.pallas_call(
         pair_kernel,
-        out_shape=shape((HALF, COUT), bf16),
+        out_shape=shape((CIN, WIDE), bf16),
         in_specs=[VMEM] * 2,
         out_specs=VMEM,
         compiler_params=params(),
         name="pair_sum",
     )(keep, got)
-    arrived = lax.all_to_all(halves.reshape(N_X, HALF // N_X, COUT), "x", 0, 0)
+    arrived = lax.all_to_all(halves.reshape(N_X, CIN // N_X, WIDE), "x", 0, 0)
     lines = pl.pallas_call(
         line_kernel,
-        out_shape=shape((N_Y, N_Z, 8, 128), bf16),
+        out_shape=shape((4, 16, 8, 128), bf16),
         in_specs=[VMEM],
         out_specs=VMEM,
         compiler_params=params(),

time: 108 us -> 107 us (level)
  no operation moved by 1% of the time
where the time goes in v11:
time: 107 us; the launch traced here: 106 us
  blocking collectives  83.8 us (78%)
  starting transfers between devices  11.5 us (11%)
  Pallas kernels  9.19 us (9%)
  waiting for transfers between devices  1.2 us (1%)
    all_to_all x1, blocking collectives, body(): arrived = lax.all_to_all(lines.reshape(N_Y * N_Z, 8, 128), PLANE, 0, 0)  19.1 us
    all_to_all x1, blocking collectives, body(): lax.all_to_all(block, PLANE, 0, 0)  17.4 us
    all_to_all x1, blocking collectives, body(): mine = lax.all_to_all(wide, 'x', 0, 0)  13.3 us
    all_to_all x1, blocking collectives, body(): stats = lax.all_to_all(chip, 'z', 0, 0)  13.1 us
    all_to_all x1, blocking collectives, body(): arrived = lax.all_to_all(halves.reshape(N_X, CIN // N_X, WIDE), 'x', 0, 0)  12.4 us
    all_gather x1, blocking collectives, body(): lax.all_gather(msg, 'core')  8.38 us
    ppermute x1, starting transfers between devices, body(): other = lax.ppermute(mine, 'core', swap)  7.53 us
    ppermute x1, starting transfers between devices, body(): got = lax.ppermute(send, 'core', swap)  3.98 us
  transfers between devices with their start and end apart: 2, of which 2 were waited for; matrix products, arithmetic and copies ran while one was open for 0% of the time, Pallas kernels for 2%

profile of v11, /device:TPU:1, one launch (start us, length us, event | category | flops | bytes accessed | tf_op | source)
XLA Modules:
  0.0 106.4 jit_solution(14647604345938320077)
XLA Ops:
  0.6 0.0 copy-start.1
  0.6 3.6 %conv_stats.1 = (f32[40,128]{1,0:T(8,128)S(1)}, bf16[768,1024]{1,0:T(8,128)(2,1)S(1)}, bf16[768,512]{1,0:T(8,128)(2,1)S(1)}, bf16[12,49,1024]{2,1,0:T(8,128)(2,1)S(1)}, f32[12,1024]{1,0:T(8,128)S(1)}) custom-call(bf16[12,49,512]{2,1,0:T(8,128)(2,1)} %act_hbm.1, bf16[12,49,1024]{2,1,0:T(8,128)(2,1)} %pre_hbm.1, f32[12,1024]{1,0:T(8,128)} %pool_hbm.1, ...), custom_call_target="tpu_custom_call" | custom-call | tf_op jit(solution)/shard_map/conv_stats/pallas_call | solution.py:311
  4.2 8.4 %all-gather = f32[80,128]{1,0:T(8,128)S(1)} all-gather(f32[40,128]{1,0:T(8,128)S(1)} %get-tuple-element.23.msg_ref), channel_id=2, replica_groups=mesh['x'=4,'y'=8,'z'=8,'core'=2] {'core'}, dimensions={0}, use_global_device_ids=true | all-gather | bytes 61440 | tf_op jit(solution)/shard_map/all_gather | solution.py:337
  12.6 13.1 %all_to_all.25.stat_ref = f32[8,40,128]{2,1,0:T(8,128)S(1)} all-to-all(f32[8,40,128]{2,1,0:T(8,128)S(1)} %chip_stats.1), channel_id=1, replica_groups=mesh['x'=4,'y'=8,'z'=8,'core'=2] {'z'}, dimensions={0} | all-to-all | bytes 327680 | tf_op jit(solution)/shard_map/all_to_all | solution.py:338
  25.7 0.0 copy-done.1
  25.7 0.8 conv_grad.1
  26.6 4.0 %collective-permute-start = (bf16[512,512]{1,0:T(8,128)(2,1)S(1)}, bf16[512,512]{1,0:T(8,128)(2,1)S(1)}, u32[]{:S(2)}, u32[]{:S(2)}) collective-permute-start(bf16[512,512]{1,0:T(8,128)(2,1)S(1)} %get-tuple-element.33), channel_id=1, source_target_pairs={{0,1},{1,0},{2,3},{3,2},{4,5},{5,4},{6,7},{7,6},{8,9},{9,8},{10,11... | collective-permute-start | bytes 1572872 | tf_op jit(solution)/shard_map/ppermute | solution.py:355
  30.5 0.7 keep_grad.1
  31.3 0.8 collective-permute-done.got_ref
  32.1 0.1 pair_sum.1
  32.1 0.0 copy-start.2
  32.2 0.0 copy-start.3
  32.2 12.4 %all_to_all.26.got_ref = bf16[4,128,512]{2,1,0:T(8,128)(2,1)S(1)} all-to-all(bf16[4,128,512]{2,1,0:T(8,128)(2,1)S(1)} %bitcast.3), channel_id=1, replica_groups=mesh['x'=4,'y'=8,'z'=8,'core'=2] {'x'}, dimensions={0} | all-to-all | bytes 1048576 | tf_op jit(solution)/shard_map/all_to_all | solution.py:382
  44.6 0.1 line_sum.1
  44.7 19.1 %all_to_all.27.got_ref = bf16[64,8,128]{2,1,0:T(8,128)(2,1)S(1)} all-to-all(bf16[64,8,128]{2,1,0:T(8,128)(2,1)S(1)} %bitcast.4), channel_id=1, replica_groups=mesh['x'=4,'y'=8,'z'=8,'core'=2] {'y','z'}, dimensions={0} | all-to-all | bytes 262144 | tf_op jit(solution)/shard_map/all_to_all | solution.py:391
  63.8 0.0 copy-done.2
  63.8 0.0 copy-done.3
  63.8 0.2 block_sum.1
  64.0 17.4 %all_to_all.28.got_ref = bf16[64,24,128]{2,1,0:T(8,128)(2,1)S(1)} all-to-all(bf16[64,24,128]{2,1,0:T(8,128)(2,1)S(1)} %block_sum.1), channel_id=1, replica_groups=mesh['x'=4,'y'=8,'z'=8,'core'=2] {'y','z'}, dimensions={0} | all-to-all | bytes 786432 | tf_op jit(solution)/shard_map/all_to_all | solution.py:407
  81.4 0.2 plane_join.1
  81.6 0.0 copy-start
  81.6 13.3 %all_to_all.29.mine_ref = bf16[4,1056,128]{2,1,0:T(8,128)(2,1)S(1)} all-to-all(bf16[4,1056,128]{2,1,0:T(8,128)(2,1)S(1)} %plane_join.1), channel_id=1, replica_groups=mesh['x'=4,'y'=8,'z'=8,'core'=2] {'x'}, dimensions={0} | all-to-all | bytes 2162688 | tf_op jit(solution)/shard_map/all_to_all | solution.py:408
  94.9 7.5 %collective-permute-start.1 = (bf16[4,1056,128]{2,1,0:T(8,128)(2,1)S(1)}, bf16[4,1056,128]{2,1,0:T(8,128)(2,1)S(1)}, u32[]{:S(2)}, u32[]{:S(2)}) collective-permute-start(bf16[4,1056,128]{2,1,0:T(8,128)(2,1)S(1)} %all_to_all.29.mine_ref), channel_id=1, source_target_pairs={{0,1},{1,0},{2,3},{3,2},{4,5},{5,4},{6,7},{7,6},{8,9},{9,8},{10,11... | collective-permute-start | bytes 3244040 | tf_op jit(solution)/shard_map/ppermute | solution.py:409
  102.4 0.0 copy-done
  102.5 0.0 copy-start.4
  102.5 1.9 %input_grad.1 = bf16[12,49,512]{2,1,0:T(8,128)(2,1)} custom-call(bf16[768,512]{1,0:T(8,128)(2,1)S(1)} %get-tuple-element.28.sent_ref, bf16[768,512]{1,0:T(8,128)(2,1)S(1)} %get-tuple-element.31.kept_ref, bf16[512,1024]{1,0:T(8,128)(2,1)S(1)} %copy-done), custom_call_target="tpu_custom_call" | custom-call | flops 805306368 | bytes 4194304 | tf_op jit(solution)/shard_map/input_grad/pallas_call | solution.py:365
  104.3 0.4 collective-permute-done.1.other_ref
  104.8 0.0 copy-done.4
  104.8 1.7 %update.1 = (f32[16,64]{1,0:T(8,128)}, f32[16,64]{1,0:T(8,128)}, bf16[512,1024]{1,0:T(8,128)(2,1)}, f32[2,1024]{1,0:T(2,128)}, f32[2,1024]{1,0:T(2,128)}) custom-call(bf16[4,1056,128]{2,1,0:T(8,128)(2,1)S(1)} %all_to_all.29.mine_ref, bf16[4,1056,128]{2,1,0:T(8,128)(2,1)S(1)} %collective-permute-done.1.other_ref, bf16[512,1024]{1,0:T(8,128)(2,1)S(1)} %copy-done, ...), custom_call_target="tpu_custom_call" | custom-call | tf_op jit(solution)/shard_map/update/pallas_call | solution.py:410
  (1 shorter events, 0.0 us)
Async XLA Ops:
  0.6 25.1 %copy-start.1 = (f32[2,1024]{1,0:T(2,128)S(1)}, f32[2,1024]{1,0:T(2,128)}, u32[]{:S(2)}) copy-start(f32[2,1024]{1,0:T(2,128)} %bn_ref.3) | copy-start | bytes 24580
  26.6 5.5 %collective-permute-start = (bf16[512,512]{1,0:T(8,128)(2,1)S(1)}, bf16[512,512]{1,0:T(8,128)(2,1)S(1)}, u32[]{:S(2)}, u32[]{:S(2)}) collective-permute-start(bf16[512,512]{1,0:T(8,128)(2,1)S(1)} %get-tuple-element.33), channel_id=1, source_target_pairs={{0,1},{1,0},{2,3},{3,2},{4,5},{5,4},{6,7},{7,6},{8,9},{9,8},{10,11... | collective-permute-start | bytes 1572872 | tf_op jit(solution)/shard_map/ppermute | solution.py:355
  32.1 31.7 %copy-start.2 = (f32[16,64]{1,0:T(8,128)S(1)}, f32[16,64]{1,0:T(8,128)}, u32[]{:S(2)}) copy-start(f32[16,64]{1,0:T(8,128)} %master_ref.3) | copy-start | bytes 12292
  32.2 31.7 %copy-start.3 = (f32[16,64]{1,0:T(8,128)S(1)}, f32[16,64]{1,0:T(8,128)}, u32[]{:S(2)}) copy-start(f32[16,64]{1,0:T(8,128)} %vel_ref.3) | copy-start | bytes 12292
  81.6 20.8 %copy-start = (bf16[512,1024]{1,0:T(8,128)(2,1)S(1)}, bf16[512,1024]{1,0:T(8,128)(2,1)}, u32[]{:S(2)}) copy-start(bf16[512,1024]{1,0:T(8,128)(2,1)} %w_ref.3) | copy-start | bytes 3145732
  94.9 9.9 %collective-permute-start.1 = (bf16[4,1056,128]{2,1,0:T(8,128)(2,1)S(1)}, bf16[4,1056,128]{2,1,0:T(8,128)(2,1)S(1)}, u32[]{:S(2)}, u32[]{:S(2)}) collective-permute-start(bf16[4,1056,128]{2,1,0:T(8,128)(2,1)S(1)} %all_to_all.29.mine_ref), channel_id=1, source_target_pairs={{0,1},{1,0},{2,3},{3,2},{4,5},{5,4},{6,7},{7,6},{8,9},{9,8},{10,11... | collective-permute-start | bytes 3244040 | tf_op jit(solution)/shard_map/ppermute | solution.py:409
  102.5 2.3 %copy-start.4 = (f32[2,1024]{1,0:T(2,128)S(1)}, f32[2,1024]{1,0:T(2,128)}, u32[]{:S(2)}) copy-start(f32[2,1024]{1,0:T(2,128)} %bnv_ref.1) | copy-start | bytes 24580

commit v12 on v11

--- a/solution.py
+++ b/solution.py
@@ -76,7 +76,8 @@
         copy.wait()
     for i in range(IMG):
         actp[STRIDE * i : STRIDE * i + PIX, :] = act[i]
-    act_total = jnp.sum(actp[...].astype(f32), axis=0, keepdims=True)
+    act_total = actp[...].astype(f32).reshape(IMG, STRIDE, CIN)[:, :56]
+    act_total = jnp.sum(jnp.sum(act_total, axis=0), axis=0, keepdims=True)
     strips = [slice(STRIP * k, STRIP * k + STRIP) for k in range(COUT // STRIP)]
     lines = []
     for strip in strips:

time: 107 us -> 107 us (level)
  no operation moved by 1% of the time
where the time goes in v12:
time: 107 us; the launch traced here: 106 us
  blocking collectives  83.8 us (78%)
  starting transfers between devices  11.5 us (11%)
  Pallas kernels  9.2 us (9%)
  waiting for transfers between devices  1.2 us (1%)
    all_to_all x1, blocking collectives, body(): arrived = lax.all_to_all(lines.reshape(N_Y * N_Z, 8, 128), PLANE, 0, 0)  19.1 us
    all_to_all x1, blocking collectives, body(): lax.all_to_all(block, PLANE, 0, 0)  17.4 us
    all_to_all x1, blocking collectives, body(): mine = lax.all_to_all(wide, 'x', 0, 0)  13.3 us
    all_to_all x1, blocking collectives, body(): stats = lax.all_to_all(chip, 'z', 0, 0)  13.1 us
    all_to_all x1, blocking collectives, body(): arrived = lax.all_to_all(halves.reshape(N_X, CIN // N_X, WIDE), 'x', 0, 0)  12.4 us
    all_gather x1, blocking collectives, body(): lax.all_gather(msg, 'core')  8.37 us
    ppermute x1, starting transfers between devices, body(): other = lax.ppermute(mine, 'core', swap)  7.53 us
    ppermute x1, starting transfers between devices, body(): got = lax.ppermute(send, 'core', swap)  3.98 us
  transfers between devices with their start and end apart: 2, of which 2 were waited for; matrix products, arithmetic and copies ran while one was open for 0% of the time, Pallas kernels for 2%

profile of v12, /device:TPU:1, one launch (start us, length us, event | category | flops | bytes accessed | tf_op | source)
XLA Modules:
  0.0 106.4 jit_solution(6402387481850041826)
XLA Ops:
  0.6 0.0 copy-start.1
  0.6 3.6 %conv_stats.1 = (f32[40,128]{1,0:T(8,128)S(1)}, bf16[768,1024]{1,0:T(8,128)(2,1)S(1)}, bf16[768,512]{1,0:T(8,128)(2,1)S(1)}, bf16[12,49,1024]{2,1,0:T(8,128)(2,1)S(1)}, f32[12,1024]{1,0:T(8,128)S(1)}) custom-call(bf16[12,49,512]{2,1,0:T(8,128)(2,1)} %act_hbm.1, bf16[12,49,1024]{2,1,0:T(8,128)(2,1)} %pre_hbm.1, f32[12,1024]{1,0:T(8,128)} %pool_hbm.1, ...), custom_call_target="tpu_custom_call" | custom-call | tf_op jit(solution)/shard_map/conv_stats/pallas_call | solution.py:312
  4.3 8.4 %all-gather = f32[80,128]{1,0:T(8,128)S(1)} all-gather(f32[40,128]{1,0:T(8,128)S(1)} %get-tuple-element.23.msg_ref), channel_id=2, replica_groups=mesh['x'=4,'y'=8,'z'=8,'core'=2] {'core'}, dimensions={0}, use_global_device_ids=true | all-gather | bytes 61440 | tf_op jit(solution)/shard_map/all_gather | solution.py:338
  12.6 13.1 %all_to_all.25.stat_ref = f32[8,40,128]{2,1,0:T(8,128)S(1)} all-to-all(f32[8,40,128]{2,1,0:T(8,128)S(1)} %chip_stats.1), channel_id=1, replica_groups=mesh['x'=4,'y'=8,'z'=8,'core'=2] {'z'}, dimensions={0} | all-to-all | bytes 327680 | tf_op jit(solution)/shard_map/all_to_all | solution.py:339
  25.8 0.0 copy-done.1
  25.8 0.8 conv_grad.1
  26.6 4.0 %collective-permute-start = (bf16[512,512]{1,0:T(8,128)(2,1)S(1)}, bf16[512,512]{1,0:T(8,128)(2,1)S(1)}, u32[]{:S(2)}, u32[]{:S(2)}) collective-permute-start(bf16[512,512]{1,0:T(8,128)(2,1)S(1)} %get-tuple-element.33), channel_id=1, source_target_pairs={{0,1},{1,0},{2,3},{3,2},{4,5},{5,4},{6,7},{7,6},{8,9},{9,8},{10,11... | collective-permute-start | bytes 1572872 | tf_op jit(solution)/shard_map/ppermute | solution.py:356
  30.5 0.7 keep_grad.1
  31.3 0.8 collective-permute-done.got_ref
  32.1 0.1 pair_sum.1
  32.2 0.0 copy-start.2
  32.2 0.0 copy-start.3
  32.2 12.4 %all_to_all.26.got_ref = bf16[4,128,512]{2,1,0:T(8,128)(2,1)S(1)} all-to-all(bf16[4,128,512]{2,1,0:T(8,128)(2,1)S(1)} %bitcast.3), channel_id=1, replica_groups=mesh['x'=4,'y'=8,'z'=8,'core'=2] {'x'}, dimensions={0} | all-to-all | bytes 1048576 | tf_op jit(solution)/shard_map/all_to_all | solution.py:383
  44.6 0.1 line_sum.1
  44.7 19.1 %all_to_all.27.got_ref = bf16[64,8,128]{2,1,0:T(8,128)(2,1)S(1)} all-to-all(bf16[64,8,128]{2,1,0:T(8,128)(2,1)S(1)} %bitcast.4), channel_id=1, replica_groups=mesh['x'=4,'y'=8,'z'=8,'core'=2] {'y','z'}, dimensions={0} | all-to-all | bytes 262144 | tf_op jit(solution)/shard_map/all_to_all | solution.py:392
  63.8 0.0 copy-done.2
  63.8 0.0 copy-done.3
  63.8 0.2 block_sum.1
  64.0 17.4 %all_to_all.28.got_ref = bf16[64,24,128]{2,1,0:T(8,128)(2,1)S(1)} all-to-all(bf16[64,24,128]{2,1,0:T(8,128)(2,1)S(1)} %block_sum.1), channel_id=1, replica_groups=mesh['x'=4,'y'=8,'z'=8,'core'=2] {'y','z'}, dimensions={0} | all-to-all | bytes 786432 | tf_op jit(solution)/shard_map/all_to_all | solution.py:408
  81.4 0.2 plane_join.1
  81.6 0.0 copy-start
  81.6 13.3 %all_to_all.29.mine_ref = bf16[4,1056,128]{2,1,0:T(8,128)(2,1)S(1)} all-to-all(bf16[4,1056,128]{2,1,0:T(8,128)(2,1)S(1)} %plane_join.1), channel_id=1, replica_groups=mesh['x'=4,'y'=8,'z'=8,'core'=2] {'x'}, dimensions={0} | all-to-all | bytes 2162688 | tf_op jit(solution)/shard_map/all_to_all | solution.py:409
  94.9 7.5 %collective-permute-start.1 = (bf16[4,1056,128]{2,1,0:T(8,128)(2,1)S(1)}, bf16[4,1056,128]{2,1,0:T(8,128)(2,1)S(1)}, u32[]{:S(2)}, u32[]{:S(2)}) collective-permute-start(bf16[4,1056,128]{2,1,0:T(8,128)(2,1)S(1)} %all_to_all.29.mine_ref), channel_id=1, source_target_pairs={{0,1},{1,0},{2,3},{3,2},{4,5},{5,4},{6,7},{7,6},{8,9},{9,8},{10,11... | collective-permute-start | bytes 3244040 | tf_op jit(solution)/shard_map/ppermute | solution.py:410
  102.4 0.0 copy-done
  102.5 0.0 copy-start.4
  102.5 1.9 %input_grad.1 = bf16[12,49,512]{2,1,0:T(8,128)(2,1)} custom-call(bf16[768,512]{1,0:T(8,128)(2,1)S(1)} %get-tuple-element.28.sent_ref, bf16[768,512]{1,0:T(8,128)(2,1)S(1)} %get-tuple-element.31.kept_ref, bf16[512,1024]{1,0:T(8,128)(2,1)S(1)} %copy-done), custom_call_target="tpu_custom_call" | custom-call | flops 805306368 | bytes 4194304 | tf_op jit(solution)/shard_map/input_grad/pallas_call | solution.py:366
  104.3 0.4 collective-permute-done.1.other_ref
  104.8 0.0 copy-done.4
  104.8 1.7 %update.1 = (f32[16,64]{1,0:T(8,128)}, f32[16,64]{1,0:T(8,128)}, bf16[512,1024]{1,0:T(8,128)(2,1)}, f32[2,1024]{1,0:T(2,128)}, f32[2,1024]{1,0:T(2,128)}) custom-call(bf16[4,1056,128]{2,1,0:T(8,128)(2,1)S(1)} %all_to_all.29.mine_ref, bf16[4,1056,128]{2,1,0:T(8,128)(2,1)S(1)} %collective-permute-done.1.other_ref, bf16[512,1024]{1,0:T(8,128)(2,1)S(1)} %copy-done, ...), custom_call_target="tpu_custom_call" | custom-call | tf_op jit(solution)/shard_map/update/pallas_call | solution.py:411
  (1 shorter events, 0.0 us)
Async XLA Ops:
  0.6 25.1 %copy-start.1 = (f32[2,1024]{1,0:T(2,128)S(1)}, f32[2,1024]{1,0:T(2,128)}, u32[]{:S(2)}) copy-start(f32[2,1024]{1,0:T(2,128)} %bn_ref.3) | copy-start | bytes 24580
  26.6 5.5 %collective-permute-start = (bf16[512,512]{1,0:T(8,128)(2,1)S(1)}, bf16[512,512]{1,0:T(8,128)(2,1)S(1)}, u32[]{:S(2)}, u32[]{:S(2)}) collective-permute-start(bf16[512,512]{1,0:T(8,128)(2,1)S(1)} %get-tuple-element.33), channel_id=1, source_target_pairs={{0,1},{1,0},{2,3},{3,2},{4,5},{5,4},{6,7},{7,6},{8,9},{9,8},{10,11... | collective-permute-start | bytes 1572872 | tf_op jit(solution)/shard_map/ppermute | solution.py:356
  32.2 31.7 %copy-start.2 = (f32[16,64]{1,0:T(8,128)S(1)}, f32[16,64]{1,0:T(8,128)}, u32[]{:S(2)}) copy-start(f32[16,64]{1,0:T(8,128)} %master_ref.3) | copy-start | bytes 12292
  32.2 31.7 %copy-start.3 = (f32[16,64]{1,0:T(8,128)S(1)}, f32[16,64]{1,0:T(8,128)}, u32[]{:S(2)}) copy-start(f32[16,64]{1,0:T(8,128)} %vel_ref.3) | copy-start | bytes 12292
  81.6 20.8 %copy-start = (bf16[512,1024]{1,0:T(8,128)(2,1)S(1)}, bf16[512,1024]{1,0:T(8,128)(2,1)}, u32[]{:S(2)}) copy-start(bf16[512,1024]{1,0:T(8,128)(2,1)} %w_ref.3) | copy-start | bytes 3145732
  94.9 9.9 %collective-permute-start.1 = (bf16[4,1056,128]{2,1,0:T(8,128)(2,1)S(1)}, bf16[4,1056,128]{2,1,0:T(8,128)(2,1)S(1)}, u32[]{:S(2)}, u32[]{:S(2)}) collective-permute-start(bf16[4,1056,128]{2,1,0:T(8,128)(2,1)S(1)} %all_to_all.29.mine_ref), channel_id=1, source_target_pairs={{0,1},{1,0},{2,3},{3,2},{4,5},{5,4},{6,7},{7,6},{8,9},{9,8},{10,11... | collective-permute-start | bytes 3244040 | tf_op jit(solution)/shard_map/ppermute | solution.py:410
  102.5 2.3 %copy-start.4 = (f32[2,1024]{1,0:T(2,128)S(1)}, f32[2,1024]{1,0:T(2,128)}, u32[]{:S(2)}) copy-start(f32[2,1024]{1,0:T(2,128)} %bnv_ref.1) | copy-start | bytes 24580
